TPU v7x, 128 devices: a whole 4x4x4 slice. The times are simulated.
128 devices in a mesh: section: 4 (over y), tp: 8 (over x, z_lo), dec: 4 (over z_hi, core).
Axes of the slice: x: 4, y: 4, z: 4 (z_hi: 2, z_lo: 2; z = z_hi * 2 + z_lo), core: 2. Of those that a mesh axis runs over, the one named last changes fastest.
Arguments:
- hidden_in: bfloat16 [4, 1024, 8192], P('section', ('dec', 'tp')), may hold values from -3 to 3
- attn_gain: float32 [4, 8192], P('section'), may hold values from 0.5 to 1.5
- q_weight: bfloat16 [4, 8192, 4096], P('section', None, 'tp'), may hold values from -0.0625 to 0.0625
- key_weight_matrix: bfloat16 [4, 8192, 1024], P('section', None, 'tp'), may hold values from -0.0625 to 0.0625
- value_weight_matrix: bfloat16 [4, 8192, 1024], P('section', None, 'tp'), may hold values from -0.0625 to 0.0625
- o_weight: bfloat16 [4, 4096, 8192], P('section', 'tp'), may hold values from -0.375 to 0.375
- kv_pool: bfloat16 [4, 640, 16, 8, 256], P('section', 'dec', None, 'tp'), may hold values from -384 to 384
- block_table: int32 [4, 4, 160], P('section', 'dec'), may hold values from 0 to 159, each once within a row
- request_len: int32 [4, 16], P('section', 'dec'), may hold values from 16 to 3407, as said below
- prefix_len: int32 [4, 16], P('section', 'dec'), may hold values from 480 to 640, as said below
- new_len: int32 [4, 16], P('section', 'dec'), may hold values from 16 to 208, as said below
- page_owner: int32 [4, 896, 1], P('section', 'dec'), may hold values from 0 to 127; in each aligned block of 224 rows (0 to 223, 224 to 447, ..., all dimensions but the last counted through in order) at most 3 rows name the same one
Outputs:
- passed: bfloat16 [4, 1024, 8192], P('section', ('dec', 'tp'))
- received_pages: bfloat16 [128, 128, 3, 16, 1, 256], P(('section', 'tp', 'dec'))
- received_tags: int32 [128, 128, 3], P(('section', 'tp', 'dec'))
Inputs may be any that keep to these rules, and one draw needn't show every extreme that they name: `prefix_len`: a multiple of 16; some request has exactly 640. `new_len`: a multiple of 16; the 4 entries of one section and decode index sum to 256. `request_len`: at least prefix_len + new_len of the same request. `block_table`: for each section and decode index, every pool page once. `page_owner`: among the rows of one device, no owner is named more than 3 times.
All inputs are finite; a program needn't handle non-finite values.
Results may differ from a plain program's by a relative error of at most 0.02.
The roundings to bfloat16 on the way count: a program that leaves them out, or rounds other values in their place, can miss the bound.
Values may be sent and summed in bfloat16 or wider, within the bound.
No kernel may reach another device: no remote copies, remote signals or barrier semaphores. Data moves between devices by JAX's collectives and lax.ppermute only.
A program may use at most 128 MiB of HBM per device.

v0:
```python
import math

import jax
import jax.numpy as jnp
from jax import lax
from jax.sharding import PartitionSpec as P

HEAD_DIMENSION = 128
PAGE_TOKENS = 16
MAXB = 40
NB = 56


theta_base = 500000.0
eps_norm = 1e-05
neg_large = -1e30


def shifted(block, axis, distance):
    devices = range(lax.axis_size(axis))
    route = [((i - distance) % len(devices), i) for i in devices]
    return lax.ppermute(block, axis, route)


def rotary_embedding(values, token_positions, head_size):
    half_size = head_size // 2
    frequency = theta_base ** (-(jnp.arange(half_size, dtype=jnp.float32) * 2.0) / head_size)
    angles = token_positions.astype(jnp.float32)[:, None] * frequency[None, :]
    cosine = jnp.cos(angles)[:, None, :]
    sine_part = jnp.sin(angles)[:, None, :]
    first_half = values[..., :half_size]
    second = values[..., half_size:]
    return jnp.concatenate(
        [first_half * cosine - second * sine_part, second * cosine + first_half * sine_part],
        axis=-1,
    )


def token_layout(prefix, new_tokens, token_batch):
    new_ends = jnp.cumsum(new_tokens)
    new_starts = new_ends - new_tokens
    token_index = jnp.arange(token_batch, dtype=jnp.int32)
    token_req = jnp.sum((token_index[:, None] >= new_ends[None, :]).astype(jnp.int32), axis=1)
    membership = token_req[:, None] == jnp.arange(new_tokens.shape[0], dtype=jnp.int32)[None, :]
    own_prefix = jnp.sum(jnp.where(membership, prefix[None, :], 0), axis=1)
    own_start = jnp.sum(jnp.where(membership, new_starts[None, :], 0), axis=1)
    token_positions = own_prefix + token_index - own_start
    return (token_req, token_positions, new_starts, own_prefix)


def attention_mask(token_req, own_prefix, prefix_slots, token_batch):
    slot_number = jnp.arange(prefix_slots, dtype=jnp.int32)
    slot_req = slot_number // (MAXB * PAGE_TOKENS)
    slot_pos = slot_number % (MAXB * PAGE_TOKENS)
    prefix_ok = (slot_req[None, :] == token_req[:, None]) & (
        slot_pos[None, :] < own_prefix[:, None]
    )
    token_index = jnp.arange(token_batch, dtype=jnp.int32)
    recent_ok = (token_req[None, :] == token_req[:, None]) & (
        token_index[None, :] <= token_index[:, None]
    )
    return jnp.concatenate([prefix_ok, recent_ok], axis=1)


def apply_attention(query_rows_all, key_row_values, value_row_values, permitted_mask):
    scores = jnp.einsum(
        "tkgd,skd->kgts", query_rows_all, key_row_values, preferred_element_type=jnp.float32
    ) / math.sqrt(query_rows_all.shape[-1])
    scores = jnp.where(permitted_mask[None, None], scores, neg_large)
    row_max = jnp.max(scores, axis=-1, keepdims=True)
    exp_scores = jnp.exp(scores - row_max)
    probabilities = (exp_scores / jnp.sum(exp_scores, axis=-1, keepdims=True)).astype(jnp.bfloat16)
    mixed_heads = jnp.einsum(
        "kgts,skd->tkgd", probabilities, value_row_values, preferred_element_type=jnp.float32
    )
    return mixed_heads.astype(jnp.bfloat16)


def collect_pages(prefix_page_list, fresh_pages, prefix, new_tokens, full_length, new_starts):
    request_number = jnp.arange(prefix.shape[0], dtype=jnp.int32)[:, None]
    block_number = jnp.arange(NB, dtype=jnp.int32)[None, :]
    prefix_count = (prefix // PAGE_TOKENS)[:, None]
    new_count = (new_tokens // PAGE_TOKENS)[:, None]
    page_base = (new_starts // PAGE_TOKENS)[:, None]
    from_prefix = block_number < prefix_count
    new_index = jnp.clip(page_base + block_number - prefix_count, 0, fresh_pages.shape[0] - 1)
    source_row = jnp.where(
        from_prefix,
        request_number * MAXB + jnp.minimum(block_number, MAXB - 1),
        prefix_page_list.shape[0] + new_index,
    ).reshape(-1)
    exists = block_number < prefix_count + new_count
    finished = (full_length == prefix + new_tokens)[:, None]
    sent_flag = (exists & finished).reshape(-1)
    sources = jnp.concatenate([prefix_page_list, fresh_pages], axis=0)
    return (sources[source_row], sent_flag)


def place_pages(pages, owner_list, sent_flag, devices, capacity):
    row_total = owner_list.shape[0]
    owner_hits = (
        (owner_list[:, None] == jnp.arange(devices, dtype=jnp.int32)[None, :]) & sent_flag[:, None]
    ).astype(jnp.int32)
    earlier = jnp.cumsum(owner_hits, axis=0) - owner_hits
    slot_index = jnp.sum(earlier * owner_hits, axis=1)
    target = jnp.where(sent_flag, owner_list, devices)
    page_buffer = (
        jnp.zeros((devices, capacity) + pages.shape[1:], pages.dtype)
        .at[target, slot_index]
        .set(pages, mode="drop")
    )
    page_tags = (
        jnp.zeros((devices, capacity), jnp.int32)
        .at[target, slot_index]
        .set(jnp.arange(row_total, dtype=jnp.int32) + 1, mode="drop")
    )
    return (page_buffer, page_tags)


def deliver(page_buffer, page_tags):
    result = (
        lax.all_to_all(
            page_buffer, ("section", "tp", "dec"), split_axis=0, concat_axis=0, tiled=True
        ),
        lax.all_to_all(
            page_tags, ("section", "tp", "dec"), split_axis=0, concat_axis=0, tiled=True
        ),
    )
    return result


def on_device(
    hidden_in,
    attn_gain,
    q_weight,
    key_weight_matrix,
    value_weight_matrix,
    o_weight,
    kv_pool,
    block_table,
    request_len,
    prefix_len,
    new_len,
    page_owner,
):
    local_rows = hidden_in[0]
    rows_float = local_rows.astype(jnp.float32)
    norm_scale = lax.rsqrt(jnp.mean(rows_float * rows_float, axis=-1, keepdims=True) + eps_norm)
    normalized_hidden = (rows_float * norm_scale * attn_gain[0]).astype(jnp.bfloat16)
    q_heads = q_weight.shape[2] // HEAD_DIMENSION
    key_value_heads = key_weight_matrix.shape[2] // HEAD_DIMENSION
    group_size = q_heads // key_value_heads
    token_batch = local_rows.shape[0] * lax.axis_size("tp")
    prefix = prefix_len[0]
    new_tokens = new_len[0]
    full_length = request_len[0]
    token_req, token_positions, new_starts, own_prefix = token_layout(
        prefix, new_tokens, token_batch
    )
    row_piece = lax.all_gather(normalized_hidden, "tp", axis=0, tiled=True)
    row_count = row_piece.shape[0]
    query_part = rotary_embedding(
        jnp.dot(row_piece, q_weight[0], preferred_element_type=jnp.float32).reshape(
            row_count, q_heads, HEAD_DIMENSION
        ),
        token_positions,
        HEAD_DIMENSION,
    )
    key_part = rotary_embedding(
        jnp.dot(row_piece, key_weight_matrix[0], preferred_element_type=jnp.float32).reshape(
            row_count, key_value_heads, HEAD_DIMENSION
        ),
        token_positions,
        HEAD_DIMENSION,
    )
    value_part = jnp.dot(row_piece, value_weight_matrix[0], preferred_element_type=jnp.float32)
    projected = jnp.concatenate(
        [
            query_part.reshape(row_count, q_heads * HEAD_DIMENSION),
            key_part.reshape(row_count, key_value_heads * HEAD_DIMENSION),
            value_part,
        ],
        axis=1,
    ).astype(jnp.bfloat16)
    query_rows_all = projected[:, : q_heads * HEAD_DIMENSION].reshape(
        token_batch, key_value_heads, group_size, HEAD_DIMENSION
    )
    fresh_keys = projected[
        :, q_heads * HEAD_DIMENSION : (q_heads + key_value_heads) * HEAD_DIMENSION
    ].reshape(token_batch, key_value_heads, HEAD_DIMENSION)
    fresh_values = projected[:, (q_heads + key_value_heads) * HEAD_DIMENSION :].reshape(
        token_batch, key_value_heads, HEAD_DIMENSION
    )
    prefix_page_list = kv_pool[0][block_table[0, 0]]
    fresh_pages = jnp.concatenate([fresh_keys, fresh_values], axis=-1).reshape(
        token_batch // PAGE_TOKENS, PAGE_TOKENS, key_value_heads, 2 * HEAD_DIMENSION
    )
    pages, sent_flag = collect_pages(
        prefix_page_list, fresh_pages, prefix, new_tokens, full_length, new_starts
    )
    devices = lax.axis_size("section") * lax.axis_size("tp") * lax.axis_size("dec")
    owner_list = page_owner[0, :, 0]
    capacity = owner_list.shape[0] // devices + 2
    page_buffer, page_tags = place_pages(pages, owner_list, sent_flag, devices, capacity)
    flattened_prefix = prefix_page_list.reshape(-1, key_value_heads, 2 * HEAD_DIMENSION)
    key_row_values = jnp.concatenate([flattened_prefix[:, :, :HEAD_DIMENSION], fresh_keys], axis=0)
    value_row_values = jnp.concatenate(
        [flattened_prefix[:, :, HEAD_DIMENSION:], fresh_values], axis=0
    )
    permitted_mask = attention_mask(token_req, own_prefix, flattened_prefix.shape[0], token_batch)
    attention_output = apply_attention(
        query_rows_all, key_row_values, value_row_values, permitted_mask
    ).reshape(token_batch, q_heads * HEAD_DIMENSION)
    summed = lax.psum_scatter(
        jnp.dot(attention_output, o_weight[0], preferred_element_type=jnp.float32).astype(
            jnp.bfloat16
        ),
        "tp",
        scatter_dimension=0,
        tiled=True,
    ).astype(jnp.float32)
    mixed_rows = (rows_float + summed).astype(jnp.bfloat16)
    passed = shifted(mixed_rows, "section", 1)[None]
    delivered_pages, delivered_tags = deliver(page_buffer, page_tags)
    return (passed, delivered_pages[None], delivered_tags[None])


def solution(mesh):
    in_specs = (
        P("section", ("dec", "tp"), None),
        P("section", None),
        P("section", None, "tp"),
        P("section", None, "tp"),
        P("section", None, "tp"),
        P("section", "tp", None),
        P("section", "dec", None, "tp", None),
        P("section", "dec", None),
        P("section", "dec"),
        P("section", "dec"),
        P("section", "dec"),
        P("section", "dec", None),
    )
    out_specs = (
        P("section", ("dec", "tp"), None),
        P(("section", "tp", "dec"), None, None, None, None, None),
        P(("section", "tp", "dec"), None, None),
    )
    return jax.shard_map(
        on_device, mesh=mesh, in_specs=in_specs, out_specs=out_specs, check_vma=False
    )
```

profile of v0, /device:TPU:0, one launch (start us, length us, event | category | flops | bytes accessed | tf_op | source)
XLA Modules:
  0.0 295.2 jit_solution(13822589932600372342)
XLA Ops:
  7.2 1.4 fusion.20
  8.6 2.0 fusion.22
  10.8 12.0 %copy.57 = bf16[512,8192]{1,0:T(8,128)(2,1)} copy(bf16[512,8192]{0,1:T(8,128)(2,1)} %bitcast.141) | data formatting | bytes 16777216 | tf_op jit(solution)/shard_map/dot_general | solution.py:163
  22.8 0.2 reduce-window.10
  23.0 2.2 gather_fusion
  25.2 0.1 convert_reduce_fusion
  25.2 0.1 select_reduce_fusion.1
  25.4 0.1 fusion.32
  25.5 0.3 multiply_cosine_fusion
  25.8 1.8 compare_and_fusion
  27.5 1.1 pad_add_fusion
  28.7 1.2 fusion.62
  29.9 73.2 %all-gather.2.cloned.1.call-done = bf16[256,8192]{1,0:T(8,128)(2,1)} async-done(((bf16[32,8192]{1,0:T(8,128)(2,1)}), bf16[256,8192]{1,0:T(8,128)(2,1)}) %all-gather.2.cloned.1.call-update) | async-done | bytes 4194320 | tf_op jit(solution)/shard_map/all_gather | solution.py:160
  103.1 3.7 %fusion.14 = f32[256,1,128]{0,2,1:T(8,128)S(1)} fusion(bf16[256,8192]{1,0:T(8,128)(2,1)} %all-gather.2.cloned.1.call-done, bf16[1,8192,128]{2,1,0:T(8,128)(2,1)S(1)} %copy-done), kind=kOutput, calls=%fused_computation.26 | convolution fusion | flops 536870912 | bytes 6422528 | tf_op jit(solution)/shard_map/dot_general | solution.py:170
  106.8 0.3 fusion.44
  107.1 0.1 copy.42
  107.3 7.1 %fusion.5 = f32[256,4,128]{0,2,1:T(8,128)S(1)} fusion(bf16[4,128,8192]{2,1,0:T(8,128)(2,1)} %bitcast.144, bf16[256,8192]{1,0:T(8,128)(2,1)} %all-gather.2.cloned.1.call-done), kind=kOutput, calls=%fused_computation.13 | convolution fusion | flops 2147483648 | bytes 13107200 | tf_op jit(solution)/shard_map/dot_general | solution.py:163
  114.5 5.8 %fusion.1 = (f32[4,256]{1,0:T(4,128)S(1)}, f32[2816,256,4]{1,0,2:T(8,128)}) fusion(pred[256,2816]{0,1:T(8,128)(4,1)S(1)} %copy-done.4, bf16[256,4,64]{0,2,1:T(8,128)(2,1)S(1)} %get-tuple-element.22, bf16[256,4,64]{0,2,1:T(8,128)(2,1)S(1)} %get-tuple-element.21, bf16[256,1,128]{2,0,1:T(8,128)(2,1)S(1)} %copy.42, bf16[2560,1,128]{2,0,1:T(8,128)(2,1)S(1)} %copy-done.7), kind=kOutput, calls=%fused_computation.9 | convolution fusion | flops 748813312 | bytes 13242368 | tf_op jit(solution)/shard_map/tkgd,skd->kgts/dot_general | solution.py:66
  120.3 6.9 %fusion = f32[4,256]{1,0:T(4,128)S(1)} fusion(f32[2816,256,4]{1,0,2:T(8,128)} %get-tuple-element.31, f32[4,256]{1,0:T(4,128)S(1)} %get-tuple-element.30, pred[256,2816]{0,1:T(8,128)(4,1)S(1)} %copy-done.4), kind=kLoop, calls=%fused_computation.8 | loop fusion | flops 11533312 | bytes 12263424 | tf_op jit(solution)/shard_map/reduce_sum | solution.py:72
  127.2 1.2 fusion.17
  128.4 7.2 %fusion.11 = bf16[128,4,256]{2,0,1:T(8,128)(2,1)S(1)} fusion(f32[4,256]{1,0:T(4,128)S(1)} %fusion, f32[4,256]{1,0:T(4,128)S(1)} %get-tuple-element.30, f32[2816,256,4]{1,0,2:T(8,128)} %get-tuple-element.31, pred[256,2816]{0,1:T(8,128)(4,1)S(1)} %copy-done.4, bf16[256,1,128]{2,0,1:T(8,128)(2,1)S(1)} %bitcast.151, bf16[2560,1,128]{2,0,1:T(8,128)(2,1)S(1)} %copy-done.6), kind=kOutput, calls=%fused_computation.25 | convolution fusion | flops 754188288 | bytes 13246464 | tf_op jit(solution)/shard_map/kgts,skd->tkgd/dot_general | solution.py:73
  135.7 4.4 %convolution_convert_fusion = bf16[256,8192]{1,0:T(8,128)(2,1)} fusion(bf16[256,512]{0,1:T(8,128)(2,1)S(1)} %bitcast.153, bf16[1,512,8192]{2,1,0:T(8,128)(2,1)S(1)} %bitcast.143), kind=kOutput, calls=%fused_computation.7 | convolution fusion | flops 2149580800 | bytes 12845056 | tf_op jit(solution)/shard_map/dot_general | solution.py:215
  140.1 0.6 copy-done.12
  140.8 0.1 and.111
  141.0 0.1 add.206
  141.2 0.1 and.114
  141.4 0.1 lt.142
  141.5 0.1 add.208
  141.7 0.1 lt.135
  141.8 0.1 lt.133
  141.8 0.1 fusion.38
  142.0 0.1 fusion.33
  142.2 0.2 fusion.36
  142.5 10.8 %scatter_fusion.1 = s32[128,3]{0,1:T(4,128)S(1)} fusion(s32[128,3]{0,1:T(4,128)S(1)} %broadcast_in_dim.59, s32[224]{0:T(256)S(1)} %bitcast.137, s32[224]{0:T(256)S(1)} %iota_add_fusion), kind=kCustom, calls=%fused_computation.3 | custom fusion | bytes 4480 | tf_op jit(solution)/shard_map/scatter | solution.py:115
  153.3 0.7 copy.50
  154.0 11.2 %all-to-all-start.1 = ((s32[128,1,3]{2,1,0:T(1,128)}), s32[128,1,3]{2,1,0:T(1,128)S(1)}, u32[]{:S(2)}, u32[]{:S(2)}) async-start(s32[128,1,3]{2,1,0:T(1,128)} %copy.50), calls=%async_computation.2 | async-start | bytes 131072 | tf_op jit(solution)/shard_map/all_to_all | solution.py:125
  165.2 0.1 maximum_bitcast_fusion
  165.3 0.9 gather_fusion.1
  166.2 1.9 broadcast.451
  168.1 22.9 %scatter_fusion = bf16[128,3,16,256]{3,2,1,0:T(8,128)(2,1)} fusion(bf16[128,3,16,256]{3,2,1,0:T(8,128)(2,1)} %broadcast.451, s32[224]{0:T(256)S(1)} %bitcast.138, bf16[224,16,256]{2,1,0:T(8,128)(2,1)S(1)} %gather_fusion.1), kind=kCustom, calls=%fused_computation.2 | custom fusion | bytes 5506816 | tf_op jit(solution)/shard_map/scatter | solution.py:110
  191.0 11.0 %all-to-all-start = ((bf16[128,3,16,1,256]{4,2,1,3,0:T(8,128)(2,1)}), bf16[128,3,16,1,256]{4,2,1,3,0:T(8,128)(2,1)}, u32[]{:S(2)}, u32[]{:S(2)}) async-start(bf16[128,3,16,1,256]{4,2,1,3,0:T(8,128)(2,1)} %bitcast.47), calls=%async_computation.1 | async-start | bytes 6291456 | tf_op jit(solution)/shard_map/all_to_all | solution.py:122
  202.1 65.6 %reduce-scatter.2.cloned.1.call-done = bf16[32,8192]{1,0:T(8,128)(2,1)} async-done(((bf16[256,8192]{1,0:T(8,128)(2,1)}), bf16[32,8192]{1,0:T(8,128)(2,1)}) %reduce-scatter.2.cloned.1.call-update) | async-done | bytes 524304 | tf_op jit(solution)/shard_map/reduce_scatter | solution.py:214
  267.6 1.2 fusion.23
  268.8 2.4 collective-permute-start
  271.2 0.6 copy.52
  271.8 12.0 %collective-permute-done = bf16[32,8192]{1,0:T(8,128)(2,1)S(1)} collective-permute-done((bf16[32,8192]{1,0:T(8,128)(2,1)S(1)}, bf16[32,8192]{1,0:T(8,128)(2,1)S(1)}, u32[]{:S(2)}, u32[]{:S(2)}) %collective-permute-start) | collective-permute-done | bytes 524320 | tf_op jit(solution)/shard_map/ppermute | solution.py:22
  283.8 0.8 copy.64
  284.6 3.8 %copy.65 = bf16[1,128,3,16,1,256]{5,3,4,2,1,0:T(8,128)(2,1)} copy(bf16[1,128,3,16,1,256]{5,3,4,2,1,0:T(8,128)(2,1)} %bitcast.49) | data formatting | bytes 6291456
  (71 shorter events, 0.9 us)
Async XLA Ops:
  7.2 95.9 %copy-start = (bf16[1,8192,128]{2,1,0:T(8,128)(2,1)S(1)}, bf16[1,8192,128]{2,1,0:T(8,128)(2,1)}, u32[]{:S(2)}) copy-start(bf16[1,8192,128]{2,1,0:T(8,128)(2,1)} %param.15) | copy-start | bytes 6291460
  7.2 95.9 %all-gather.2.cloned.1.call-start = ((), (), s32[]{:S(2)}) async-start(), calls=%async_computation.3 | async-start | bytes 4718592 | tf_op jit(solution)/shard_map/all_gather | solution.py:160
  10.7 257.0 %reduce-scatter.2.cloned.1.call-start = ((), (), s32[]{:S(2)}) async-start(), calls=%async_computation.4 | async-start | bytes 4718592 | tf_op jit(solution)/shard_map/reduce_scatter | solution.py:214
  10.7 12.0 %copy-start.10 = (s32[1,4]{1,0:T(1,128)S(1)}, s32[1,4]{1,0:T(1,128)}, u32[]{:S(2)}) copy-start(s32[1,4]{1,0:T(1,128)} %param.22) | copy-start | bytes 52
  10.7 12.2 %copy-start.11 = (s32[1,1,160]{2,1,0:T(1,128)S(1)}, s32[1,1,160]{2,1,0:T(1,128)}, u32[]{:S(2)}) copy-start(s32[1,1,160]{2,1,0:T(1,128)} %param.19) | copy-start | bytes 1924
  10.8 14.5 %copy-start.9 = (s32[1,4]{1,0:T(1,128)S(1)}, s32[1,4]{1,0:T(1,128)}, u32[]{:S(2)}) copy-start(s32[1,4]{1,0:T(1,128)} %param.21) | copy-start | bytes 52
  22.9 2.4 copy-start.13
  107.2 7.2 %copy-start.4 = (pred[256,2816]{0,1:T(8,128)(4,1)S(1)}, pred[256,2816]{0,1:T(8,128)(4,1)}, u32[]{:S(2)}) copy-start(pred[256,2816]{0,1:T(8,128)(4,1)} %pad_add_fusion) | copy-start | bytes 2162692
  107.3 7.2 %copy-start.7 = (bf16[2560,1,128]{2,0,1:T(8,128)(2,1)S(1)}, bf16[2560,1,128]{2,0,1:T(8,128)(2,1)}, u32[]{:S(2)}) copy-start(bf16[2560,1,128]{2,0,1:T(8,128)(2,1)} %get-tuple-element.20) | copy-start | bytes 1966084
  120.3 6.9 %copy-start.2 = (bf16[256,8192]{1,0:T(8,128)(2,1)S(1)}, bf16[256,8192]{1,0:T(8,128)(2,1)}, u32[]{:S(2)}) copy-start(bf16[256,8192]{1,0:T(8,128)(2,1)} %all-gather.2.cloned.1.call-done) | copy-start | bytes 12582916
  120.3 6.9 %copy-start.5 = (bf16[1,8192,128]{2,1,0:T(8,128)(2,1)S(1)}, bf16[1,8192,128]{2,1,0:T(8,128)(2,1)}, u32[]{:S(2)}) copy-start(bf16[1,8192,128]{2,1,0:T(8,128)(2,1)} %param.16) | copy-start | bytes 6291460
  127.1 1.3 copy-start.6
  127.1 8.5 %slice-start = ((s8[8388608]{0:T(1024)(128)(4,1)}), s8[4194304]{0:T(1024)(128)(4,1)S(1)}, s32[]{:S(2)}) async-start(s8[8388608]{0:T(1024)(128)(4,1)} %bitcast.142), calls=%async_computation.5 | async-start | bytes 8388608
  128.4 7.2 %slice-start.1 = ((s8[8388608]{0:T(1024)(128)(4,1)}), s8[4194304]{0:T(1024)(128)(4,1)S(1)}, s32[]{:S(2)}) async-start(s8[8388608]{0:T(1024)(128)(4,1)} %bitcast.142), calls=%async_computation.6 | async-start | bytes 8388608
  140.1 0.7 copy-start.12
  140.1 1.0 copy-start.14
  140.1 1.7 copy-start.8
  154.0 37.0 %all-to-all-start.1 = ((s32[128,1,3]{2,1,0:T(1,128)}), s32[128,1,3]{2,1,0:T(1,128)S(1)}, u32[]{:S(2)}, u32[]{:S(2)}) async-start(s32[128,1,3]{2,1,0:T(1,128)} %copy.50), calls=%async_computation.2 | async-start | bytes 131072 | tf_op jit(solution)/shard_map/all_to_all | solution.py:125
  191.0 76.6 %copy-start.3 = (bf16[1,32,8192]{2,1,0:T(8,128)(2,1)S(1)}, bf16[1,32,8192]{2,1,0:T(8,128)(2,1)}, u32[]{:S(2)}) copy-start(bf16[1,32,8192]{2,1,0:T(8,128)(2,1)} %param.12) | copy-start | bytes 1572868
  191.0 80.8 %all-to-all-start = ((bf16[128,3,16,1,256]{4,2,1,3,0:T(8,128)(2,1)}), bf16[128,3,16,1,256]{4,2,1,3,0:T(8,128)(2,1)}, u32[]{:S(2)}, u32[]{:S(2)}) async-start(bf16[128,3,16,1,256]{4,2,1,3,0:T(8,128)(2,1)} %bitcast.47), calls=%async_computation.1 | async-start | bytes 6291456 | tf_op jit(solution)/shard_map/all_to_all | solution.py:122
  268.8 15.0 %collective-permute-start = (bf16[32,8192]{1,0:T(8,128)(2,1)S(1)}, bf16[32,8192]{1,0:T(8,128)(2,1)S(1)}, u32[]{:S(2)}, u32[]{:S(2)}) collective-permute-start(bf16[32,8192]{1,0:T(8,128)(2,1)S(1)} %fusion.23), channel_id=1, source_target_pairs={{96,0},{0,32},{32,64},{64,96},{97,1},{1,33},{33,65},{65,97},{98,2}... | collective-permute-start | bytes 1572872 | tf_op jit(solution)/shard_map/ppermute | solution.py:22
  283.8 4.6 %copy-start.1 = (bf16[1,8192,128]{2,1,0:T(8,128)(2,1)S(1)}, bf16[1,8192,128]{2,1,0:T(8,128)(2,1)}, u32[]{:S(2)}) copy-start(bf16[1,8192,128]{2,1,0:T(8,128)(2,1)} %param.15) | copy-start | bytes 6291460
Sparse Core Ops, SparseCore 0:
  10.8 92.2 all-gather.1
  140.3 127.3 reduce-scatter.1
where the time goes:
time: 298 us; the launch traced here: 295 us
  waiting for transfers between devices  151 us (51%)
  local copies, waits for them, and re-layouts  59.5 us (20%)
  matrix products  29.4 us (10%)
  starting transfers between devices  24.7 us (8%)
  other arithmetic  16.4 us (6%)
  between operations  14.4 us (5%)
    all_gather x1, waiting for transfers between devices, on_device(): row_piece = lax.all_gather(normalized_hidden, 'tp', axis=0, tiled=True)  73.2 us
    reduce_scatter x1, waiting for transfers between devices, on_device(): lax.psum_scatter(jnp.dot(attention_output, o_weight[0], preferred_element...  65.6 us
    scatter x1, local copies, waits for them, and re-layouts, place_pages(): page_buffer = jnp.zeros((devices, capacity) + pages.shape[1:], pages.dtyp...  22.9 us
    dot_general x1, local copies, waits for them, and re-layouts, on_device(): jnp.dot(row_piece, q_weight[0], preferred_element_type=jnp.float32)  12 us
    ppermute x1, waiting for transfers between devices, shifted(): return lax.ppermute(block, axis, route)  12 us
    all_to_all x1, starting transfers between devices, deliver(): lax.all_to_all(page_tags, ('section', 'tp', 'dec'), split_axis=0, concat_...  11.2 us
    all_to_all x1, starting transfers between devices, deliver(): lax.all_to_all(page_buffer, ('section', 'tp', 'dec'), split_axis=0, conca...  11 us
    scatter x1, local copies, waits for them, and re-layouts, place_pages(): page_tags = jnp.zeros((devices, capacity), jnp.int32).at[target, slot_ind...  10.8 us
  transfers between devices with their start and end apart: 5, of which 3 were waited for; matrix products, arithmetic and copies ran while one was open for 20% of the time, Pallas kernels for 0%

commit v1 on v0

v1 whole, which is shorter than its diff:
```python
import functools
import math

import jax
import jax.numpy as jnp
from jax import lax
from jax.experimental import pallas as pl
from jax.experimental.pallas import tpu as pltpu
from jax.sharding import PartitionSpec as P

HEAD_DIMENSION = 128
PAGE_TOKENS = 16
MAXB = 40
NB = 56
CAP = 3
ROWS = 32

theta_base = 500000.0
eps_norm = 1e-05
neg_large = -1e30

MIB = 1 << 20
VMEM = pl.BlockSpec(memory_space=pltpu.VMEM)
SMEM = pl.BlockSpec(memory_space=pltpu.SMEM)
ANY = pl.BlockSpec(memory_space=pl.ANY)

PIECES = ((0, 0), (0, 1), (1, 0), (3, 0), (1, 1), (3, 1), (2, 0), (2, 1))


def tp_route(dx, dz, n_tp):
    nx = n_tp // 2
    return [(x * 2 + z, ((x + dx) % nx) * 2 + (z ^ dz)) for x in range(nx) for z in range(2)]


def send(block, dx, dz):
    return lax.ppermute(block, "tp", tp_route(dx, dz, lax.axis_size("tp")))


def shifted(block, axis, distance):
    count = lax.axis_size(axis)
    return lax.ppermute(block, axis, [((i - distance) % count, i) for i in range(count)])


def norm_kernel(x_ref, gain_ref, out_ref):
    x = x_ref[...].astype(jnp.float32)
    scale = lax.rsqrt(jnp.mean(x * x, axis=-1, keepdims=True) + eps_norm)
    out_ref[...] = (x * scale * gain_ref[...]).astype(jnp.bfloat16)


def normalize(x, gain):
    return pl.pallas_call(
        norm_kernel,
        out_shape=jax.ShapeDtypeStruct(x.shape, jnp.bfloat16),
        in_specs=[VMEM, VMEM],
        out_specs=VMEM,
        compiler_params=pltpu.CompilerParams(vmem_limit_bytes=16 * MIB),
        cost_estimate=pl.CostEstimate(flops=4 * x.size, bytes_accessed=4 * x.size, transcendentals=0),
        name="norm",
    )(x, gain)


def qkv_kernel(order, *refs):
    pieces = refs[:8]
    wq, wk, wv, cos_ref, sin_ref, q_ref, kv_ref, acc_q, acc_kv = refs[8:]
    step = pl.program_id(0)

    @pl.when(step == 0)
    def _():
        acc_q[...] = jnp.zeros_like(acc_q)
        acc_kv[...] = jnp.zeros_like(acc_kv)

    x = jnp.concatenate([p[...] for p in pieces], axis=0)
    wkv = jnp.concatenate([wk[...], wv[...]], axis=1)
    acc_q[...] += jnp.dot(x, wq[...], preferred_element_type=jnp.float32)
    acc_kv[...] += jnp.dot(x, wkv, preferred_element_type=jnp.float32)

    @pl.when(step == pl.num_programs(0) - 1)
    def _():
        heads = acc_q.shape[1] // HEAD_DIMENSION
        for p in range(8):
            rows = pl.ds(pl.multiple_of(order[p] * ROWS, ROWS), ROWS)
            cos = cos_ref[rows, :]
            sin = sin_ref[rows, :]
            here = slice(p * ROWS, (p + 1) * ROWS)

            def rotate(v):
                return v * cos + pltpu.roll(v, HEAD_DIMENSION // 2, 1) * sin

            for h in range(heads):
                cols = slice(h * HEAD_DIMENSION, (h + 1) * HEAD_DIMENSION)
                q_ref[rows, cols] = rotate(acc_q[here, cols]).astype(jnp.bfloat16)
            kv_ref[rows, :HEAD_DIMENSION] = rotate(acc_kv[here, :HEAD_DIMENSION]).astype(jnp.bfloat16)
            kv_ref[rows, HEAD_DIMENSION:] = acc_kv[here, HEAD_DIMENSION:].astype(jnp.bfloat16)


def project(order, pieces, wq, wk, wv, cos, sin):
    depth = wq.shape[0]
    block = 1024
    tokens = 8 * ROWS
    n_q, n_kv = wq.shape[1], wk.shape[1] + wv.shape[1]
    grid_spec = pltpu.PrefetchScalarGridSpec(
        num_scalar_prefetch=1,
        grid=(depth // block,),
        in_specs=[pl.BlockSpec((ROWS, block), lambda k, o: (0, k))] * 8
        + [
            pl.BlockSpec((block, n_q), lambda k, o: (k, 0)),
            pl.BlockSpec((block, wk.shape[1]), lambda k, o: (k, 0)),
            pl.BlockSpec((block, wv.shape[1]), lambda k, o: (k, 0)),
            pl.BlockSpec((tokens, HEAD_DIMENSION), lambda k, o: (0, 0)),
            pl.BlockSpec((tokens, HEAD_DIMENSION), lambda k, o: (0, 0)),
        ],
        out_specs=[
            pl.BlockSpec((tokens, n_q), lambda k, o: (0, 0)),
            pl.BlockSpec((tokens, n_kv), lambda k, o: (0, 0)),
        ],
        scratch_shapes=[
            pltpu.VMEM((tokens, n_q), jnp.float32),
            pltpu.VMEM((tokens, n_kv), jnp.float32),
        ],
    )
    return pl.pallas_call(
        qkv_kernel,
        grid_spec=grid_spec,
        out_shape=[
            jax.ShapeDtypeStruct((tokens, n_q), jnp.bfloat16),
            jax.ShapeDtypeStruct((tokens, n_kv), jnp.bfloat16),
        ],
        compiler_params=pltpu.CompilerParams(vmem_limit_bytes=24 * MIB),
        cost_estimate=pl.CostEstimate(
            flops=2 * tokens * depth * (n_q + n_kv),
            bytes_accessed=2 * depth * (n_q + n_kv + tokens),
            transcendentals=0,
        ),
        name="qkv",
    )(order, *pieces, wq, wk, wv, cos, sin)


def pages_kernel(take_ref, table_ref, pool_ref, buffer_ref, prefix_ref):
    def fill(i, _):
        row = take_ref[i]
        page = pool_ref[jnp.maximum(row, 0)]
        buffer_ref[i] = jnp.where(row >= 0, page, jnp.zeros_like(page))
        return 0

    lax.fori_loop(0, buffer_ref.shape[0], fill, 0, unroll=8)

    def gather(i, _):
        prefix_ref[i] = pool_ref[table_ref[i]]
        return 0

    lax.fori_loop(0, prefix_ref.shape[0], gather, 0, unroll=8)


def build_pages(take, table, pool):
    slots = take.shape[0]
    return pl.pallas_call(
        pages_kernel,
        out_shape=[
            jax.ShapeDtypeStruct((slots,) + pool.shape[1:], pool.dtype),
            jax.ShapeDtypeStruct((table.shape[0],) + pool.shape[1:], pool.dtype),
        ],
        in_specs=[SMEM, SMEM, VMEM],
        out_specs=[VMEM, VMEM],
        compiler_params=pltpu.CompilerParams(vmem_limit_bytes=24 * MIB),
        cost_estimate=pl.CostEstimate(flops=0, bytes_accessed=6 * MIB, transcendentals=0),
        name="pages",
    )(take, table, pool)


def patch_kernel(place_ref, fresh_ref, buffer_ref, out_ref, sems):
    del buffer_ref
    count = fresh_ref.shape[0]
    slots = out_ref.shape[0]

    def copy(i):
        return pltpu.make_async_copy(
            fresh_ref.at[i], out_ref.at[jnp.minimum(place_ref[i], slots - 1)], sems.at[i]
        )

    for i in range(count):
        @pl.when(place_ref[i] < slots)
        def _():
            copy(i).start()

    for i in range(count):
        @pl.when(place_ref[i] < slots)
        def _():
            copy(i).wait()


def patch_pages(place, fresh, buffer):
    return pl.pallas_call(
        patch_kernel,
        out_shape=jax.ShapeDtypeStruct(buffer.shape, buffer.dtype),
        in_specs=[SMEM, VMEM, ANY],
        out_specs=ANY,
        scratch_shapes=[pltpu.SemaphoreType.DMA((fresh.shape[0],))],
        input_output_aliases={2: 0},
        compiler_params=pltpu.CompilerParams(vmem_limit_bytes=8 * MIB),
        cost_estimate=pl.CostEstimate(flops=0, bytes_accessed=4 * fresh.size, transcendentals=0),
        name="patch",
    )(place, fresh, buffer)


TILE = 64


def attention_kernel(order_ref, ends_ref, prefix_len_ref, q_ref, kv_ref, prefix_ref, out_ref, q_s, o_s):
    tokens = q_ref.shape[0]
    heads = q_ref.shape[1] // HEAD_DIMENSION
    tiles = tokens // TILE
    requests = ends_ref.shape[0]
    slots = MAXB * PAGE_TOKENS
    for j in range(tiles):
        for h in range(heads):
            q_s[j, h * TILE : (h + 1) * TILE, :] = q_ref[
                j * TILE : (j + 1) * TILE, h * HEAD_DIMENSION : (h + 1) * HEAD_DIMENSION
            ]
    scale = 1.0 / math.sqrt(HEAD_DIMENSION)
    nt = (((1,), (1,)), ((), ()))

    def body(i, _):
        j, r = i // requests, i % requests
        end = ends_ref[r]
        start = jnp.where(r == 0, 0, ends_ref[jnp.maximum(r - 1, 0)])

        @pl.when((start < (j + 1) * TILE) & (end > j * TILE))
        def _():
            q = q_s[j]
            rows = pl.ds(pl.multiple_of(r * slots, slots), slots)
            s1 = lax.dot_general(
                q, prefix_ref[rows, :HEAD_DIMENSION], nt, preferred_element_type=jnp.float32
            )
            s2 = lax.dot_general(
                q, kv_ref[:, :HEAD_DIMENSION], nt, preferred_element_type=jnp.float32
            )
            slot = lax.broadcasted_iota(jnp.int32, s1.shape, 1)
            s1 = jnp.where(slot < prefix_len_ref[r], s1 * scale, neg_large)
            token = j * TILE + lax.rem(lax.broadcasted_iota(jnp.int32, s2.shape, 0), TILE)
            key = lax.broadcasted_iota(jnp.int32, s2.shape, 1)
            s2 = jnp.where((key >= start) & (key <= token), s2 * scale, neg_large)
            top = jnp.maximum(
                jnp.max(s1, axis=1, keepdims=True), jnp.max(s2, axis=1, keepdims=True)
            )
            p1 = jnp.exp(s1 - top)
            p2 = jnp.exp(s2 - top)
            total = jnp.sum(p1, axis=1, keepdims=True) + jnp.sum(p2, axis=1, keepdims=True)
            inverse = 1.0 / total
            o = jnp.dot(
                (p1 * inverse).astype(jnp.bfloat16),
                prefix_ref[rows, HEAD_DIMENSION:],
                preferred_element_type=jnp.float32,
            ) + jnp.dot(
                (p2 * inverse).astype(jnp.bfloat16),
                kv_ref[:, HEAD_DIMENSION:],
                preferred_element_type=jnp.float32,
            )
            own = j * TILE + lax.rem(lax.broadcasted_iota(jnp.int32, o.shape, 0), TILE)
            mine = (own >= start) & (own < end)
            o_s[j] = jnp.where(mine, o, o_s[j])

        return 0

    lax.fori_loop(0, tiles * requests, body, 0)
    per_tile = TILE // ROWS
    for p in range(8):
        at = order_ref[p]
        tile, part = at // per_tile, at % per_tile
        for h in range(heads):
            out_ref[p * ROWS : (p + 1) * ROWS, h * HEAD_DIMENSION : (h + 1) * HEAD_DIMENSION] = o_s[
                tile, pl.ds(pl.multiple_of(h * TILE + part * ROWS, ROWS), ROWS), :
            ].astype(jnp.bfloat16)


def attend(order, ends, prefix_len, q, kv, prefix):
    tokens, width = q.shape
    heads = width // HEAD_DIMENSION
    work = 2 * tokens * heads * (MAXB * PAGE_TOKENS + tokens) * HEAD_DIMENSION * 2 * 2
    return pl.pallas_call(
        attention_kernel,
        out_shape=jax.ShapeDtypeStruct((tokens, width), jnp.bfloat16),
        in_specs=[SMEM, SMEM, SMEM, VMEM, VMEM, VMEM],
        out_specs=VMEM,
        scratch_shapes=[
            pltpu.VMEM((tokens // TILE, heads * TILE, HEAD_DIMENSION), jnp.bfloat16),
            pltpu.VMEM((tokens // TILE, heads * TILE, HEAD_DIMENSION), jnp.float32),
        ],
        compiler_params=pltpu.CompilerParams(vmem_limit_bytes=24 * MIB),
        cost_estimate=pl.CostEstimate(
            flops=work, bytes_accessed=3 * MIB, transcendentals=2 * tokens * heads * 896
        ),
        name="attention",
    )(order, ends, prefix_len, q, kv, prefix)


def out_kernel(x_ref, w_ref, *outs):
    y = jnp.dot(x_ref[...], w_ref[...], preferred_element_type=jnp.float32).astype(jnp.bfloat16)
    for p in range(8):
        outs[p][...] = y[p * ROWS : (p + 1) * ROWS]


def out_project(x, w):
    tokens, depth = x.shape
    width = w.shape[1]
    block = 1024
    return pl.pallas_call(
        out_kernel,
        grid=(width // block,),
        in_specs=[
            pl.BlockSpec((tokens, depth), lambda n: (0, 0)),
            pl.BlockSpec((depth, block), lambda n: (0, n)),
        ],
        out_specs=[pl.BlockSpec((ROWS, block), lambda n: (0, n))] * 8,
        out_shape=[jax.ShapeDtypeStruct((ROWS, width), jnp.bfloat16)] * 8,
        compiler_params=pltpu.CompilerParams(vmem_limit_bytes=16 * MIB),
        cost_estimate=pl.CostEstimate(
            flops=2 * tokens * depth * width,
            bytes_accessed=2 * (depth * width + tokens * width),
            transcendentals=0,
        ),
        name="out",
    )(x, w)


def token_tables(prefix, new_tokens, new_ends, tokens):
    new_starts = new_ends - new_tokens
    index = jnp.arange(tokens, dtype=jnp.int32)
    request = jnp.sum((index[:, None] >= new_ends[None, :]).astype(jnp.int32), axis=1)
    member = request[:, None] == jnp.arange(new_tokens.shape[0], dtype=jnp.int32)[None, :]
    position = index + jnp.sum(jnp.where(member, (prefix - new_starts)[None, :], 0), axis=1)
    half = HEAD_DIMENSION // 2
    frequency = theta_base ** (-(jnp.arange(half, dtype=jnp.float32) * 2.0) / HEAD_DIMENSION)
    angles = position.astype(jnp.float32)[:, None] * frequency[None, :]
    cosine, sine = jnp.cos(angles), jnp.sin(angles)
    return (
        jnp.concatenate([cosine, cosine], axis=1),
        jnp.concatenate([-sine, sine], axis=1),
    )


def page_plan(prefix, new_tokens, new_ends, full_length, table, owners, devices, fresh_count):
    requests = prefix.shape[0]
    prefix_count = (prefix // PAGE_TOKENS)[:, None]
    new_count = (new_tokens // PAGE_TOKENS)[:, None]
    page_base = ((new_ends - new_tokens) // PAGE_TOKENS)[:, None]
    block = jnp.arange(NB, dtype=jnp.int32)[None, :]
    request = jnp.arange(requests, dtype=jnp.int32)[:, None]
    from_prefix = block < prefix_count
    exists = block < prefix_count + new_count
    finished = (full_length == prefix + new_tokens)[:, None]
    sent = (exists & finished).reshape(-1)
    target = jnp.where(sent, owners, devices)
    rows = target.shape[0]
    row = jnp.arange(rows, dtype=jnp.int32)
    rank = jnp.sum(
        ((target[:, None] == target[None, :]) & (row[None, :] < row[:, None])).astype(jnp.int32),
        axis=1,
    )
    code = jnp.where(sent, target * CAP + rank, devices * CAP)
    place = jnp.arange(devices * CAP, dtype=jnp.int32)
    hit = code[:, None] == place[None, :]
    tags = jnp.sum(jnp.where(hit, row[:, None] + 1, 0), axis=0)
    padded = jnp.pad(table.reshape(requests, MAXB), ((0, 0), (0, NB - MAXB)))
    source = jnp.where(from_prefix, padded, -1).reshape(-1)
    take = jnp.sum(jnp.where(hit, source[:, None] + 1, 0), axis=0) - 1
    fresh_of = jnp.where(exists & ~from_prefix, page_base + block - prefix_count, -1).reshape(-1)
    number = jnp.arange(fresh_count, dtype=jnp.int32)
    fresh_place = jnp.sum(
        jnp.where(fresh_of[None, :] == number[:, None], code[None, :], 0), axis=1
    )
    return tags, take, fresh_place


def on_device(
    hidden_in,
    attn_gain,
    q_weight,
    key_weight_matrix,
    value_weight_matrix,
    o_weight,
    kv_pool,
    block_table,
    request_len,
    prefix_len,
    new_len,
    page_owner,
):
    n_section, n_tp, n_dec = (lax.axis_size(a) for a in ("section", "tp", "dec"))
    devices = n_section * n_tp * n_dec
    x = hidden_in[0]
    tokens = ROWS * n_tp
    normed = normalize(x, attn_gain)

    near_z = send(normed, 0, 1)
    far = send(normed, 2, 0)
    right = send(normed, 3, 0)
    left = send(normed, 1, 0)
    right_z = send(near_z, 3, 0)
    left_z = send(near_z, 1, 0)
    far_z = send(far, 0, 1)
    gathered = (normed, near_z, right, left, right_z, left_z, far, far_z)

    tp = lax.axis_index("tp")
    px, pz = tp // 2, tp % 2
    order = jnp.stack([((px + dx) % (n_tp // 2)) * 2 + (pz ^ dz) for dx, dz in PIECES]).astype(
        jnp.int32
    )

    prefix, new_tokens, full_length = prefix_len[0], new_len[0], request_len[0]
    new_ends = jnp.cumsum(new_tokens).astype(jnp.int32)
    table = block_table[0, 0]
    fresh_count = tokens // PAGE_TOKENS
    cos, sin = token_tables(prefix, new_tokens, new_ends, tokens)
    tags, take, fresh_place = page_plan(
        prefix, new_tokens, new_ends, full_length, table, page_owner[0, :, 0], devices, fresh_count
    )
    pool = kv_pool[0, :, :, 0, :]
    buffer, prefix_pages = build_pages(take, table, pool)

    by_tp = lax.dynamic_index_in_dim(
        tags.reshape(n_section, n_tp, n_dec, CAP), tp, axis=1, keepdims=False
    ).reshape(n_section * n_dec, CAP)
    own_tags = lax.all_to_all(by_tp, ("section", "dec"), split_axis=0, concat_axis=0, tiled=True)
    received_tags = jnp.broadcast_to(
        own_tags.reshape(n_section, 1, n_dec, CAP), (n_section, n_tp, n_dec, CAP)
    ).reshape(1, devices, CAP)

    q, kv = project(
        order, gathered, q_weight[0], key_weight_matrix[0], value_weight_matrix[0], cos, sin
    )
    buffer = patch_pages(
        fresh_place, kv.reshape(fresh_count, PAGE_TOKENS, 2 * HEAD_DIMENSION), buffer
    )
    received_pages = lax.all_to_all(
        buffer.reshape(devices, CAP, PAGE_TOKENS, 2 * HEAD_DIMENSION),
        ("section", "tp", "dec"),
        split_axis=0,
        concat_axis=0,
        tiled=True,
    )

    attended = attend(
        order, new_ends, prefix, q, kv, prefix_pages.reshape(-1, 2 * HEAD_DIMENSION)
    )
    parts = dict(zip(PIECES, out_project(attended, o_weight[0])))

    def total(*terms):
        return sum(t.astype(jnp.float32) for t in terms)

    far_pair = send(parts[2, 1], 0, 1)
    from_left_z = send(parts[1, 1], 1, 0)
    from_right_z = send(parts[3, 1], 3, 0)
    from_left = send(parts[1, 0], 1, 0)
    from_right = send(parts[3, 0], 3, 0)
    from_far = send(total(parts[2, 0], far_pair).astype(jnp.bfloat16), 2, 0)
    from_z = send(
        total(parts[0, 1], from_left_z, from_right_z).astype(jnp.bfloat16), 0, 1
    )
    mixed = total(x, parts[0, 0], from_left, from_right, from_z, from_far).astype(jnp.bfloat16)
    passed = shifted(mixed, "section", 1)[None]
    return passed, received_pages[None, :, :, :, None, :], received_tags


def solution(mesh):
    in_specs = (
        P("section", ("dec", "tp"), None),
        P("section", None),
        P("section", None, "tp"),
        P("section", None, "tp"),
        P("section", None, "tp"),
        P("section", "tp", None),
        P("section", "dec", None, "tp", None),
        P("section", "dec", None),
        P("section", "dec"),
        P("section", "dec"),
        P("section", "dec"),
        P("section", "dec", None),
    )
    out_specs = (
        P("section", ("dec", "tp"), None),
        P(("section", "tp", "dec"), None, None, None, None, None),
        P(("section", "tp", "dec"), None, None),
    )
    return jax.shard_map(
        on_device, mesh=mesh, in_specs=in_specs, out_specs=out_specs, check_vma=False
    )
```

time: 298 us -> 166 us (0.56)
  waiting for transfers between devices: 151 us -> 67.2 us
  local copies, waits for them, and re-layouts: 59.5 us -> 18.5 us
  matrix products: 29.4 us -> 0 us
  Pallas kernels: 0 us -> 25.5 us
  starting transfers between devices: 24.7 us -> 41.5 us
  between operations: 14.4 us -> 0.86 us
  other arithmetic: 16.4 us -> 12 us
    all_gather x1 -> x0, waiting for transfers between devices: 73.2 us -> none  [on_device(): row_piece = lax.all_gather(normalized_hidden, 'tp', axis=0, tiled=True)]
    reduce_scatter x1 -> x0, waiting for transfers between devices: 65.6 us -> none  [on_device(): lax.psum_scatter(jnp.dot(attention_output, o_weight[0], preferred_element...]
    ppermute x1 -> x15, waiting for transfers between devices: 12 us -> 67.2 us  [the longest x14 54.8 us: send(): return lax.ppermute(block, 'tp', tp_route(dx, dz, lax.axis_size('tp')))]
    scatter x2 -> x0, local copies, waits for them, and re-layouts: 33.7 us -> none  [the longest x1 22.9 us: place_pages(): page_buffer = jnp.zeros((devices, capacity) + pages.shape[1:], pages.dtyp...]
    dot_general x6 -> x0, matrix products: 29.4 us -> none  [the longest x1 7.2 us: apply_attention(): jnp.einsum('kgts,skd->tkgd', probabilities, value_row_values, preferred_e...]
    pallas_call x0 -> x6, Pallas kernels: none -> 25.5 us  [the longest x1 8.44 us: project(): pl.pallas_call(qkv_kernel, grid_spec=grid_spec, out_shape=[jax.ShapeDtype...]
    ppermute x1 -> x15, starting transfers between devices: 2.37 us -> 24.3 us  [the longest x14 22.8 us: send(): return lax.ppermute(block, 'tp', tp_route(dx, dz, lax.axis_size('tp')))]
    dot_general x1 -> x0, local copies, waits for them, and re-layouts: 12 us -> none  [on_device(): jnp.dot(row_piece, q_weight[0], preferred_element_type=jnp.float32)]
  transfers between devices with their start and end apart: 5 -> 17, of which waited for: 3 -> 5; matrix products, arithmetic and copies ran while one was open for 20% -> 9% of each run, Pallas kernels for 0% -> 3%
where the time goes in v1:
time: 166 us
  waiting for transfers between devices  67.2 us (40%)
  starting transfers between devices  41.5 us (25%)
  Pallas kernels  25.5 us (15%)
  local copies, waits for them, and re-layouts  18.5 us (11%)
  other arithmetic  12 us (7%)
    ppermute x14, waiting for transfers between devices, send(): return lax.ppermute(block, 'tp', tp_route(dx, dz, lax.axis_size('tp')))  54.8 us
    ppermute x14, starting transfers between devices, send(): return lax.ppermute(block, 'tp', tp_route(dx, dz, lax.axis_size('tp')))  22.8 us
    unnamed x29, local copies, waits for them, and re-layouts  15.8 us
    ppermute x1, waiting for transfers between devices, shifted(): lax.ppermute(block, axis, [((i - distance) % count, i) for i in range(cou...  12.4 us
    all_to_all x1, starting transfers between devices, on_device(): lax.all_to_all(buffer.reshape(devices, CAP, PAGE_TOKENS, 2 * HEAD_DIMENSI...  9.74 us
    pallas_call x1, Pallas kernels, project(): pl.pallas_call(qkv_kernel, grid_spec=grid_spec, out_shape=[jax.ShapeDtype...  8.44 us
    all_to_all x1, starting transfers between devices, on_device(): lax.all_to_all(by_tp, ('section', 'dec'), split_axis=0, concat_axis=0, ti...  7.46 us
    pallas_call x1, Pallas kernels, attend(): pl.pallas_call(attention_kernel, out_shape=jax.ShapeDtypeStruct((tokens,...  6.41 us
  transfers between devices with their start and end apart: 17, of which 5 were waited for; matrix products, arithmetic and copies ran while one was open for 9% of the time, Pallas kernels for 3%

profile of v1, /device:TPU:0, one launch (start us, length us, event | category | flops | bytes accessed | tf_op | source)
XLA Modules:
  0.0 165.6 jit_solution(306154260024361680)
XLA Ops:
  0.7 1.2 copy-done.4
  1.8 0.8 copy-done.7
  2.9 3.2 %collective-permute-start.5 = (bf16[32,8192]{1,0:T(8,128)(2,1)S(1)}, bf16[32,8192]{1,0:T(8,128)(2,1)S(1)}, u32[]{:S(2)}, u32[]{:S(2)}) collective-permute-start(bf16[32,8192]{1,0:T(8,128)(2,1)S(1)} %norm.1.refs_0_), channel_id=1, source_target_pairs={{0,16},{4,20},{8,24},{12,28},{16,0},{20,4},{24,8},{28,12},{1,17},{... | collective-permute-start | bytes 1572872 | tf_op jit(solution)/shard_map/ppermute | solution.py:36
  6.1 0.6 collective-permute-start.2
  6.7 2.6 %collective-permute-start.1 = (bf16[32,8192]{1,0:T(8,128)(2,1)S(1)}, bf16[32,8192]{1,0:T(8,128)(2,1)}, u32[]{:S(2)}, u32[]{:S(2)}) collective-permute-start(bf16[32,8192]{1,0:T(8,128)(2,1)S(1)} %norm.1.refs_0_), channel_id=1, source_target_pairs={{0,24},{4,28},{8,0},{12,4},{16,8},{20,12},{24,16},{28,20},{1,25},{... | collective-permute-start | bytes 1572872 | tf_op jit(solution)/shard_map/ppermute | solution.py:36
  9.3 1.9 %collective-permute-start = (bf16[32,8192]{1,0:T(8,128)(2,1)S(1)}, bf16[32,8192]{1,0:T(8,128)(2,1)}, u32[]{:S(2)}, u32[]{:S(2)}) collective-permute-start(bf16[32,8192]{1,0:T(8,128)(2,1)S(1)} %norm.1.refs_0_), channel_id=1, source_target_pairs={{0,4},{4,0},{8,12},{12,8},{16,20},{20,16},{24,28},{28,24},{1,5},{5... | collective-permute-start | bytes 1572872 | tf_op jit(solution)/shard_map/ppermute | solution.py:36
  11.3 0.8 reduce-window.4
  12.1 0.7 bitcast_compare_fusion
  13.0 0.5 broadcast.231
  13.5 1.3 reduce.3
  14.9 0.7 fusion.4
  16.3 0.7 broadcast_select_fusion
  17.2 0.7 add_select_fusion
  18.1 1.3 copy-done.6
  19.4 0.7 copy-done.9
  20.1 3.7 %pages.1 = (bf16[384,16,256]{2,1,0:T(8,128)(2,1)}, bf16[160,16,256]{2,1,0:T(8,128)(2,1)S(1)}) custom-call(s32[384]{0:T(512)S(1)} %broadcast_add_fusion.take_ref, s32[160]{0:T(256)S(1)} %bitcast.71, bf16[160,16,256]{2,1,0:T(8,128)(2,1)S(1)} %bitcast.68), custom_call_target="tpu_custom_call" | custom-call | bytes 6291456 | tf_op jit(solution)/shard_map/pages/pallas_call | solution.py:156
  23.8 1.1 copy-done.10
  25.0 0.7 fusion.3
  25.9 3.2 %collective-permute-start.3 = (bf16[32,8192]{1,0:T(8,128)(2,1)}, bf16[32,8192]{1,0:T(8,128)(2,1)S(1)}, u32[]{:S(2)}, u32[]{:S(2)}) collective-permute-start(bf16[32,8192]{1,0:T(8,128)(2,1)} %collective-permute-done.refs_1_), channel_id=1, source_target_pairs={{0,24},{4,28},{8,0},{12,4},{16,8},{20,12},{24,16},{28,20},{1,25},{... | collective-permute-start | bytes 1572872 | tf_op jit(solution)/shard_map/ppermute | solution.py:36
  29.2 0.5 fusion.1
  29.9 1.0 collective-permute-done.1.refs_2_
  30.9 10.2 %collective-permute-done.6.refs_7_ = bf16[32,8192]{1,0:T(8,128)(2,1)S(1)} collective-permute-done((bf16[32,8192]{1,0:T(8,128)(2,1)S(1)}, bf16[32,8192]{1,0:T(8,128)(2,1)S(1)}, u32[]{:S(2)}, u32[]{:S(2)}) %collective-permute-start.6) | collective-permute-done | bytes 524320 | tf_op jit(solution)/shard_map/ppermute | solution.py:36
  41.1 3.4 %copy-done = bf16[1,8192,512]{2,1,0:T(8,128)(2,1)S(1)} copy-done((bf16[1,8192,512]{2,1,0:T(8,128)(2,1)S(1)}, bf16[1,8192,512]{2,1,0:T(8,128)(2,1)}, u32[]{:S(2)}) %copy-start) | copy-done | bytes 8388632
  44.5 1.6 copy-done.3
  46.1 8.4 %qkv.1 = (bf16[256,512]{1,0:T(8,128)(2,1)S(1)}, bf16[256,256]{1,0:T(8,128)(2,1)S(1)}) custom-call(s32[8]{0:T(128)S(1)} %stack.35.order.order_ref, bf16[32,8192]{1,0:T(8,128)(2,1)S(1)} %norm.1.refs_0_, bf16[32,8192]{1,0:T(8,128)(2,1)} %collective-permute-done.refs_1_, bf16[32,8192]{1,0:T(8,128)(2,1)} %collective-permute-done.1.refs_2_, ...), custom_call_target="tpu_custom_call" | custom-call | flops 3221225472 | bytes 16777216 | tf_op jit(solution)/shard_map/qkv/pallas_call | solution.py:121
  54.5 6.4 %attention.1.x_ref = bf16[256,512]{1,0:T(8,128)(2,1)S(1)} custom-call(s32[8]{0:T(128)S(1)} %stack.35.order.order_ref, s32[4]{0:T(128)S(1)} %bitcast.73, s32[4]{0:T(128)S(1)} %bitcast.70, bf16[256,512]{1,0:T(8,128)(2,1)S(1)} %get-tuple-element.15.q_ref, bf16[256,256]{1,0:T(8,128)(2,1)S(1)} %get-tuple-element.16.kv_ref, bf16[2560,256]{1,0:T(8,128)(2,1)S(1)} %bitcast.74), custom_call_target="tpu_custom_call" | custom-call | flops 939524096 | bytes 3145728 | tf_op jit(solution)/shard_map/attention/pallas_call | solution.py:279
  61.0 5.3 %out.1 = (bf16[32,8192]{1,0:T(8,128)(2,1)S(1)}, bf16[32,8192]{1,0:T(8,128)(2,1)S(1)}, bf16[32,8192]{1,0:T(8,128)(2,1)S(1)}, bf16[32,8192]{1,0:T(8,128)(2,1)S(1)}...) custom-call(bf16[256,512]{1,0:T(8,128)(2,1)S(1)} %attention.1.x_ref,, ...), custom_call_target="tpu_custom_call" | custom-call | flops 2147483648 | bytes 12582912 | tf_op jit(solution)/shard_map/out/pallas_call | solution.py:306
  66.3 0.8 copy-done.12
  67.1 1.2 collective-permute-start.9
  68.3 2.0 %collective-permute-start.10 = (bf16[32,8192]{1,0:T(8,128)(2,1)}, bf16[32,8192]{1,0:T(8,128)(2,1)}, u32[]{:S(2)}, u32[]{:S(2)}) collective-permute-start(bf16[32,8192]{1,0:T(8,128)(2,1)} %get-tuple-element.23), channel_id=1, source_target_pairs={{0,24},{4,28},{8,0},{12,4},{16,8},{20,12},{24,16},{28,20},{1,25},{... | collective-permute-start | bytes 1572872 | tf_op jit(solution)/shard_map/ppermute | solution.py:36
  70.6 0.6 constant_dynamic-slice_fusion
  71.2 7.5 %all-to-all-start.1 = ((s32[16,1,3]{2,1,0:T(1,128)}), s32[16,1,3]{2,1,0:T(1,128)S(1)}, u32[]{:S(2)}, u32[]{:S(2)}) async-start(s32[16,1,3]{2,1,0:T(1,128)} %bitcast.30), calls=%async_computation.1 | async-start | bytes 16384 | tf_op jit(solution)/shard_map/all_to_all | solution.py:423
  79.1 3.0 %collective-permute-start.8 = (bf16[32,8192]{1,0:T(8,128)(2,1)S(1)}, bf16[32,8192]{1,0:T(8,128)(2,1)}, u32[]{:S(2)}, u32[]{:S(2)}) collective-permute-start(bf16[32,8192]{1,0:T(8,128)(2,1)S(1)} %get-tuple-element.20), channel_id=1, source_target_pairs={{0,24},{4,28},{8,0},{12,4},{16,8},{20,12},{24,16},{28,20},{1,25},{... | collective-permute-start | bytes 1572872 | tf_op jit(solution)/shard_map/ppermute | solution.py:36
  82.1 1.0 collective-permute-start.12
  83.1 1.3 patch.1
  84.5 2.2 %add_convert_fusion.2 = bf16[32,8192]{1,0:T(8,128)(2,1)} fusion(bf16[32,8192]{1,0:T(8,128)(2,1)} %collective-permute-done.10, bf16[32,8192]{1,0:T(8,128)(2,1)} %collective-permute-done.9, bf16[32,8192]{1,0:T(8,128)(2,1)S(1)} %get-tuple-element.21), kind=kLoop, calls=%fused_computation.2 | loop fusion | flops 1572864 | bytes 2097152 | tf_op jit(solution)/shard_map/convert_element_type | solution.py:457
  86.6 1.0 collective-permute-start.11
  87.7 9.7 %all-to-all-start = ((bf16[128,3,16,256]{3,2,1,0:T(8,128)(2,1)}), bf16[128,3,16,256]{3,2,1,0:T(8,128)(2,1)}, u32[]{:S(2)}, u32[]{:S(2)}) async-start(bf16[128,3,16,256]{3,2,1,0:T(8,128)(2,1)} %bitcast.26), calls=%async_computation | async-start | bytes 6291456 | tf_op jit(solution)/shard_map/all_to_all | solution.py:434
  97.4 1.2 add_convert_fusion.1
  98.6 2.5 %collective-permute-start.13 = (bf16[32,8192]{1,0:T(8,128)(2,1)S(1)}, bf16[32,8192]{1,0:T(8,128)(2,1)S(1)}, u32[]{:S(2)}, u32[]{:S(2)}) collective-permute-start(bf16[32,8192]{1,0:T(8,128)(2,1)S(1)} %add_convert_fusion.1), channel_id=1, source_target_pairs={{0,16},{4,20},{8,24},{12,28},{16,0},{20,4},{24,8},{28,12},{1,17},{... | collective-permute-start | bytes 1572872 | tf_op jit(solution)/shard_map/ppermute | solution.py:36
  101.1 38.9 %collective-permute-done.11 = bf16[32,8192]{1,0:T(8,128)(2,1)} collective-permute-done((bf16[32,8192]{1,0:T(8,128)(2,1)}, bf16[32,8192]{1,0:T(8,128)(2,1)}, u32[]{:S(2)}, u32[]{:S(2)}) %collective-permute-start.11) | collective-permute-done | bytes 524320 | tf_op jit(solution)/shard_map/ppermute | solution.py:36
  140.0 4.7 %collective-permute-done.13 = bf16[32,8192]{1,0:T(8,128)(2,1)S(1)} collective-permute-done((bf16[32,8192]{1,0:T(8,128)(2,1)S(1)}, bf16[32,8192]{1,0:T(8,128)(2,1)S(1)}, u32[]{:S(2)}, u32[]{:S(2)}) %collective-permute-start.13) | collective-permute-done | bytes 524320 | tf_op jit(solution)/shard_map/ppermute | solution.py:36
  144.7 1.6 add_convert_fusion
  146.3 1.5 collective-permute-start.14
  147.9 0.7 reshape.306
  148.6 12.4 %collective-permute-done.14 = bf16[32,8192]{1,0:T(8,128)(2,1)S(1)} collective-permute-done((bf16[32,8192]{1,0:T(8,128)(2,1)S(1)}, bf16[32,8192]{1,0:T(8,128)(2,1)S(1)}, u32[]{:S(2)}, u32[]{:S(2)}) %collective-permute-start.14) | collective-permute-done | bytes 524320 | tf_op jit(solution)/shard_map/ppermute | solution.py:41
  161.0 0.8 copy.40
  161.8 3.8 %copy.41 = bf16[1,128,3,16,1,256]{5,3,4,2,1,0:T(8,128)(2,1)} copy(bf16[1,128,3,16,1,256]{5,3,4,2,1,0:T(8,128)(2,1)} %bitcast.27) | data formatting | bytes 6291456
  (62 shorter events, 3.1 us)
Async XLA Ops:
  0.6 40.5 %copy-start.2 = (bf16[1,8192,128]{2,1,0:T(8,128)(2,1)S(1)}, bf16[1,8192,128]{2,1,0:T(8,128)(2,1)}, u32[]{:S(2)}) copy-start(bf16[1,8192,128]{2,1,0:T(8,128)(2,1)} %param.15) | copy-start | bytes 6291460
  0.6 1.2 copy-start.4
  1.8 0.8 copy-start.7
  2.9 26.2 %collective-permute-start.5 = (bf16[32,8192]{1,0:T(8,128)(2,1)S(1)}, bf16[32,8192]{1,0:T(8,128)(2,1)S(1)}, u32[]{:S(2)}, u32[]{:S(2)}) collective-permute-start(bf16[32,8192]{1,0:T(8,128)(2,1)S(1)} %norm.1.refs_0_), channel_id=1, source_target_pairs={{0,16},{4,20},{8,24},{12,28},{16,0},{20,4},{24,8},{28,12},{1,17},{... | collective-permute-start | bytes 1572872 | tf_op jit(solution)/shard_map/ppermute | solution.py:36
  6.1 23.8 %collective-permute-start.2 = (bf16[32,8192]{1,0:T(8,128)(2,1)S(1)}, bf16[32,8192]{1,0:T(8,128)(2,1)}, u32[]{:S(2)}, u32[]{:S(2)}) collective-permute-start(bf16[32,8192]{1,0:T(8,128)(2,1)S(1)} %norm.1.refs_0_), channel_id=1, source_target_pairs={{0,8},{4,12},{8,16},{12,20},{16,24},{20,28},{24,0},{28,4},{1,9},{5... | collective-permute-start | bytes 1572872 | tf_op jit(solution)/shard_map/ppermute | solution.py:36
  6.7 24.2 %collective-permute-start.1 = (bf16[32,8192]{1,0:T(8,128)(2,1)S(1)}, bf16[32,8192]{1,0:T(8,128)(2,1)}, u32[]{:S(2)}, u32[]{:S(2)}) collective-permute-start(bf16[32,8192]{1,0:T(8,128)(2,1)S(1)} %norm.1.refs_0_), channel_id=1, source_target_pairs={{0,24},{4,28},{8,0},{12,4},{16,8},{20,12},{24,16},{28,20},{1,25},{... | collective-permute-start | bytes 1572872 | tf_op jit(solution)/shard_map/ppermute | solution.py:36
  9.3 16.5 %collective-permute-start = (bf16[32,8192]{1,0:T(8,128)(2,1)S(1)}, bf16[32,8192]{1,0:T(8,128)(2,1)}, u32[]{:S(2)}, u32[]{:S(2)}) collective-permute-start(bf16[32,8192]{1,0:T(8,128)(2,1)S(1)} %norm.1.refs_0_), channel_id=1, source_target_pairs={{0,4},{4,0},{8,12},{12,8},{16,20},{20,16},{24,28},{28,24},{1,5},{5... | collective-permute-start | bytes 1572872 | tf_op jit(solution)/shard_map/ppermute | solution.py:36
  18.1 1.3 copy-start.6
  19.4 0.7 copy-start.9
  23.8 1.1 copy-start.10
  25.8 15.3 %collective-permute-start.4 = (bf16[32,8192]{1,0:T(8,128)(2,1)}, bf16[32,8192]{1,0:T(8,128)(2,1)S(1)}, u32[]{:S(2)}, u32[]{:S(2)}) collective-permute-start(bf16[32,8192]{1,0:T(8,128)(2,1)} %collective-permute-done.refs_1_), channel_id=1, source_target_pairs={{0,8},{4,12},{8,16},{12,20},{16,24},{20,28},{24,0},{28,4},{1,9},{5... | collective-permute-start | bytes 1572872 | tf_op jit(solution)/shard_map/ppermute | solution.py:36
  25.9 15.2 %collective-permute-start.3 = (bf16[32,8192]{1,0:T(8,128)(2,1)}, bf16[32,8192]{1,0:T(8,128)(2,1)S(1)}, u32[]{:S(2)}, u32[]{:S(2)}) collective-permute-start(bf16[32,8192]{1,0:T(8,128)(2,1)} %collective-permute-done.refs_1_), channel_id=1, source_target_pairs={{0,24},{4,28},{8,0},{12,4},{16,8},{20,12},{24,16},{28,20},{1,25},{... | collective-permute-start | bytes 1572872 | tf_op jit(solution)/shard_map/ppermute | solution.py:36
  29.1 12.0 %collective-permute-start.6 = (bf16[32,8192]{1,0:T(8,128)(2,1)S(1)}, bf16[32,8192]{1,0:T(8,128)(2,1)S(1)}, u32[]{:S(2)}, u32[]{:S(2)}) collective-permute-start(bf16[32,8192]{1,0:T(8,128)(2,1)S(1)} %collective-permute-done.5.refs_6_), channel_id=1, source_target_pairs={{0,4},{4,0},{8,12},{12,8},{16,20},{20,16},{24,28},{28,24},{1,5},{5... | collective-permute-start | bytes 1572872 | tf_op jit(solution)/shard_map/ppermute | solution.py:36
  41.1 3.4 %copy-start = (bf16[1,8192,512]{2,1,0:T(8,128)(2,1)S(1)}, bf16[1,8192,512]{2,1,0:T(8,128)(2,1)}, u32[]{:S(2)}) copy-start(bf16[1,8192,512]{2,1,0:T(8,128)(2,1)} %param.14) | copy-start | bytes 25165828
  44.5 1.6 copy-start.3
  46.1 8.5 %copy-start.8 = (s32[1,4]{1,0:T(1,128)S(1)}, s32[1,4]{1,0:T(1,128)}, u32[]{:S(2)}) copy-start(s32[1,4]{1,0:T(1,128)} %param.21) | copy-start | bytes 52
  46.1 8.5 %copy-start.11 = (bf16[160,16,256]{2,1,0:T(8,128)(2,1)S(1)}, bf16[160,16,256]{2,1,0:T(8,128)(2,1)}, u32[]{:S(2)}) copy-start(bf16[160,16,256]{2,1,0:T(8,128)(2,1)} %copy-done.10) | copy-start | bytes 3932164
  46.1 14.9 %copy-start.1 = (bf16[1,512,8192]{2,1,0:T(8,128)(2,1)S(1)}, bf16[1,512,8192]{2,1,0:T(8,128)(2,1)}, u32[]{:S(2)}) copy-start(bf16[1,512,8192]{2,1,0:T(8,128)(2,1)} %param.17) | copy-start | bytes 25165828
  66.3 0.8 copy-start.12
  67.1 17.3 %collective-permute-start.9 = (bf16[32,8192]{1,0:T(8,128)(2,1)}, bf16[32,8192]{1,0:T(8,128)(2,1)}, u32[]{:S(2)}, u32[]{:S(2)}) collective-permute-start(bf16[32,8192]{1,0:T(8,128)(2,1)} %get-tuple-element.22), channel_id=1, source_target_pairs={{0,8},{4,12},{8,16},{12,20},{16,24},{20,28},{24,0},{28,4},{1,9},{5... | collective-permute-start | bytes 1572872 | tf_op jit(solution)/shard_map/ppermute | solution.py:36
  68.3 16.2 %collective-permute-start.10 = (bf16[32,8192]{1,0:T(8,128)(2,1)}, bf16[32,8192]{1,0:T(8,128)(2,1)}, u32[]{:S(2)}, u32[]{:S(2)}) collective-permute-start(bf16[32,8192]{1,0:T(8,128)(2,1)} %get-tuple-element.23), channel_id=1, source_target_pairs={{0,24},{4,28},{8,0},{12,4},{16,8},{20,12},{24,16},{28,20},{1,25},{... | collective-permute-start | bytes 1572872 | tf_op jit(solution)/shard_map/ppermute | solution.py:36
  71.2 16.5 %all-to-all-start.1 = ((s32[16,1,3]{2,1,0:T(1,128)}), s32[16,1,3]{2,1,0:T(1,128)S(1)}, u32[]{:S(2)}, u32[]{:S(2)}) async-start(s32[16,1,3]{2,1,0:T(1,128)} %bitcast.30), calls=%async_computation.1 | async-start | bytes 16384 | tf_op jit(solution)/shard_map/all_to_all | solution.py:423
  78.8 22.3 %collective-permute-start.7 = (bf16[32,8192]{1,0:T(8,128)(2,1)S(1)}, bf16[32,8192]{1,0:T(8,128)(2,1)S(1)}, u32[]{:S(2)}, u32[]{:S(2)}) collective-permute-start(bf16[32,8192]{1,0:T(8,128)(2,1)S(1)} %get-tuple-element.19), channel_id=1, source_target_pairs={{0,8},{4,12},{8,16},{12,20},{16,24},{20,28},{24,0},{28,4},{1,9},{5... | collective-permute-start | bytes 1572872 | tf_op jit(solution)/shard_map/ppermute | solution.py:36
  79.1 22.0 %collective-permute-start.8 = (bf16[32,8192]{1,0:T(8,128)(2,1)S(1)}, bf16[32,8192]{1,0:T(8,128)(2,1)}, u32[]{:S(2)}, u32[]{:S(2)}) collective-permute-start(bf16[32,8192]{1,0:T(8,128)(2,1)S(1)} %get-tuple-element.20), channel_id=1, source_target_pairs={{0,24},{4,28},{8,0},{12,4},{16,8},{20,12},{24,16},{28,20},{1,25},{... | collective-permute-start | bytes 1572872 | tf_op jit(solution)/shard_map/ppermute | solution.py:36
  82.1 15.3 %collective-permute-start.12 = (bf16[32,8192]{1,0:T(8,128)(2,1)}, bf16[32,8192]{1,0:T(8,128)(2,1)}, u32[]{:S(2)}, u32[]{:S(2)}) collective-permute-start(bf16[32,8192]{1,0:T(8,128)(2,1)} %copy-done.12), channel_id=1, source_target_pairs={{0,4},{4,0},{8,12},{12,8},{16,20},{20,16},{24,28},{28,24},{1,5},{5... | collective-permute-start | bytes 1572872 | tf_op jit(solution)/shard_map/ppermute | solution.py:36
  86.6 53.3 %collective-permute-start.11 = (bf16[32,8192]{1,0:T(8,128)(2,1)}, bf16[32,8192]{1,0:T(8,128)(2,1)}, u32[]{:S(2)}, u32[]{:S(2)}) collective-permute-start(bf16[32,8192]{1,0:T(8,128)(2,1)} %add_convert_fusion.2), channel_id=1, source_target_pairs={{0,4},{4,0},{8,12},{12,8},{16,20},{20,16},{24,28},{28,24},{1,5},{5... | collective-permute-start | bytes 1572872 | tf_op jit(solution)/shard_map/ppermute | solution.py:36
  87.7 57.0 %copy-start.5 = (bf16[1,32,8192]{2,1,0:T(8,128)(2,1)S(1)}, bf16[1,32,8192]{2,1,0:T(8,128)(2,1)}, u32[]{:S(2)}) copy-start(bf16[1,32,8192]{2,1,0:T(8,128)(2,1)} %param.12) | copy-start | bytes 1572868
  87.7 73.4 %all-to-all-start = ((bf16[128,3,16,256]{3,2,1,0:T(8,128)(2,1)}), bf16[128,3,16,256]{3,2,1,0:T(8,128)(2,1)}, u32[]{:S(2)}, u32[]{:S(2)}) async-start(bf16[128,3,16,256]{3,2,1,0:T(8,128)(2,1)} %bitcast.26), calls=%async_computation | async-start | bytes 6291456 | tf_op jit(solution)/shard_map/all_to_all | solution.py:434
  98.6 46.1 %collective-permute-start.13 = (bf16[32,8192]{1,0:T(8,128)(2,1)S(1)}, bf16[32,8192]{1,0:T(8,128)(2,1)S(1)}, u32[]{:S(2)}, u32[]{:S(2)}) collective-permute-start(bf16[32,8192]{1,0:T(8,128)(2,1)S(1)} %add_convert_fusion.1), channel_id=1, source_target_pairs={{0,16},{4,20},{8,24},{12,28},{16,0},{20,4},{24,8},{28,12},{1,17},{... | collective-permute-start | bytes 1572872 | tf_op jit(solution)/shard_map/ppermute | solution.py:36
  146.3 14.7 %collective-permute-start.14 = (bf16[32,8192]{1,0:T(8,128)(2,1)S(1)}, bf16[32,8192]{1,0:T(8,128)(2,1)S(1)}, u32[]{:S(2)}, u32[]{:S(2)}) collective-permute-start(bf16[32,8192]{1,0:T(8,128)(2,1)S(1)} %add_convert_fusion), channel_id=1, source_target_pairs={{96,0},{0,32},{32,64},{64,96},{97,1},{1,33},{33,65},{65,97},{98,2}... | collective-permute-start | bytes 1572872 | tf_op jit(solution)/shard_map/ppermute | solution.py:41

commit v2 on v1

v2 whole, which is shorter than its diff:
```python
import functools
import math

import jax
import jax.numpy as jnp
from jax import lax
from jax.experimental import pallas as pl
from jax.experimental.pallas import tpu as pltpu
from jax.sharding import PartitionSpec as P

HEAD_DIMENSION = 128
PAGE_TOKENS = 16
MAXB = 40
NB = 56
CAP = 3
EARLY = 2
ROWS = 32

theta_base = 500000.0
eps_norm = 1e-05
neg_large = -1e30

MIB = 1 << 20
VMEM = pl.BlockSpec(memory_space=pltpu.VMEM)
SMEM = pl.BlockSpec(memory_space=pltpu.SMEM)
ANY = pl.BlockSpec(memory_space=pl.ANY)

PIECES = ((0, 0), (0, 1), (1, 0), (3, 0), (1, 1), (3, 1), (2, 0), (2, 1))


def tp_route(dx, dz, n_tp):
    nx = n_tp // 2
    return [(x * 2 + z, ((x + dx) % nx) * 2 + (z ^ dz)) for x in range(nx) for z in range(2)]


def send(block, dx, dz):
    return lax.ppermute(block, "tp", tp_route(dx, dz, lax.axis_size("tp")))


def shifted(block, axis, distance):
    count = lax.axis_size(axis)
    return lax.ppermute(block, axis, [((i - distance) % count, i) for i in range(count)])


def send_on(block, dx, dz):
    n_section, n_tp = lax.axis_size("section"), lax.axis_size("tp")
    pairs = [
        (s * n_tp + a, ((s + 1) % n_section) * n_tp + b)
        for s in range(n_section)
        for a, b in tp_route(dx, dz, n_tp)
    ]
    return lax.ppermute(block, ("section", "tp"), pairs)


def norm_kernel(x_ref, gain_ref, out_ref, x_s, gain_s, sems):
    copies = (
        pltpu.make_async_copy(x_ref, x_s, sems.at[0]),
        pltpu.make_async_copy(gain_ref, gain_s, sems.at[1]),
    )
    for copy in copies:
        copy.start()
    for copy in copies:
        copy.wait()
    x = x_s[...].astype(jnp.float32)
    scale = lax.rsqrt(jnp.mean(x * x, axis=-1, keepdims=True) + eps_norm)
    out_ref[...] = (x * scale * gain_s[...]).astype(jnp.bfloat16)


def in_hbm(array):
    return pltpu.with_memory_space_constraint(array, pltpu.HBM)


def in_vmem(array):
    return pltpu.with_memory_space_constraint(array, pltpu.VMEM)


def normalize(x, gain):
    return pl.pallas_call(
        norm_kernel,
        out_shape=jax.ShapeDtypeStruct(x.shape, jnp.bfloat16),
        in_specs=[ANY, ANY],
        out_specs=VMEM,
        scratch_shapes=[
            pltpu.VMEM(x.shape, x.dtype),
            pltpu.VMEM(gain.shape, gain.dtype),
            pltpu.SemaphoreType.DMA((2,)),
        ],
        compiler_params=pltpu.CompilerParams(vmem_limit_bytes=16 * MIB),
        cost_estimate=pl.CostEstimate(flops=4 * x.size, bytes_accessed=4 * x.size, transcendentals=0),
        name="norm",
    )(in_hbm(x), in_hbm(gain))


def project_rows(pieces, w_ref, acc_ref):
    depth = w_ref.shape[0]
    block = 2048
    for c in range(depth // block):
        cols = slice(c * block, (c + 1) * block)
        x = jnp.concatenate([p[:, cols] for p in pieces], axis=0)
        part = jnp.dot(x, w_ref[cols, :], preferred_element_type=jnp.float32)
        acc_ref[...] = part if c == 0 else acc_ref[...] + part


def rotate(v, cos, sin):
    return v * cos + pltpu.roll(v, HEAD_DIMENSION // 2, 1) * sin


def qkv_kernel(order, place, *refs):
    pieces = refs[:8]
    wq, wkv, cos_ref, sin_ref = refs[8:12]
    q_ref, kv_ref, early_ref, late_ref, acc_q, acc_kv, sems = refs[14:]
    slots = late_ref.shape[0] * CAP
    count = kv_ref.shape[0] // PAGE_TOKENS
    heads = acc_q.shape[1] // HEAD_DIMENSION

    project_rows(pieces, wkv, acc_kv)
    for p in range(8):
        rows = pl.ds(pl.multiple_of(order[p] * ROWS, ROWS), ROWS)
        here = slice(p * ROWS, (p + 1) * ROWS)
        kv_ref[rows, :HEAD_DIMENSION] = rotate(
            acc_kv[here, :HEAD_DIMENSION], cos_ref[rows, :], sin_ref[rows, :]
        ).astype(jnp.bfloat16)
        kv_ref[rows, HEAD_DIMENSION:] = acc_kv[here, HEAD_DIMENSION:].astype(jnp.bfloat16)

    def each(i, act):
        at = jnp.minimum(place[0, i], slots - 1)
        owner, slot = at // CAP, at % CAP
        page = kv_ref.at[pl.ds(i * PAGE_TOKENS, PAGE_TOKENS), :]

        @pl.when((place[0, i] < slots) & (slot < EARLY))
        def _():
            to = early_ref.at[owner * EARLY + jnp.minimum(slot, EARLY - 1)]
            act(pltpu.make_async_copy(page, to, sems.at[i]))

        @pl.when((place[0, i] < slots) & (slot >= EARLY))
        def _():
            act(pltpu.make_async_copy(page, late_ref.at[owner], sems.at[i]))

    for i in range(count):
        each(i, lambda copy: copy.start())

    project_rows(pieces, wq, acc_q)
    for p in range(8):
        rows = pl.ds(pl.multiple_of(order[p] * ROWS, ROWS), ROWS)
        here = slice(p * ROWS, (p + 1) * ROWS)
        for h in range(heads):
            cols = slice(h * HEAD_DIMENSION, (h + 1) * HEAD_DIMENSION)
            q_ref[rows, cols] = rotate(
                acc_q[here, cols], cos_ref[rows, :], sin_ref[rows, :]
            ).astype(jnp.bfloat16)

    for i in range(count):
        each(i, lambda copy: copy.wait())


def project(order, place, pieces, wq, wkv, cos, sin, early, late):
    depth, n_q = wq.shape
    n_kv = wkv.shape[1]
    tokens = 8 * ROWS
    return pl.pallas_call(
        qkv_kernel,
        in_specs=[SMEM, SMEM] + [VMEM] * 12 + [ANY, ANY],
        out_specs=[VMEM, VMEM, ANY, ANY],
        out_shape=[
            jax.ShapeDtypeStruct((tokens, n_q), jnp.bfloat16),
            jax.ShapeDtypeStruct((tokens, n_kv), jnp.bfloat16),
            pltpu.HBM(early.shape, early.dtype),
            pltpu.HBM(late.shape, late.dtype),
        ],
        scratch_shapes=[
            pltpu.VMEM((tokens, n_q), jnp.float32),
            pltpu.VMEM((tokens, n_kv), jnp.float32),
            pltpu.SemaphoreType.DMA((tokens // PAGE_TOKENS,)),
        ],
        input_output_aliases={14: 2, 15: 3},
        compiler_params=pltpu.CompilerParams(vmem_limit_bytes=12 * MIB),
        cost_estimate=pl.CostEstimate(
            flops=2 * tokens * depth * (n_q + n_kv),
            bytes_accessed=2 * depth * (n_q + n_kv + tokens),
            transcendentals=0,
        ),
        name="qkv",
    )(order, place, *pieces, in_vmem(wq), in_vmem(wkv), cos, sin, early, late)


def prepare_kernel(
    devices,
    prefix_len_in,
    new_len_in,
    full_len_in,
    table_in,
    owner_in,
    pool_in,
    frequency_ref,
    wq_ref,
    wk_ref,
    wv_ref,
    angles_ref,
    early_ref,
    late_ref,
    prefix_ref,
    place_ref,
    wq_out,
    wkv_out,
    prefix_len_ref,
    new_len_ref,
    full_len_ref,
    table_ref,
    owner_ref,
    pool_ref,
    take_v,
    take_s,
    sems,
):
    pairs = (
        (prefix_len_in, prefix_len_ref),
        (new_len_in, new_len_ref),
        (full_len_in, full_len_ref),
        (table_in, table_ref),
        (owner_in, owner_ref),
        (pool_in, pool_ref),
        (wk_ref, wkv_out.at[:, pl.ds(0, HEAD_DIMENSION)]),
        (wv_ref, wkv_out.at[:, pl.ds(HEAD_DIMENSION, HEAD_DIMENSION)]),
        (wq_ref, wq_out),
    )
    copies = [pltpu.make_async_copy(a, b, sems.at[i]) for i, (a, b) in enumerate(pairs)]
    for copy in copies:
        copy.start()
    for copy in copies[:5]:
        copy.wait()

    requests = prefix_len_ref.shape[1]
    rows = owner_ref.shape[1]
    old = [prefix_len_ref[0, r] // PAGE_TOKENS for r in range(requests)]
    new = [new_len_ref[0, r] // PAGE_TOKENS for r in range(requests)]
    open_ = [
        full_len_ref[0, r] != prefix_len_ref[0, r] + new_len_ref[0, r] for r in range(requests)
    ]
    base = [0]
    for r in range(requests - 1):
        base.append(base[r] + new[r])

    def by_request(row, values):
        out = jnp.full(row.shape, values[0], jnp.int32)
        for r in range(1, requests):
            out = jnp.where(row >= r * NB, values[r], out)
        return out

    def targets(row, owner):
        block = row - by_request(row, [r * NB for r in range(requests)])
        kept = by_request(row, [jnp.where(open_[r], 0, old[r] + new[r]) for r in range(requests)])
        return block, jnp.where(block < kept, owner, devices)

    row = lax.broadcasted_iota(jnp.int32, (rows, 1), 0)
    lane = lax.broadcasted_iota(jnp.int32, (1, rows), 1)
    owner = owner_ref[...]
    block, target = targets(
        row, jnp.sum(jnp.where(lane == row, owner, 0), axis=1, keepdims=True)
    )
    _, across = targets(lane, owner)
    rank = jnp.sum(
        jnp.where((across == target) & (lane < row), 1, 0), axis=1, keepdims=True
    )
    slots = devices * CAP
    code = jnp.where(target < devices, target * CAP + rank, slots)
    ages = by_request(row, old)
    first = by_request(row, [r * MAXB for r in range(requests)])
    source = jnp.where(block < ages, first + block + 1, 0)
    hit = code == lax.broadcasted_iota(jnp.int32, (1, slots), 1)
    take_v[...] = jnp.sum(jnp.where(hit, source, 0), axis=0, keepdims=True) - 1
    taken = pltpu.make_async_copy(take_v, take_s, sems.at[len(pairs)])
    taken.start()
    fresh = jnp.where(
        (block >= ages) & (block < by_request(row, [old[r] + new[r] for r in range(requests)])),
        by_request(row, base) + block - ages,
        -1,
    )
    number = lax.broadcasted_iota(jnp.int32, place_ref.shape, 1)
    place_ref[...] = jnp.sum(jnp.where(fresh == number, code, 0), axis=0, keepdims=True)

    token = lax.broadcasted_iota(jnp.int32, (angles_ref.shape[0], 1), 0)
    shift = jnp.full(token.shape, prefix_len_ref[0, 0], jnp.int32)
    for r in range(1, requests):
        start = base[r] * PAGE_TOKENS
        shift = jnp.where(token >= start, prefix_len_ref[0, r] - start, shift)
    angles_ref[...] = (token + shift).astype(jnp.float32) * frequency_ref[...]

    copies[5].wait()

    def gather(i, _):
        prefix_ref[i] = pool_ref[table_ref[0, i]]
        return 0

    lax.fori_loop(0, prefix_ref.shape[0], gather, 0, unroll=8)
    taken.wait()

    def page(i):
        at = take_s[0, i]
        found = pool_ref[table_ref[0, jnp.maximum(at, 0)]]
        return jnp.where(at >= 0, found, jnp.zeros_like(found))

    def fill(o, _):
        for j in range(EARLY):
            early_ref[o * EARLY + j] = page(o * CAP + j)
        late_ref[o] = page(o * CAP + EARLY)
        return 0

    lax.fori_loop(0, devices, fill, 0, unroll=4)
    for copy in copies[6:]:
        copy.wait()


def prepare(
    devices, tokens, prefix_len, new_len, full_len, table, owner, pool, wq, wk, wv
):
    slots = devices * CAP
    half = HEAD_DIMENSION // 2
    frequency = theta_base ** (-(jnp.arange(half, dtype=jnp.float32) * 2.0) / HEAD_DIMENSION)
    depth = wq.shape[0]
    return pl.pallas_call(
        functools.partial(prepare_kernel, devices),
        out_shape=[
            jax.ShapeDtypeStruct((tokens, half), jnp.float32),
            pltpu.HBM((devices * EARLY,) + pool.shape[1:], pool.dtype),
            pltpu.HBM((devices,) + pool.shape[1:], pool.dtype),
            jax.ShapeDtypeStruct((table.shape[1],) + pool.shape[1:], pool.dtype),
            jax.ShapeDtypeStruct((1, 128), jnp.int32),
            pltpu.VMEM(wq.shape, wq.dtype),
            pltpu.VMEM((depth, 2 * HEAD_DIMENSION), wk.dtype),
        ],
        in_specs=[ANY] * 6 + [VMEM] + [ANY] * 3,
        out_specs=[VMEM] * 7,
        scratch_shapes=[
            pltpu.SMEM(prefix_len.shape, jnp.int32),
            pltpu.SMEM(new_len.shape, jnp.int32),
            pltpu.SMEM(full_len.shape, jnp.int32),
            pltpu.SMEM(table.shape, jnp.int32),
            pltpu.VMEM(owner.shape, jnp.int32),
            pltpu.VMEM(pool.shape, pool.dtype),
            pltpu.VMEM((1, slots), jnp.int32),
            pltpu.SMEM((1, slots), jnp.int32),
            pltpu.SemaphoreType.DMA((10,)),
        ],
        compiler_params=pltpu.CompilerParams(vmem_limit_bytes=16 * MIB),
        cost_estimate=pl.CostEstimate(flops=0, bytes_accessed=20 * MIB, transcendentals=0),
        name="prepare",
    )(
        in_hbm(prefix_len),
        in_hbm(new_len),
        in_hbm(full_len),
        in_hbm(table),
        in_hbm(owner),
        in_hbm(pool),
        frequency[None, :],
        in_hbm(wq),
        in_hbm(wk),
        in_hbm(wv),
    )


TILE = 64


def attention_kernel(
    order_ref, new_len_ref, prefix_len_ref, q_ref, kv_ref, prefix_in, w_ref, *rest
):
    outs, (prefix_ref, x_ref, q_s, o_s, w_s, y_s, sems, out_sems, prefix_sem) = rest[:8], rest[8:]
    prefix_copy = pltpu.make_async_copy(prefix_in, prefix_ref, prefix_sem)
    prefix_copy.start()
    chunk = w_s.shape[2]

    def weights(c):
        return pltpu.make_async_copy(w_ref.at[:, pl.ds(c * chunk, chunk)], w_s.at[c], sems.at[c])

    def written(c, p):
        return pltpu.make_async_copy(
            y_s.at[c, pl.ds(p * ROWS, ROWS), :],
            outs[p].at[:, pl.ds(c * chunk, chunk)],
            out_sems.at[c, p],
        )


    tokens = q_ref.shape[0]
    heads = q_ref.shape[1] // HEAD_DIMENSION
    tiles = tokens // TILE
    requests = new_len_ref.shape[1]
    slots = MAXB * PAGE_TOKENS
    for j in range(tiles):
        for h in range(heads):
            q_s[j, h * TILE : (h + 1) * TILE, :] = q_ref[
                j * TILE : (j + 1) * TILE, h * HEAD_DIMENSION : (h + 1) * HEAD_DIMENSION
            ]
    prefix_copy.wait()
    for c in range(w_s.shape[0]):
        weights(c).start()
    scale = 1.0 / math.sqrt(HEAD_DIMENSION)
    nt = (((1,), (1,)), ((), ()))

    def body(i, _):
        j, r = i // requests, i % requests
        start = 0
        for i in range(requests - 1):
            start = start + jnp.where(i < r, new_len_ref[0, i], 0)
        end = start + new_len_ref[0, r]

        @pl.when((start < (j + 1) * TILE) & (end > j * TILE))
        def _():
            q = q_s[j]
            rows = pl.ds(pl.multiple_of(r * slots, slots), slots)
            s1 = lax.dot_general(
                q, prefix_ref[rows, :HEAD_DIMENSION], nt, preferred_element_type=jnp.float32
            )
            s2 = lax.dot_general(
                q, kv_ref[:, :HEAD_DIMENSION], nt, preferred_element_type=jnp.float32
            )
            slot = lax.broadcasted_iota(jnp.int32, s1.shape, 1)
            s1 = jnp.where(slot < prefix_len_ref[0, r], s1 * scale, neg_large)
            token = j * TILE + lax.rem(lax.broadcasted_iota(jnp.int32, s2.shape, 0), TILE)
            key = lax.broadcasted_iota(jnp.int32, s2.shape, 1)
            s2 = jnp.where((key >= start) & (key <= token), s2 * scale, neg_large)
            top = jnp.maximum(
                jnp.max(s1, axis=1, keepdims=True), jnp.max(s2, axis=1, keepdims=True)
            )
            p1 = jnp.exp(s1 - top)
            p2 = jnp.exp(s2 - top)
            total = jnp.sum(p1, axis=1, keepdims=True) + jnp.sum(p2, axis=1, keepdims=True)
            inverse = 1.0 / total
            o = jnp.dot(
                (p1 * inverse).astype(jnp.bfloat16),
                prefix_ref[rows, HEAD_DIMENSION:],
                preferred_element_type=jnp.float32,
            ) + jnp.dot(
                (p2 * inverse).astype(jnp.bfloat16),
                kv_ref[:, HEAD_DIMENSION:],
                preferred_element_type=jnp.float32,
            )
            own = j * TILE + lax.rem(lax.broadcasted_iota(jnp.int32, o.shape, 0), TILE)
            mine = (own >= start) & (own < end)
            o_s[j] = jnp.where(mine, o, o_s[j])

        return 0

    lax.fori_loop(0, tiles * requests, body, 0)
    per_tile = TILE // ROWS
    for p in range(8):
        at = order_ref[p]
        tile, part = at // per_tile, at % per_tile
        for h in range(heads):
            x_ref[p * ROWS : (p + 1) * ROWS, h * HEAD_DIMENSION : (h + 1) * HEAD_DIMENSION] = o_s[
                tile, pl.ds(pl.multiple_of(h * TILE + part * ROWS, ROWS), ROWS), :
            ].astype(jnp.bfloat16)
    for c in range(w_s.shape[0]):
        weights(c).wait()
        y_s[c] = jnp.dot(x_ref[...], w_s[c], preferred_element_type=jnp.float32).astype(
            jnp.bfloat16
        )
        for p in range(8):
            written(c, p).start()
    for c in range(w_s.shape[0]):
        for p in range(8):
            written(c, p).wait()


def attend(order, new_len, prefix_len, q, kv, prefix, w):
    tokens, width = q.shape
    heads = width // HEAD_DIMENSION
    columns = w.shape[1]
    chunk = 2048
    work = 2 * tokens * heads * (MAXB * PAGE_TOKENS + tokens) * HEAD_DIMENSION * 2 * 2
    return pl.pallas_call(
        attention_kernel,
        out_shape=[pltpu.HBM((ROWS, columns), jnp.bfloat16)] * 8,
        in_specs=[SMEM, SMEM, SMEM, VMEM, VMEM, ANY, ANY],
        out_specs=[ANY] * 8,
        scratch_shapes=[
            pltpu.VMEM(prefix.shape, prefix.dtype),
            pltpu.VMEM((tokens, width), jnp.bfloat16),
            pltpu.VMEM((tokens // TILE, heads * TILE, HEAD_DIMENSION), jnp.bfloat16),
            pltpu.VMEM((tokens // TILE, heads * TILE, HEAD_DIMENSION), jnp.float32),
            pltpu.VMEM((columns // chunk, width, chunk), jnp.bfloat16),
            pltpu.VMEM((columns // chunk, tokens, chunk), jnp.bfloat16),
            pltpu.SemaphoreType.DMA((columns // chunk,)),
            pltpu.SemaphoreType.DMA((columns // chunk, 8)),
            pltpu.SemaphoreType.DMA,
        ],
        compiler_params=pltpu.CompilerParams(vmem_limit_bytes=28 * MIB),
        cost_estimate=pl.CostEstimate(
            flops=0, bytes_accessed=0, transcendentals=0
        ),
        name="attention",
    )(order, new_len, prefix_len, q, kv, in_hbm(prefix), in_hbm(w))


def merge_kernel(early_ref, late_ref, out_ref):
    out_ref[:, :EARLY] = early_ref[...]
    out_ref[:, EARLY:] = late_ref[...]


def merged(early, late):
    devices = early.shape[0]
    page = early.shape[2:]

    def spec(slots):
        return pl.BlockSpec((devices // 8, slots) + page, lambda i: (i, 0, 0, 0))

    return pl.pallas_call(
        merge_kernel,
        grid=(8,),
        in_specs=[spec(EARLY), spec(CAP - EARLY)],
        out_specs=spec(CAP),
        out_shape=jax.ShapeDtypeStruct((devices, CAP) + page, early.dtype),
        compiler_params=pltpu.CompilerParams(vmem_limit_bytes=16 * MIB),
        cost_estimate=pl.CostEstimate(flops=0, bytes_accessed=6 * MIB, transcendentals=0),
        name="keep",
    )(early, late)


def rotary_tables(angles):
    cosine, sine = jnp.cos(angles), jnp.sin(angles)
    return (
        jnp.concatenate([cosine, cosine], axis=1),
        jnp.concatenate([-sine, sine], axis=1),
    )


def page_tags(groups, me, requests):
    rows = requests * NB
    owners = groups[:, :rows]
    prefix, new_tokens, full_length = (
        groups[:, rows + i * requests : rows + (i + 1) * requests] for i in range(3)
    )
    block = jnp.arange(NB, dtype=jnp.int32)
    pages = jnp.where(
        full_length == prefix + new_tokens, (prefix + new_tokens) // PAGE_TOKENS, 0
    )
    sent = (block < pages[:, :, None]).reshape(-1, rows)
    number = jnp.where((owners == me) & sent, jnp.arange(1, rows + 1, dtype=jnp.int32), rows + 1)
    tags = []
    last = jnp.zeros((groups.shape[0], 1), jnp.int32)
    for _ in range(CAP):
        last = jnp.min(jnp.where(number > last, number, rows + 1), axis=1, keepdims=True)
        tags.append(jnp.where(last <= rows, last, 0))
    return jnp.concatenate(tags, axis=1)


def on_device(
    hidden_in,
    attn_gain,
    q_weight,
    key_weight_matrix,
    value_weight_matrix,
    o_weight,
    kv_pool,
    block_table,
    request_len,
    prefix_len,
    new_len,
    page_owner,
):
    n_section, n_tp, n_dec = (lax.axis_size(a) for a in ("section", "tp", "dec"))
    devices = n_section * n_tp * n_dec
    x = hidden_in[0]
    tokens = ROWS * n_tp
    normed = normalize(x, attn_gain)

    far = send(normed, 2, 0)
    near_z = send(normed, 0, 1)
    right = send(normed, 3, 0)
    left = send(normed, 1, 0)

    tp = lax.axis_index("tp")
    px, pz = tp // 2, tp % 2
    order = jnp.stack([((px + dx) % (n_tp // 2)) * 2 + (pz ^ dz) for dx, dz in PIECES]).astype(
        jnp.int32
    )

    prefix, new_tokens, full_length = prefix_len[0], new_len[0], request_len[0]
    owners = page_owner[0, :, 0]
    plain = jnp.concatenate([owners, prefix, new_tokens, full_length])
    near_z, owner_row = lax.optimization_barrier((near_z, owners[None, :]))
    right_z = send(near_z, 3, 0)
    left_z = send(near_z, 1, 0)
    plain, normed = lax.optimization_barrier((plain, normed))
    groups = lax.all_to_all(
        jnp.broadcast_to(plain, (n_section * n_dec,) + plain.shape),
        ("section", "dec"),
        split_axis=0,
        concat_axis=0,
        tiled=True,
    )
    groups, far = lax.optimization_barrier((groups, far))
    far_z = send(far, 0, 1)
    gathered = (normed, near_z, right, left, right_z, left_z, far, far_z)

    pool = kv_pool[0, :, :, 0, :]
    angles, early, late, prefix_pages, place, wq, wkv = prepare(
        devices,
        tokens,
        prefix_len,
        new_len,
        request_len,
        block_table[0],
        owner_row,
        pool,
        q_weight[0],
        key_weight_matrix[0],
        value_weight_matrix[0],
    )
    cos, sin = rotary_tables(angles)
    q, kv, early, late = project(order, place, gathered, wq, wkv, cos, sin, early, late)

    def deliver(pages):
        return lax.all_to_all(
            pages.reshape(devices, -1, PAGE_TOKENS, 2 * HEAD_DIMENSION),
            ("section", "tp", "dec"),
            split_axis=0,
            concat_axis=0,
            tiled=True,
        )

    early = deliver(early)
    parts = dict(
        zip(
            PIECES,
            attend(
                order,
                new_len,
                prefix_len,
                q,
                kv,
                prefix_pages.reshape(-1, 2 * HEAD_DIMENSION),
                o_weight[0],
            ),
        )
    )

    far_pair = send(parts[2, 1], 0, 1)
    from_left_z = send(parts[1, 1], 1, 0)
    from_right_z = send(parts[3, 1], 3, 0)

    early, far_pair, from_left_z, from_right_z = lax.optimization_barrier(
        (early, far_pair, from_left_z, from_right_z)
    )

    def total(*terms):
        return sum(t.astype(jnp.float32) for t in terms)

    from_left = send(parts[1, 0], 1, 0)
    from_right = send(parts[3, 0], 3, 0)
    from_far = send(total(parts[2, 0], far_pair).astype(jnp.bfloat16), 2, 0)
    from_z = send_on(total(parts[0, 1], from_left_z, from_right_z).astype(jnp.bfloat16), 0, 1)
    own = send_on(
        total(x, parts[0, 0], from_left, from_right, from_far).astype(jnp.bfloat16), 0, 0
    )
    kept = merged(early, deliver(late))
    passed = total(own, from_z).astype(jnp.bfloat16)[None]

    me = (lax.axis_index("section") * n_tp + tp) * n_dec + lax.axis_index("dec")
    received_tags = jnp.broadcast_to(
        page_tags(groups, me, prefix.shape[0]).reshape(n_section, 1, n_dec, CAP),
        (n_section, n_tp, n_dec, CAP),
    ).reshape(1, devices, CAP)
    return passed, kept[None, :, :, :, None, :], received_tags


def solution(mesh):
    in_specs = (
        P("section", ("dec", "tp"), None),
        P("section", None),
        P("section", None, "tp"),
        P("section", None, "tp"),
        P("section", None, "tp"),
        P("section", "tp", None),
        P("section", "dec", None, "tp", None),
        P("section", "dec", None),
        P("section", "dec"),
        P("section", "dec"),
        P("section", "dec"),
        P("section", "dec", None),
    )
    out_specs = (
        P("section", ("dec", "tp"), None),
        P(("section", "tp", "dec"), None, None, None, None, None),
        P(("section", "tp", "dec"), None, None),
    )
    return jax.shard_map(
        on_device, mesh=mesh, in_specs=in_specs, out_specs=out_specs, check_vma=False
    )
```

time: 166 us -> 149 us (0.90)
  local copies, waits for them, and re-layouts: 18.5 us -> 2.97 us
  waiting for transfers between devices: 67.2 us -> 58.6 us
  starting transfers between devices: 41.5 us -> 47.2 us
  Pallas kernels: 25.5 us -> 28.8 us
  other arithmetic: 12 us -> 9.65 us
    ppermute x14 -> x13, waiting for transfers between devices: 54.8 us -> 34.5 us  [send(): return lax.ppermute(block, 'tp', tp_route(dx, dz, lax.axis_size('tp')))]
    unnamed x29 -> x13, local copies, waits for them, and re-layouts: 15.8 us -> 0.63 us
    all_to_all x2 -> x3, waiting for transfers between devices: 0.01 us -> 14.4 us  [the longest x2 10.1 us: deliver(): lax.all_to_all(pages.reshape(devices, -1, PAGE_TOKENS, 2 * HEAD_DIMENSION...]
    all_to_all x2 -> x3, starting transfers between devices: 17.2 us -> 22.1 us  [the longest x2 14.5 us: deliver(): lax.all_to_all(pages.reshape(devices, -1, PAGE_TOKENS, 2 * HEAD_DIMENSION...]
    ppermute x1 -> x2, waiting for transfers between devices: 12.4 us -> 9.61 us  [send_on(): return lax.ppermute(block, ('section', 'tp'), pairs)]
    pallas_call x5 -> x4, Pallas kernels: 25.2 us -> 27.4 us  [the longest x1 11.8 us: attend(): pl.pallas_call(attention_kernel, out_shape=[pltpu.HBM((ROWS, columns), jn...]
    ppermute x1 -> x2, starting transfers between devices: 1.54 us -> 3.25 us  [send_on(): return lax.ppermute(block, ('section', 'tp'), pairs)]
    ppermute x14 -> x13, starting transfers between devices: 22.8 us -> 21.9 us  [send(): return lax.ppermute(block, 'tp', tp_route(dx, dz, lax.axis_size('tp')))]
  transfers between devices with their start and end apart: 17 -> 18, of which waited for: 5 -> 9; matrix products, arithmetic and copies ran while one was open for 9% -> 7% of each run, Pallas kernels for 3% -> 15%
where the time goes in v2:
time: 149 us; the launch traced here: 148 us
  waiting for transfers between devices  58.6 us (39%)
  starting transfers between devices  47.2 us (32%)
  Pallas kernels  28.8 us (19%)
  other arithmetic  9.65 us (6%)
  local copies, waits for them, and re-layouts  2.97 us (2%)
    ppermute x13, waiting for transfers between devices, send(): return lax.ppermute(block, 'tp', tp_route(dx, dz, lax.axis_size('tp')))  34.5 us
    ppermute x13, starting transfers between devices, send(): return lax.ppermute(block, 'tp', tp_route(dx, dz, lax.axis_size('tp')))  21.9 us
    all_to_all x2, starting transfers between devices, deliver(): lax.all_to_all(pages.reshape(devices, -1, PAGE_TOKENS, 2 * HEAD_DIMENSION...  14.5 us
    pallas_call x1, Pallas kernels, attend(): pl.pallas_call(attention_kernel, out_shape=[pltpu.HBM((ROWS, columns), jn...  11.8 us
    all_to_all x2, waiting for transfers between devices, deliver(): lax.all_to_all(pages.reshape(devices, -1, PAGE_TOKENS, 2 * HEAD_DIMENSION...  10.1 us
    ppermute x2, waiting for transfers between devices, send_on(): return lax.ppermute(block, ('section', 'tp'), pairs)  9.61 us
    all_to_all x1, starting transfers between devices, on_device(): lax.all_to_all(jnp.broadcast_to(plain, (n_section * n_dec,) + plain.shape...  7.59 us
    pallas_call x1, Pallas kernels, prepare(): pl.pallas_call(functools.partial(prepare_kernel, devices), out_shape=[jax...  6.85 us
  transfers between devices with their start and end apart: 18, of which 9 were waited for; matrix products, arithmetic and copies ran while one was open for 7% of the time, Pallas kernels for 15%

profile of v2, /device:TPU:0, one launch (start us, length us, event | category | flops | bytes accessed | tf_op | source)
XLA Modules:
  0.0 148.1 jit_solution(16729830110023018490)
XLA Ops:
  0.6 1.4 norm.1.refs_0_
  2.0 3.2 %collective-permute-start.5 = (bf16[32,8192]{1,0:T(8,128)(2,1)S(1)}, bf16[32,8192]{1,0:T(8,128)(2,1)S(1)}, u32[]{:S(2)}, u32[]{:S(2)}) collective-permute-start(bf16[32,8192]{1,0:T(8,128)(2,1)S(1)} %norm.1.refs_0_), channel_id=1, source_target_pairs={{0,16},{4,20},{8,24},{12,28},{16,0},{20,4},{24,8},{28,12},{1,17},{... | collective-permute-start | bytes 1572872 | tf_op jit(solution)/shard_map/ppermute | solution.py:37
  5.2 1.9 %collective-permute-start = (bf16[32,8192]{1,0:T(8,128)(2,1)S(1)}, bf16[32,8192]{1,0:T(8,128)(2,1)S(1)}, u32[]{:S(2)}, u32[]{:S(2)}) collective-permute-start(bf16[32,8192]{1,0:T(8,128)(2,1)S(1)} %norm.1.refs_0_), channel_id=1, source_target_pairs={{0,4},{4,0},{8,12},{12,8},{16,20},{20,16},{24,28},{28,24},{1,5},{5... | collective-permute-start | bytes 1572872 | tf_op jit(solution)/shard_map/ppermute | solution.py:37
  7.1 0.8 pad_add_fusion
  7.9 0.6 broadcast_in_dim.42
  8.6 7.6 %all-to-all-start = ((s32[16,1,236]{2,1,0:T(1,128)}), s32[16,1,236]{2,1,0:T(1,128)S(1)}, u32[]{:S(2)}, u32[]{:S(2)}) async-start(s32[16,1,236]{2,1,0:T(1,128)} %broadcast_in_dim.42), calls=%async_computation | async-start | bytes 32768 | tf_op jit(solution)/shard_map/all_to_all | solution.py:584
  16.2 0.7 collective-permute-start.2
  16.8 2.6 %collective-permute-start.1 = (bf16[32,8192]{1,0:T(8,128)(2,1)S(1)}, bf16[32,8192]{1,0:T(8,128)(2,1)S(1)}, u32[]{:S(2)}, u32[]{:S(2)}) collective-permute-start(bf16[32,8192]{1,0:T(8,128)(2,1)S(1)} %norm.1.refs_0_), channel_id=1, source_target_pairs={{0,24},{4,28},{8,0},{12,4},{16,8},{20,12},{24,16},{28,20},{1,25},{... | collective-permute-start | bytes 1572872 | tf_op jit(solution)/shard_map/ppermute | solution.py:37
  19.5 4.3 %all-to-all-done = s32[16,1,236]{2,1,0:T(1,128)S(1)} async-done(((s32[16,1,236]{2,1,0:T(1,128)}), s32[16,1,236]{2,1,0:T(1,128)S(1)}, u32[]{:S(2)}, u32[]{:S(2)}) %all-to-all-start) | async-done | bytes 15136 | tf_op jit(solution)/shard_map/all_to_all | solution.py:584
  23.7 0.6 copy.26
  24.4 0.7 collective-permute-start.4
  25.0 2.6 %collective-permute-start.3 = (bf16[32,8192]{1,0:T(8,128)(2,1)S(1)}, bf16[32,8192]{1,0:T(8,128)(2,1)}, u32[]{:S(2)}, u32[]{:S(2)}) collective-permute-start(bf16[32,8192]{1,0:T(8,128)(2,1)S(1)} %collective-permute-done.refs_1_), channel_id=1, source_target_pairs={{0,24},{4,28},{8,0},{12,4},{16,8},{20,12},{24,16},{28,20},{1,25},{... | collective-permute-start | bytes 1572872 | tf_op jit(solution)/shard_map/ppermute | solution.py:37
  27.7 0.1 stack.35.order.order_ref
  27.8 6.8 %prepare.1 = (f32[256,64]{1,0:T(8,128)S(1)}, bf16[256,16,256]{2,1,0:T(8,128)(2,1)}, bf16[128,16,256]{2,1,0:T(8,128)(2,1)}, bf16[160,16,256]{2,1,0:T(8,128)(2,1)S...) custom-call(s32[1,4]{1,0:T(1,128)} %prefix_len_ref.1, ...), custom_call_target="tpu_custom_call" | custom-call | bytes 20971520 | tf_op jit(solution)/shard_map/prepare/pallas_call | solution.py:320
  34.6 0.5 fusion.9
  35.1 0.1 pad_maximum_fusion
  35.3 3.0 %collective-permute-done.6.refs_7_ = bf16[32,8192]{1,0:T(8,128)(2,1)S(1)} collective-permute-done((bf16[32,8192]{1,0:T(8,128)(2,1)S(1)}, bf16[32,8192]{1,0:T(8,128)(2,1)S(1)}, u32[]{:S(2)}, u32[]{:S(2)}) %collective-permute-start.6) | collective-permute-done | bytes 524320 | tf_op jit(solution)/shard_map/ppermute | solution.py:37
  38.3 4.6 %collective-permute-done.4.refs_5_ = bf16[32,8192]{1,0:T(8,128)(2,1)} collective-permute-done((bf16[32,8192]{1,0:T(8,128)(2,1)S(1)}, bf16[32,8192]{1,0:T(8,128)(2,1)}, u32[]{:S(2)}, u32[]{:S(2)}) %collective-permute-start.4) | collective-permute-done | bytes 524320 | tf_op jit(solution)/shard_map/ppermute | solution.py:37
  42.9 5.5 %qkv.1 = (bf16[256,512]{1,0:T(8,128)(2,1)S(1)}, bf16[256,256]{1,0:T(8,128)(2,1)S(1)}, bf16[256,16,256]{2,1,0:T(8,128)(2,1)}, bf16[128,16,256]{2,1,0:T(8,128)(2,1)}) custom-call(s32[8]{0:T(128)S(1)} %stack.35.order.order_ref, s32[1,128]{1,0:T(1,128)S(1)} %get-tuple-element.33.place, ...), custom_call_target="tpu_custom_call", output_to_operand_aliasing={{2}: (14, {}), {3}: (15, {})} | custom-call | flops 3221225472 | bytes 16777216 | tf_op jit(solution)/shard_map/qkv/pallas_call | solution.py:160
  48.5 9.9 %all-to-all-start.1 = ((bf16[128,2,16,256]{3,2,1,0:T(8,128)(2,1)}), bf16[128,2,16,256]{3,2,1,0:T(8,128)(2,1)S(1)}, u32[]{:S(2)}, u32[]{:S(2)}) async-start(bf16[128,2,16,256]{3,2,1,0:T(8,128)(2,1)} %bitcast.42), calls=%async_computation.1 | async-start | bytes 4194304 | tf_op jit(solution)/shard_map/all_to_all | solution.py:613
  58.4 0.1 lt.56
  58.5 11.8 %attention.1 = (bf16[32,8192]{1,0:T(8,128)(2,1)}, bf16[32,8192]{1,0:T(8,128)(2,1)}, bf16[32,8192]{1,0:T(8,128)(2,1)}, bf16[32,8192]{1,0:T(8,128)(2,1)}, bf16[32,...) custom-call(s32[8]{0:T(128)S(1)} %stack.35.order.order_ref, ...), custom_call_target="tpu_custom_call" | custom-call | tf_op jit(solution)/shard_map/attention/pallas_call | solution.py:470
  70.4 1.2 collective-permute-start.9
  71.5 1.5 collective-permute-start.10
  73.0 1.8 %collective-permute-start.11 = (bf16[32,8192]{1,0:T(8,128)(2,1)}, bf16[32,8192]{1,0:T(8,128)(2,1)}, u32[]{:S(2)}, u32[]{:S(2)}) collective-permute-start(bf16[32,8192]{1,0:T(8,128)(2,1)} %get-tuple-element.53), channel_id=1, source_target_pairs={{0,24},{4,28},{8,0},{12,4},{16,8},{20,12},{24,16},{28,20},{1,25},{... | collective-permute-start | bytes 1572872 | tf_op jit(solution)/shard_map/ppermute | solution.py:37
  74.9 0.1 lt.59
  75.0 0.1 fusion.1
  75.2 0.2 fusion.2
  75.4 0.1 reduce_min.36
  75.5 0.2 fusion.3
  75.8 0.3 collective-permute-start.7
  76.0 3.0 %collective-permute-start.8 = (bf16[32,8192]{1,0:T(8,128)(2,1)}, bf16[32,8192]{1,0:T(8,128)(2,1)}, u32[]{:S(2)}, u32[]{:S(2)}) collective-permute-start(bf16[32,8192]{1,0:T(8,128)(2,1)} %get-tuple-element.48), channel_id=1, source_target_pairs={{0,24},{4,28},{8,0},{12,4},{16,8},{20,12},{24,16},{28,20},{1,25},{... | collective-permute-start | bytes 1572872 | tf_op jit(solution)/shard_map/ppermute | solution.py:37
  79.0 10.1 %all-to-all-done.1.early_ref = bf16[128,2,16,256]{3,2,1,0:T(8,128)(2,1)S(1)} async-done(((bf16[128,2,16,256]{3,2,1,0:T(8,128)(2,1)}), bf16[128,2,16,256]{3,2,1,0:T(8,128)(2,1)S(1)}, u32[]{:S(2)}, u32[]{:S(2)}) %all-to-all-start.1) | async-done | bytes 2097184 | tf_op jit(solution)/shard_map/all_to_all | solution.py:613
  89.2 4.6 %all-to-all-start.2 = ((bf16[128,1,16,256]{3,2,1,0:T(8,128)(2,1)}), bf16[128,1,16,256]{3,2,1,0:T(8,128)(2,1)S(1)}, u32[]{:S(2)}, u32[]{:S(2)}) async-start(bf16[128,1,16,256]{3,2,1,0:T(8,128)(2,1)} %bitcast.44), calls=%async_computation.2 | async-start | bytes 2097152 | tf_op jit(solution)/shard_map/all_to_all | solution.py:613
  93.8 1.1 collective-permute-done.9
  94.9 0.2 collective-permute-done.10
  95.1 1.3 add_convert_fusion.3
  96.4 2.5 %collective-permute-start.12 = (bf16[32,8192]{1,0:T(8,128)(2,1)S(1)}, bf16[32,8192]{1,0:T(8,128)(2,1)S(1)}, u32[]{:S(2)}, u32[]{:S(2)}) collective-permute-start(bf16[32,8192]{1,0:T(8,128)(2,1)S(1)} %add_convert_fusion.3), channel_id=1, source_target_pairs={{0,16},{4,20},{8,24},{12,28},{16,0},{20,4},{24,8},{28,12},{1,17},{... | collective-permute-start | bytes 1572872 | tf_op jit(solution)/shard_map/ppermute | solution.py:37
  98.9 2.3 %add_convert_fusion.1 = bf16[32,8192]{1,0:T(8,128)(2,1)} fusion(bf16[32,8192]{1,0:T(8,128)(2,1)} %collective-permute-done.11, bf16[32,8192]{1,0:T(8,128)(2,1)} %collective-permute-done.10, bf16[32,8192]{1,0:T(8,128)(2,1)} %get-tuple-element.55), kind=kLoop, calls=%fused_computation.1 | loop fusion | flops 1572864 | bytes 2097152 | tf_op jit(solution)/shard_map/convert_element_type | solution.py:651
  101.2 1.8 %collective-permute-start.14 = (bf16[32,8192]{1,0:T(8,128)(2,1)}, bf16[32,8192]{1,0:T(8,128)(2,1)}, u32[]{:S(2)}, u32[]{:S(2)}) collective-permute-start(bf16[32,8192]{1,0:T(8,128)(2,1)} %add_convert_fusion.1), channel_id=1, source_target_pairs={{0,36},{4,32},{8,44},{12,40},{16,52},{20,48},{24,60},{28,56},{32,6... | collective-permute-start | bytes 1572872 | tf_op jit(solution)/shard_map/ppermute | solution.py:52
  103.0 3.5 %collective-permute-done.7 = bf16[32,8192]{1,0:T(8,128)(2,1)} collective-permute-done((bf16[32,8192]{1,0:T(8,128)(2,1)}, bf16[32,8192]{1,0:T(8,128)(2,1)}, u32[]{:S(2)}, u32[]{:S(2)}) %collective-permute-start.7) | collective-permute-done | bytes 524320 | tf_op jit(solution)/shard_map/ppermute | solution.py:37
  106.5 22.2 %collective-permute-done.12 = bf16[32,8192]{1,0:T(8,128)(2,1)S(1)} collective-permute-done((bf16[32,8192]{1,0:T(8,128)(2,1)S(1)}, bf16[32,8192]{1,0:T(8,128)(2,1)S(1)}, u32[]{:S(2)}, u32[]{:S(2)}) %collective-permute-start.12) | collective-permute-done | bytes 524320 | tf_op jit(solution)/shard_map/ppermute | solution.py:37
  128.6 2.3 %add_convert_fusion.2 = bf16[32,8192]{1,0:T(8,128)(2,1)} fusion(bf16[32,8192]{1,0:T(8,128)(2,1)S(1)} %collective-permute-done.12, bf16[32,8192]{1,0:T(8,128)(2,1)} %collective-permute-done.8, bf16[32,8192]{1,0:T(8,128)(2,1)} %collective-permute-done.7, bf16[32,8192]{1,0:T(8,128)(2,1)S(1)} %copy-done.4, bf16[1,32,8192]{2,1,0:T(8,128)(2,1)S(1)} %copy-done.3), kind=kLoop, calls=%fused_computation.2 | loop fusion | flops 2621440 | bytes 3145728 | tf_op jit(solution)/shard_map/convert_element_type | solution.py:653
  131.0 1.5 collective-permute-start.13
  132.5 0.7 reshape.118
  133.1 3.2 %keep.1 = bf16[128,3,16,256]{3,2,1,0:T(8,128)(2,1)} custom-call(bf16[128,2,16,256]{3,2,1,0:T(8,128)(2,1)S(1)} %all-to-all-done.1.early_ref, bf16[128,1,16,256]{3,2,1,0:T(8,128)(2,1)S(1)} %all-to-all-done.2.late_ref), custom_call_target="tpu_custom_call" | custom-call | bytes 6291456 | tf_op jit(solution)/shard_map/keep/pallas_call | solution.py:506
  136.3 9.6 %collective-permute-done.13 = bf16[32,8192]{1,0:T(8,128)(2,1)} collective-permute-done((bf16[32,8192]{1,0:T(8,128)(2,1)}, bf16[32,8192]{1,0:T(8,128)(2,1)}, u32[]{:S(2)}, u32[]{:S(2)}) %collective-permute-start.13) | collective-permute-done | bytes 524320 | tf_op jit(solution)/shard_map/ppermute | solution.py:52
  146.0 2.1 %fusion = bf16[1,32,8192]{2,1,0:T(8,128)(2,1)} fusion(bf16[32,8192]{1,0:T(8,128)(2,1)} %collective-permute-done.14, bf16[32,8192]{1,0:T(8,128)(2,1)} %collective-permute-done.13), kind=kLoop, calls=%fused_computation.4 | loop fusion | flops 1048576 | bytes 1572864 | tf_op jit(solution)/shard_map/broadcast_in_dim | solution.py:656
  (34 shorter events, 0.4 us)
Async XLA Ops:
  2.0 22.3 %collective-permute-start.5 = (bf16[32,8192]{1,0:T(8,128)(2,1)S(1)}, bf16[32,8192]{1,0:T(8,128)(2,1)S(1)}, u32[]{:S(2)}, u32[]{:S(2)}) collective-permute-start(bf16[32,8192]{1,0:T(8,128)(2,1)S(1)} %norm.1.refs_0_), channel_id=1, source_target_pairs={{0,16},{4,20},{8,24},{12,28},{16,0},{20,4},{24,8},{28,12},{1,17},{... | collective-permute-start | bytes 1572872 | tf_op jit(solution)/shard_map/ppermute | solution.py:37
  5.2 19.1 %collective-permute-start = (bf16[32,8192]{1,0:T(8,128)(2,1)S(1)}, bf16[32,8192]{1,0:T(8,128)(2,1)S(1)}, u32[]{:S(2)}, u32[]{:S(2)}) collective-permute-start(bf16[32,8192]{1,0:T(8,128)(2,1)S(1)} %norm.1.refs_0_), channel_id=1, source_target_pairs={{0,4},{4,0},{8,12},{12,8},{16,20},{20,16},{24,28},{28,24},{1,5},{5... | collective-permute-start | bytes 1572872 | tf_op jit(solution)/shard_map/ppermute | solution.py:37
  8.6 15.2 %all-to-all-start = ((s32[16,1,236]{2,1,0:T(1,128)}), s32[16,1,236]{2,1,0:T(1,128)S(1)}, u32[]{:S(2)}, u32[]{:S(2)}) async-start(s32[16,1,236]{2,1,0:T(1,128)} %broadcast_in_dim.42), calls=%async_computation | async-start | bytes 32768 | tf_op jit(solution)/shard_map/all_to_all | solution.py:584
  16.2 19.1 %collective-permute-start.2 = (bf16[32,8192]{1,0:T(8,128)(2,1)S(1)}, bf16[32,8192]{1,0:T(8,128)(2,1)S(1)}, u32[]{:S(2)}, u32[]{:S(2)}) collective-permute-start(bf16[32,8192]{1,0:T(8,128)(2,1)S(1)} %norm.1.refs_0_), channel_id=1, source_target_pairs={{0,8},{4,12},{8,16},{12,20},{16,24},{20,28},{24,0},{28,4},{1,9},{5... | collective-permute-start | bytes 1572872 | tf_op jit(solution)/shard_map/ppermute | solution.py:37
  16.8 18.5 %collective-permute-start.1 = (bf16[32,8192]{1,0:T(8,128)(2,1)S(1)}, bf16[32,8192]{1,0:T(8,128)(2,1)S(1)}, u32[]{:S(2)}, u32[]{:S(2)}) collective-permute-start(bf16[32,8192]{1,0:T(8,128)(2,1)S(1)} %norm.1.refs_0_), channel_id=1, source_target_pairs={{0,24},{4,28},{8,0},{12,4},{16,8},{20,12},{24,16},{28,20},{1,25},{... | collective-permute-start | bytes 1572872 | tf_op jit(solution)/shard_map/ppermute | solution.py:37
  24.3 13.9 %collective-permute-start.6 = (bf16[32,8192]{1,0:T(8,128)(2,1)S(1)}, bf16[32,8192]{1,0:T(8,128)(2,1)S(1)}, u32[]{:S(2)}, u32[]{:S(2)}) collective-permute-start(bf16[32,8192]{1,0:T(8,128)(2,1)S(1)} %collective-permute-done.5.refs_6_), channel_id=1, source_target_pairs={{0,4},{4,0},{8,12},{12,8},{16,20},{20,16},{24,28},{28,24},{1,5},{5... | collective-permute-start | bytes 1572872 | tf_op jit(solution)/shard_map/ppermute | solution.py:37
  24.4 18.6 %collective-permute-start.4 = (bf16[32,8192]{1,0:T(8,128)(2,1)S(1)}, bf16[32,8192]{1,0:T(8,128)(2,1)}, u32[]{:S(2)}, u32[]{:S(2)}) collective-permute-start(bf16[32,8192]{1,0:T(8,128)(2,1)S(1)} %collective-permute-done.refs_1_), channel_id=1, source_target_pairs={{0,8},{4,12},{8,16},{12,20},{16,24},{20,28},{24,0},{28,4},{1,9},{5... | collective-permute-start | bytes 1572872 | tf_op jit(solution)/shard_map/ppermute | solution.py:37
  25.0 17.9 %collective-permute-start.3 = (bf16[32,8192]{1,0:T(8,128)(2,1)S(1)}, bf16[32,8192]{1,0:T(8,128)(2,1)}, u32[]{:S(2)}, u32[]{:S(2)}) collective-permute-start(bf16[32,8192]{1,0:T(8,128)(2,1)S(1)} %collective-permute-done.refs_1_), channel_id=1, source_target_pairs={{0,24},{4,28},{8,0},{12,4},{16,8},{20,12},{24,16},{28,20},{1,25},{... | collective-permute-start | bytes 1572872 | tf_op jit(solution)/shard_map/ppermute | solution.py:37
  34.6 13.9 %copy-start = (bf16[160,16,256]{2,1,0:T(8,128)(2,1)}, bf16[160,16,256]{2,1,0:T(8,128)(2,1)S(1)}, u32[]{:S(2)}) copy-start(bf16[160,16,256]{2,1,0:T(8,128)(2,1)S(1)} %get-tuple-element.45) | copy-start | bytes 3932164
  48.5 10.0 %copy-start.1 = (s32[1,4]{1,0:T(1,128)S(1)}, s32[1,4]{1,0:T(1,128)}, u32[]{:S(2)}) copy-start(s32[1,4]{1,0:T(1,128)} %new_len_ref.1) | copy-start | bytes 52
  48.5 10.0 %copy-start.2 = (s32[1,4]{1,0:T(1,128)S(1)}, s32[1,4]{1,0:T(1,128)}, u32[]{:S(2)}) copy-start(s32[1,4]{1,0:T(1,128)} %prefix_len_ref.1) | copy-start | bytes 52
  48.5 40.6 %all-to-all-start.1 = ((bf16[128,2,16,256]{3,2,1,0:T(8,128)(2,1)}), bf16[128,2,16,256]{3,2,1,0:T(8,128)(2,1)S(1)}, u32[]{:S(2)}, u32[]{:S(2)}) async-start(bf16[128,2,16,256]{3,2,1,0:T(8,128)(2,1)} %bitcast.42), calls=%async_computation.1 | async-start | bytes 4194304 | tf_op jit(solution)/shard_map/all_to_all | solution.py:613
  58.5 16.2 %copy-start.5 = (s32[16,1,236]{2,0,1:T(8,128)S(1)}, s32[16,1,236]{2,0,1:T(8,128)}, u32[]{:S(2)}) copy-start(s32[16,1,236]{2,0,1:T(8,128)} %copy.26) | copy-start | bytes 45316
  70.4 24.5 %collective-permute-start.9 = (bf16[32,8192]{1,0:T(8,128)(2,1)}, bf16[32,8192]{1,0:T(8,128)(2,1)}, u32[]{:S(2)}, u32[]{:S(2)}) collective-permute-start(bf16[32,8192]{1,0:T(8,128)(2,1)} %get-tuple-element.51), channel_id=1, source_target_pairs={{0,4},{4,0},{8,12},{12,8},{16,20},{20,16},{24,28},{28,24},{1,5},{5... | collective-permute-start | bytes 1572872 | tf_op jit(solution)/shard_map/ppermute | solution.py:37
  71.5 23.5 %collective-permute-start.10 = (bf16[32,8192]{1,0:T(8,128)(2,1)}, bf16[32,8192]{1,0:T(8,128)(2,1)}, u32[]{:S(2)}, u32[]{:S(2)}) collective-permute-start(bf16[32,8192]{1,0:T(8,128)(2,1)} %get-tuple-element.52), channel_id=1, source_target_pairs={{0,8},{4,12},{8,16},{12,20},{16,24},{20,28},{24,0},{28,4},{1,9},{5... | collective-permute-start | bytes 1572872 | tf_op jit(solution)/shard_map/ppermute | solution.py:37
  73.0 22.1 %collective-permute-start.11 = (bf16[32,8192]{1,0:T(8,128)(2,1)}, bf16[32,8192]{1,0:T(8,128)(2,1)}, u32[]{:S(2)}, u32[]{:S(2)}) collective-permute-start(bf16[32,8192]{1,0:T(8,128)(2,1)} %get-tuple-element.53), channel_id=1, source_target_pairs={{0,24},{4,28},{8,0},{12,4},{16,8},{20,12},{24,16},{28,20},{1,25},{... | collective-permute-start | bytes 1572872 | tf_op jit(solution)/shard_map/ppermute | solution.py:37
  75.8 30.7 %collective-permute-start.7 = (bf16[32,8192]{1,0:T(8,128)(2,1)}, bf16[32,8192]{1,0:T(8,128)(2,1)}, u32[]{:S(2)}, u32[]{:S(2)}) collective-permute-start(bf16[32,8192]{1,0:T(8,128)(2,1)} %get-tuple-element.47), channel_id=1, source_target_pairs={{0,8},{4,12},{8,16},{12,20},{16,24},{20,28},{24,0},{28,4},{1,9},{5... | collective-permute-start | bytes 1572872 | tf_op jit(solution)/shard_map/ppermute | solution.py:37
  76.0 30.4 %collective-permute-start.8 = (bf16[32,8192]{1,0:T(8,128)(2,1)}, bf16[32,8192]{1,0:T(8,128)(2,1)}, u32[]{:S(2)}, u32[]{:S(2)}) collective-permute-start(bf16[32,8192]{1,0:T(8,128)(2,1)} %get-tuple-element.48), channel_id=1, source_target_pairs={{0,24},{4,28},{8,0},{12,4},{16,8},{20,12},{24,16},{28,20},{1,25},{... | collective-permute-start | bytes 1572872 | tf_op jit(solution)/shard_map/ppermute | solution.py:37
  89.2 44.0 %all-to-all-start.2 = ((bf16[128,1,16,256]{3,2,1,0:T(8,128)(2,1)}), bf16[128,1,16,256]{3,2,1,0:T(8,128)(2,1)S(1)}, u32[]{:S(2)}, u32[]{:S(2)}) async-start(bf16[128,1,16,256]{3,2,1,0:T(8,128)(2,1)} %bitcast.44), calls=%async_computation.2 | async-start | bytes 2097152 | tf_op jit(solution)/shard_map/all_to_all | solution.py:613
  93.8 34.8 %copy-start.3 = (bf16[1,32,8192]{2,1,0:T(8,128)(2,1)S(1)}, bf16[1,32,8192]{2,1,0:T(8,128)(2,1)}, u32[]{:S(2)}) copy-start(bf16[1,32,8192]{2,1,0:T(8,128)(2,1)} %param.12) | copy-start | bytes 1572868
  93.8 34.8 %copy-start.4 = (bf16[32,8192]{1,0:T(8,128)(2,1)S(1)}, bf16[32,8192]{1,0:T(8,128)(2,1)}, u32[]{:S(2)}) copy-start(bf16[32,8192]{1,0:T(8,128)(2,1)} %get-tuple-element.46) | copy-start | bytes 1572868
  96.4 32.2 %collective-permute-start.12 = (bf16[32,8192]{1,0:T(8,128)(2,1)S(1)}, bf16[32,8192]{1,0:T(8,128)(2,1)S(1)}, u32[]{:S(2)}, u32[]{:S(2)}) collective-permute-start(bf16[32,8192]{1,0:T(8,128)(2,1)S(1)} %add_convert_fusion.3), channel_id=1, source_target_pairs={{0,16},{4,20},{8,24},{12,28},{16,0},{20,4},{24,8},{28,12},{1,17},{... | collective-permute-start | bytes 1572872 | tf_op jit(solution)/shard_map/ppermute | solution.py:37
  101.2 35.1 %collective-permute-start.14 = (bf16[32,8192]{1,0:T(8,128)(2,1)}, bf16[32,8192]{1,0:T(8,128)(2,1)}, u32[]{:S(2)}, u32[]{:S(2)}) collective-permute-start(bf16[32,8192]{1,0:T(8,128)(2,1)} %add_convert_fusion.1), channel_id=1, source_target_pairs={{0,36},{4,32},{8,44},{12,40},{16,52},{20,48},{24,60},{28,56},{32,6... | collective-permute-start | bytes 1572872 | tf_op jit(solution)/shard_map/ppermute | solution.py:52
  131.0 15.0 %collective-permute-start.13 = (bf16[32,8192]{1,0:T(8,128)(2,1)}, bf16[32,8192]{1,0:T(8,128)(2,1)}, u32[]{:S(2)}, u32[]{:S(2)}) collective-permute-start(bf16[32,8192]{1,0:T(8,128)(2,1)} %add_convert_fusion.2), channel_id=1, source_target_pairs={{0,32},{4,36},{8,40},{12,44},{16,48},{20,52},{24,56},{28,60},{32,6... | collective-permute-start | bytes 1572872 | tf_op jit(solution)/shard_map/ppermute | solution.py:52

commit v3 on v2

--- a/solution.py
+++ b/solution.py
@@ -13,7 +13,7 @@
 MAXB = 40
 NB = 56
 CAP = 3
-EARLY = 2
+SOON = 5
 ROWS = 32
 
 theta_base = 500000.0
@@ -25,7 +25,7 @@
 SMEM = pl.BlockSpec(memory_space=pltpu.SMEM)
 ANY = pl.BlockSpec(memory_space=pl.ANY)
 
-PIECES = ((0, 0), (0, 1), (1, 0), (3, 0), (1, 1), (3, 1), (2, 0), (2, 1))
+PIECES = ((0, 0), (0, 1), (1, 0), (3, 0), (2, 0), (1, 1), (3, 1), (2, 1))
 
 
 def tp_route(dx, dz, n_tp):
@@ -40,16 +40,6 @@
 def shifted(block, axis, distance):
     count = lax.axis_size(axis)
     return lax.ppermute(block, axis, [((i - distance) % count, i) for i in range(count)])
-
-
-def send_on(block, dx, dz):
-    n_section, n_tp = lax.axis_size("section"), lax.axis_size("tp")
-    pairs = [
-        (s * n_tp + a, ((s + 1) % n_section) * n_tp + b)
-        for s in range(n_section)
-        for a, b in tp_route(dx, dz, n_tp)
-    ]
-    return lax.ppermute(block, ("section", "tp"), pairs)
 
 
 def norm_kernel(x_ref, gain_ref, out_ref, x_s, gain_s, sems):
@@ -105,82 +95,118 @@
     return v * cos + pltpu.roll(v, HEAD_DIMENSION // 2, 1) * sin
 
 
-def qkv_kernel(order, place, *refs):
-    pieces = refs[:8]
-    wq, wkv, cos_ref, sin_ref = refs[8:12]
-    q_ref, kv_ref, early_ref, late_ref, acc_q, acc_kv, sems = refs[14:]
-    slots = late_ref.shape[0] * CAP
-    count = kv_ref.shape[0] // PAGE_TOKENS
+def write_rows(order, first, count, acc_q, acc_kv, cos_ref, sin_ref, q_ref, kv_ref):
     heads = acc_q.shape[1] // HEAD_DIMENSION
-
-    project_rows(pieces, wkv, acc_kv)
-    for p in range(8):
-        rows = pl.ds(pl.multiple_of(order[p] * ROWS, ROWS), ROWS)
+    for p in range(count):
+        rows = pl.ds(pl.multiple_of(order[first + p] * ROWS, ROWS), ROWS)
         here = slice(p * ROWS, (p + 1) * ROWS)
-        kv_ref[rows, :HEAD_DIMENSION] = rotate(
-            acc_kv[here, :HEAD_DIMENSION], cos_ref[rows, :], sin_ref[rows, :]
-        ).astype(jnp.bfloat16)
+        cos, sin = cos_ref[rows, :], sin_ref[rows, :]
+        kv_ref[rows, :HEAD_DIMENSION] = rotate(acc_kv[here, :HEAD_DIMENSION], cos, sin).astype(
+            jnp.bfloat16
+        )
         kv_ref[rows, HEAD_DIMENSION:] = acc_kv[here, HEAD_DIMENSION:].astype(jnp.bfloat16)
-
-    def each(i, act):
-        at = jnp.minimum(place[0, i], slots - 1)
-        owner, slot = at // CAP, at % CAP
-        page = kv_ref.at[pl.ds(i * PAGE_TOKENS, PAGE_TOKENS), :]
-
-        @pl.when((place[0, i] < slots) & (slot < EARLY))
-        def _():
-            to = early_ref.at[owner * EARLY + jnp.minimum(slot, EARLY - 1)]
-            act(pltpu.make_async_copy(page, to, sems.at[i]))
-
-        @pl.when((place[0, i] < slots) & (slot >= EARLY))
-        def _():
-            act(pltpu.make_async_copy(page, late_ref.at[owner], sems.at[i]))
-
-    for i in range(count):
-        each(i, lambda copy: copy.start())
-
-    project_rows(pieces, wq, acc_q)
-    for p in range(8):
-        rows = pl.ds(pl.multiple_of(order[p] * ROWS, ROWS), ROWS)
-        here = slice(p * ROWS, (p + 1) * ROWS)
         for h in range(heads):
             cols = slice(h * HEAD_DIMENSION, (h + 1) * HEAD_DIMENSION)
-            q_ref[rows, cols] = rotate(
-                acc_q[here, cols], cos_ref[rows, :], sin_ref[rows, :]
-            ).astype(jnp.bfloat16)
-
-    for i in range(count):
-        each(i, lambda copy: copy.wait())
-
-
-def project(order, place, pieces, wq, wkv, cos, sin, early, late):
+            q_ref[rows, cols] = rotate(acc_q[here, cols], cos, sin).astype(jnp.bfloat16)
+
+
+def first_kernel(order, *refs):
+    pieces = refs[:SOON]
+    wq, wkv, cos_ref, sin_ref, q_ref, kv_ref, acc_q, acc_kv = refs[SOON:]
+    project_rows(pieces, wkv, acc_kv)
+    project_rows(pieces, wq, acc_q)
+    q_ref[...] = jnp.zeros_like(q_ref)
+    kv_ref[...] = jnp.zeros_like(kv_ref)
+    write_rows(order, 0, SOON, acc_q, acc_kv, cos_ref, sin_ref, q_ref, kv_ref)
+
+
+def project_first(order, pieces, wq, wkv, cos, sin):
     depth, n_q = wq.shape
     n_kv = wkv.shape[1]
     tokens = 8 * ROWS
+    rows = SOON * ROWS
     return pl.pallas_call(
-        qkv_kernel,
-        in_specs=[SMEM, SMEM] + [VMEM] * 12 + [ANY, ANY],
-        out_specs=[VMEM, VMEM, ANY, ANY],
+        first_kernel,
+        in_specs=[SMEM] + [VMEM] * (SOON + 4),
+        out_specs=[VMEM, VMEM],
         out_shape=[
             jax.ShapeDtypeStruct((tokens, n_q), jnp.bfloat16),
             jax.ShapeDtypeStruct((tokens, n_kv), jnp.bfloat16),
-            pltpu.HBM(early.shape, early.dtype),
-            pltpu.HBM(late.shape, late.dtype),
         ],
         scratch_shapes=[
-            pltpu.VMEM((tokens, n_q), jnp.float32),
-            pltpu.VMEM((tokens, n_kv), jnp.float32),
-            pltpu.SemaphoreType.DMA((tokens // PAGE_TOKENS,)),
-        ],
-        input_output_aliases={14: 2, 15: 3},
+            pltpu.VMEM((rows, n_q), jnp.float32),
+            pltpu.VMEM((rows, n_kv), jnp.float32),
+        ],
         compiler_params=pltpu.CompilerParams(vmem_limit_bytes=12 * MIB),
         cost_estimate=pl.CostEstimate(
-            flops=2 * tokens * depth * (n_q + n_kv),
-            bytes_accessed=2 * depth * (n_q + n_kv + tokens),
+            flops=2 * rows * depth * (n_q + n_kv),
+            bytes_accessed=2 * depth * (n_q + n_kv + rows),
+            transcendentals=0,
+        ),
+        name="qkv_first",
+    )(order, *pieces, in_vmem(wq), in_vmem(wkv), cos, sin)
+
+
+def qkv_kernel(order, place, *refs):
+    pieces = refs[: 8 - SOON]
+    wq, wkv, cos_ref, sin_ref, q_in, kv_in, buffer_ref = refs[8 - SOON : 15 - SOON]
+    q_ref, kv_ref, out_ref, acc_q, acc_kv, sems = refs[15 - SOON :]
+    del buffer_ref
+    slots = out_ref.shape[0]
+    count = kv_ref.shape[0] // PAGE_TOKENS
+    project_rows(pieces, wkv, acc_kv)
+    project_rows(pieces, wq, acc_q)
+    q_ref[...] = q_in[...]
+    kv_ref[...] = kv_in[...]
+    write_rows(order, SOON, 8 - SOON, acc_q, acc_kv, cos_ref, sin_ref, q_ref, kv_ref)
+
+    def copy(i):
+        return pltpu.make_async_copy(
+            kv_ref.at[pl.ds(i * PAGE_TOKENS, PAGE_TOKENS), :],
+            out_ref.at[jnp.minimum(place[0, i], slots - 1)],
+            sems.at[i],
+        )
+
+    for i in range(count):
+        @pl.when(place[0, i] < slots)
+        def _():
+            copy(i).start()
+
+    for i in range(count):
+        @pl.when(place[0, i] < slots)
+        def _():
+            copy(i).wait()
+
+
+def project(order, place, pieces, wq, wkv, cos, sin, buffer):
+    depth, n_q = wq.shape
+    n_kv = wkv.shape[1]
+    tokens = 8 * ROWS
+    rows = (8 - SOON) * ROWS
+    q, kv = project_first(order, pieces[:SOON], wq, wkv, cos, sin)
+    return pl.pallas_call(
+        qkv_kernel,
+        in_specs=[SMEM, SMEM] + [VMEM] * (8 - SOON + 6) + [ANY],
+        out_specs=[VMEM, VMEM, ANY],
+        out_shape=[
+            jax.ShapeDtypeStruct((tokens, n_q), jnp.bfloat16),
+            jax.ShapeDtypeStruct((tokens, n_kv), jnp.bfloat16),
+            pltpu.HBM(buffer.shape, buffer.dtype),
+        ],
+        scratch_shapes=[
+            pltpu.VMEM((rows, n_q), jnp.float32),
+            pltpu.VMEM((rows, n_kv), jnp.float32),
+            pltpu.SemaphoreType.DMA((tokens // PAGE_TOKENS,)),
+        ],
+        input_output_aliases={16 - SOON: 2},
+        compiler_params=pltpu.CompilerParams(vmem_limit_bytes=12 * MIB),
+        cost_estimate=pl.CostEstimate(
+            flops=2 * rows * depth * (n_q + n_kv),
+            bytes_accessed=2 * depth * (n_q + n_kv + rows),
             transcendentals=0,
         ),
         name="qkv",
-    )(order, place, *pieces, in_vmem(wq), in_vmem(wkv), cos, sin, early, late)
+    )(order, place, *pieces[SOON:], in_vmem(wq), in_vmem(wkv), cos, sin, q, kv, buffer)
 
 
 def prepare_kernel(
@@ -196,8 +222,7 @@
     wk_ref,
     wv_ref,
     angles_ref,
-    early_ref,
-    late_ref,
+    buffer_ref,
     prefix_ref,
     place_ref,
     wq_out,
@@ -261,7 +286,7 @@
     rank = jnp.sum(
         jnp.where((across == target) & (lane < row), 1, 0), axis=1, keepdims=True
     )
-    slots = devices * CAP
+    slots = buffer_ref.shape[0]
     code = jnp.where(target < devices, target * CAP + rank, slots)
     ages = by_request(row, old)
     first = by_request(row, [r * MAXB for r in range(requests)])
@@ -294,18 +319,13 @@
     lax.fori_loop(0, prefix_ref.shape[0], gather, 0, unroll=8)
     taken.wait()
 
-    def page(i):
+    def fill(i, _):
         at = take_s[0, i]
-        found = pool_ref[table_ref[0, jnp.maximum(at, 0)]]
-        return jnp.where(at >= 0, found, jnp.zeros_like(found))
-
-    def fill(o, _):
-        for j in range(EARLY):
-            early_ref[o * EARLY + j] = page(o * CAP + j)
-        late_ref[o] = page(o * CAP + EARLY)
+        page = pool_ref[table_ref[0, jnp.maximum(at, 0)]]
+        buffer_ref[i] = jnp.where(at >= 0, page, jnp.zeros_like(page))
         return 0
 
-    lax.fori_loop(0, devices, fill, 0, unroll=4)
+    lax.fori_loop(0, slots, fill, 0, unroll=8)
     for copy in copies[6:]:
         copy.wait()
 
@@ -321,15 +341,14 @@
         functools.partial(prepare_kernel, devices),
         out_shape=[
             jax.ShapeDtypeStruct((tokens, half), jnp.float32),
-            pltpu.HBM((devices * EARLY,) + pool.shape[1:], pool.dtype),
-            pltpu.HBM((devices,) + pool.shape[1:], pool.dtype),
+            pltpu.HBM((slots,) + pool.shape[1:], pool.dtype),
             jax.ShapeDtypeStruct((table.shape[1],) + pool.shape[1:], pool.dtype),
             jax.ShapeDtypeStruct((1, 128), jnp.int32),
             pltpu.VMEM(wq.shape, wq.dtype),
             pltpu.VMEM((depth, 2 * HEAD_DIMENSION), wk.dtype),
         ],
         in_specs=[ANY] * 6 + [VMEM] + [ANY] * 3,
-        out_specs=[VMEM] * 7,
+        out_specs=[VMEM] * 6,
         scratch_shapes=[
             pltpu.SMEM(prefix_len.shape, jnp.int32),
             pltpu.SMEM(new_len.shape, jnp.int32),
@@ -491,28 +510,23 @@
     )(order, new_len, prefix_len, q, kv, in_hbm(prefix), in_hbm(w))
 
 
-def merge_kernel(early_ref, late_ref, out_ref):
-    out_ref[:, :EARLY] = early_ref[...]
-    out_ref[:, EARLY:] = late_ref[...]
-
-
-def merged(early, late):
-    devices = early.shape[0]
-    page = early.shape[2:]
-
-    def spec(slots):
-        return pl.BlockSpec((devices // 8, slots) + page, lambda i: (i, 0, 0, 0))
-
+def copy_kernel(in_ref, out_ref):
+    out_ref[...] = in_ref[...]
+
+
+def copied(pages):
+    block = (pages.shape[0] // 8,) + pages.shape[1:]
+    spec = pl.BlockSpec(block, lambda i: (i,) + (0,) * (len(block) - 1))
     return pl.pallas_call(
-        merge_kernel,
+        copy_kernel,
         grid=(8,),
-        in_specs=[spec(EARLY), spec(CAP - EARLY)],
-        out_specs=spec(CAP),
-        out_shape=jax.ShapeDtypeStruct((devices, CAP) + page, early.dtype),
+        in_specs=[spec],
+        out_specs=spec,
+        out_shape=jax.ShapeDtypeStruct(pages.shape, pages.dtype),
         compiler_params=pltpu.CompilerParams(vmem_limit_bytes=16 * MIB),
-        cost_estimate=pl.CostEstimate(flops=0, bytes_accessed=6 * MIB, transcendentals=0),
+        cost_estimate=pl.CostEstimate(flops=0, bytes_accessed=4 * pages.size, transcendentals=0),
         name="keep",
-    )(early, late)
+    )(pages)
 
 
 def rotary_tables(angles):
@@ -590,10 +604,10 @@
     )
     groups, far = lax.optimization_barrier((groups, far))
     far_z = send(far, 0, 1)
-    gathered = (normed, near_z, right, left, right_z, left_z, far, far_z)
+    gathered = (normed, near_z, right, left, far, right_z, left_z, far_z)
 
     pool = kv_pool[0, :, :, 0, :]
-    angles, early, late, prefix_pages, place, wq, wkv = prepare(
+    angles, buffer, prefix_pages, place, wq, wkv = prepare(
         devices,
         tokens,
         prefix_len,
@@ -607,18 +621,15 @@
         value_weight_matrix[0],
     )
     cos, sin = rotary_tables(angles)
-    q, kv, early, late = project(order, place, gathered, wq, wkv, cos, sin, early, late)
-
-    def deliver(pages):
-        return lax.all_to_all(
-            pages.reshape(devices, -1, PAGE_TOKENS, 2 * HEAD_DIMENSION),
-            ("section", "tp", "dec"),
-            split_axis=0,
-            concat_axis=0,
-            tiled=True,
-        )
-
-    early = deliver(early)
+    q, kv, buffer = project(order, place, gathered, wq, wkv, cos, sin, buffer)
+    received_pages = lax.all_to_all(
+        buffer.reshape(devices, CAP, PAGE_TOKENS, 2 * HEAD_DIMENSION),
+        ("section", "tp", "dec"),
+        split_axis=0,
+        concat_axis=0,
+        tiled=True,
+    )
+
     parts = dict(
         zip(
             PIECES,
@@ -638,22 +649,20 @@
     from_left_z = send(parts[1, 1], 1, 0)
     from_right_z = send(parts[3, 1], 3, 0)
 
-    early, far_pair, from_left_z, from_right_z = lax.optimization_barrier(
-        (early, far_pair, from_left_z, from_right_z)
-    )
+    from_left = send(parts[1, 0], 1, 0)
+    from_right = send(parts[3, 0], 3, 0)
 
     def total(*terms):
         return sum(t.astype(jnp.float32) for t in terms)
 
-    from_left = send(parts[1, 0], 1, 0)
-    from_right = send(parts[3, 0], 3, 0)
+    received_pages, far_pair, from_left_z, from_right_z = lax.optimization_barrier(
+        (received_pages, far_pair, from_left_z, from_right_z)
+    )
     from_far = send(total(parts[2, 0], far_pair).astype(jnp.bfloat16), 2, 0)
-    from_z = send_on(total(parts[0, 1], from_left_z, from_right_z).astype(jnp.bfloat16), 0, 1)
-    own = send_on(
-        total(x, parts[0, 0], from_left, from_right, from_far).astype(jnp.bfloat16), 0, 0
-    )
-    kept = merged(early, deliver(late))
-    passed = total(own, from_z).astype(jnp.bfloat16)[None]
+    from_z = send(total(parts[0, 1], from_left_z, from_right_z).astype(jnp.bfloat16), 0, 1)
+    mixed = total(x, parts[0, 0], from_left, from_right, from_z, from_far).astype(jnp.bfloat16)
+    passed = shifted(mixed, "section", 1)[None]
+    kept = copied(received_pages)
 
     me = (lax.axis_index("section") * n_tp + tp) * n_dec + lax.axis_index("dec")
     received_tags = jnp.broadcast_to(

time: 149 us -> 146 us (0.980)
  starting transfers between devices: 47.2 us -> 39.1 us
  waiting for transfers between devices: 58.6 us -> 62.1 us
  local copies, waits for them, and re-layouts: 2.97 us -> 4.83 us
    ppermute x13 -> x14, waiting for transfers between devices: 34.5 us -> 45 us  [send(): return lax.ppermute(block, 'tp', tp_route(dx, dz, lax.axis_size('tp')))]
    all_to_all x2 -> x1, waiting for transfers between devices: 10.1 us -> 0.01 us  [on_device(): lax.all_to_all(buffer.reshape(devices, CAP, PAGE_TOKENS, 2 * HEAD_DIMENSI...]
    all_to_all x2 -> x1, starting transfers between devices: 14.5 us -> 7.61 us  [on_device(): lax.all_to_all(buffer.reshape(devices, CAP, PAGE_TOKENS, 2 * HEAD_DIMENSI...]
    all_to_all x1, waiting for transfers between devices: 4.29 us -> 7.4 us  [on_device(): lax.all_to_all(jnp.broadcast_to(plain, (n_section * n_dec,) + plain.shape...]
    broadcast_in_dim x1 -> x0, other arithmetic: 2.11 us -> none  [on_device(): passed = total(own, from_z).astype(jnp.bfloat16)[None]]
    unnamed x13 -> x10, local copies, waits for them, and re-layouts: 0.63 us -> 2.49 us
    ppermute x2 -> x1, starting transfers between devices: 3.25 us -> 1.47 us  [shifted(): lax.ppermute(block, axis, [((i - distance) % count, i) for i in range(cou...]
    pallas_call x2 -> x3, Pallas kernels: 8.74 us -> 9.58 us  [the longest x1 3.48 us: project(): pl.pallas_call(qkv_kernel, in_specs=[SMEM, SMEM] + [VMEM] * (8 - SOON + 6...]
  transfers between devices with their start and end apart: 18 -> 17, of which waited for: 9 -> 8; matrix products, arithmetic and copies ran while one was open for 7% -> 6% of each run, Pallas kernels for 15% -> 17%
where the time goes in v3:
time: 146 us
  waiting for transfers between devices  62.1 us (43%)
  starting transfers between devices  39.1 us (27%)
  Pallas kernels  29.6 us (20%)
  other arithmetic  9.03 us (6%)
  local copies, waits for them, and re-layouts  4.83 us (3%)
    ppermute x14, waiting for transfers between devices, send(): return lax.ppermute(block, 'tp', tp_route(dx, dz, lax.axis_size('tp')))  45 us
    ppermute x14, starting transfers between devices, send(): return lax.ppermute(block, 'tp', tp_route(dx, dz, lax.axis_size('tp')))  22.5 us
    pallas_call x1, Pallas kernels, attend(): pl.pallas_call(attention_kernel, out_shape=[pltpu.HBM((ROWS, columns), jn...  11.8 us
    ppermute x1, waiting for transfers between devices, shifted(): lax.ppermute(block, axis, [((i - distance) % count, i) for i in range(cou...  9.62 us
    all_to_all x1, starting transfers between devices, on_device(): lax.all_to_all(buffer.reshape(devices, CAP, PAGE_TOKENS, 2 * HEAD_DIMENSI...  7.61 us
    all_to_all x1, starting transfers between devices, on_device(): lax.all_to_all(jnp.broadcast_to(plain, (n_section * n_dec,) + plain.shape...  7.59 us
    all_to_all x1, waiting for transfers between devices, on_device(): lax.all_to_all(jnp.broadcast_to(plain, (n_section * n_dec,) + plain.shape...  7.4 us
    pallas_call x1, Pallas kernels, prepare(): pl.pallas_call(functools.partial(prepare_kernel, devices), out_shape=[jax...  6.81 us
  transfers between devices with their start and end apart: 17, of which 8 were waited for; matrix products, arithmetic and copies ran while one was open for 6% of the time, Pallas kernels for 17%

profile of v3, /device:TPU:0, one launch (start us, length us, event | category | flops | bytes accessed | tf_op | source)
XLA Modules:
  0.0 145.5 jit_solution(6521669643422641942)
XLA Ops:
  0.6 1.4 norm.1.refs_0_
  2.0 2.1 %collective-permute-start = (bf16[32,8192]{1,0:T(8,128)(2,1)S(1)}, bf16[32,8192]{1,0:T(8,128)(2,1)S(1)}, u32[]{:S(2)}, u32[]{:S(2)}) collective-permute-start(bf16[32,8192]{1,0:T(8,128)(2,1)S(1)} %norm.1.refs_0_), channel_id=1, source_target_pairs={{0,4},{4,0},{8,12},{12,8},{16,20},{20,16},{24,28},{28,24},{1,5},{5... | collective-permute-start | bytes 1572872 | tf_op jit(solution)/shard_map/ppermute | solution.py:37
  4.1 3.0 %collective-permute-start.3 = (bf16[32,8192]{1,0:T(8,128)(2,1)S(1)}, bf16[32,8192]{1,0:T(8,128)(2,1)S(1)}, u32[]{:S(2)}, u32[]{:S(2)}) collective-permute-start(bf16[32,8192]{1,0:T(8,128)(2,1)S(1)} %norm.1.refs_0_), channel_id=1, source_target_pairs={{0,16},{4,20},{8,24},{12,28},{16,0},{20,4},{24,8},{28,12},{1,17},{... | collective-permute-start | bytes 1572872 | tf_op jit(solution)/shard_map/ppermute | solution.py:37
  7.1 0.6 collective-permute-start.6
  7.7 2.6 %collective-permute-start.5 = (bf16[32,8192]{1,0:T(8,128)(2,1)S(1)}, bf16[32,8192]{1,0:T(8,128)(2,1)S(1)}, u32[]{:S(2)}, u32[]{:S(2)}) collective-permute-start(bf16[32,8192]{1,0:T(8,128)(2,1)S(1)} %norm.1.refs_0_), channel_id=1, source_target_pairs={{0,24},{4,28},{8,0},{12,4},{16,8},{20,12},{24,16},{28,20},{1,25},{... | collective-permute-start | bytes 1572872 | tf_op jit(solution)/shard_map/ppermute | solution.py:37
  10.4 0.8 pad_add_fusion
  11.2 0.6 broadcast_in_dim.42
  11.8 7.6 %all-to-all-start = ((s32[16,1,236]{2,1,0:T(1,128)}), s32[16,1,236]{2,1,0:T(1,128)S(1)}, u32[]{:S(2)}, u32[]{:S(2)}) async-start(s32[16,1,236]{2,1,0:T(1,128)} %broadcast_in_dim.42), calls=%async_computation | async-start | bytes 32768 | tf_op jit(solution)/shard_map/all_to_all | solution.py:598
  19.5 0.1 stack.35.order.order_ref
  19.6 7.4 %all-to-all-done = s32[16,1,236]{2,1,0:T(1,128)S(1)} async-done(((s32[16,1,236]{2,1,0:T(1,128)}), s32[16,1,236]{2,1,0:T(1,128)S(1)}, u32[]{:S(2)}, u32[]{:S(2)}) %all-to-all-start) | async-done | bytes 15136 | tf_op jit(solution)/shard_map/all_to_all | solution.py:598
  27.0 0.6 copy.25
  27.6 3.2 %collective-permute-start.1 = (bf16[32,8192]{1,0:T(8,128)(2,1)S(1)}, bf16[32,8192]{1,0:T(8,128)(2,1)S(1)}, u32[]{:S(2)}, u32[]{:S(2)}) collective-permute-start(bf16[32,8192]{1,0:T(8,128)(2,1)S(1)} %collective-permute-done.refs_1_), channel_id=1, source_target_pairs={{0,24},{4,28},{8,0},{12,4},{16,8},{20,12},{24,16},{28,20},{1,25},{... | collective-permute-start | bytes 1572872 | tf_op jit(solution)/shard_map/ppermute | solution.py:37
  30.8 6.8 %prepare.1 = (f32[256,64]{1,0:T(8,128)S(1)}, bf16[384,16,256]{2,1,0:T(8,128)(2,1)}, bf16[160,16,256]{2,1,0:T(8,128)(2,1)S(1)}, s32[1,128]{1,0:T(1,128)S(1)}, bf1...) custom-call(s32[1,4]{1,0:T(1,128)} %prefix_len_ref.1, s32[1,4]{1,0:T(1,128)} %new_len_ref.1, ...), custom_call_target="tpu_custom_call" | custom-call | bytes 20971520 | tf_op jit(solution)/shard_map/prepare/pallas_call | solution.py:340
  37.7 0.5 fusion.8
  38.1 0.1 pad_maximum_fusion
  38.3 2.9 %qkv_first.1 = (bf16[256,512]{1,0:T(8,128)(2,1)S(1)}, bf16[256,256]{1,0:T(8,128)(2,1)S(1)}) custom-call(s32[8]{0:T(128)S(1)} %stack.35.order.order_ref, bf16[32,8192]{1,0:T(8,128)(2,1)S(1)} %norm.1.refs_0_, bf16[32,8192]{1,0:T(8,128)(2,1)S(1)} %collective-permute-done.refs_1_, bf16[32,8192]{1,0:T(8,128)(2,1)S(1)} %collective-permute-done.5.refs_2_, ...), custom_call_target="tpu_custom_call" | custom-call | flops 2013265920 | bytes 15204352 | tf_op jit(solution)/shard_map/qkv_first/pallas_call | solution.py:128
  41.2 3.0 %collective-permute-done.4.refs_2_ = bf16[32,8192]{1,0:T(8,128)(2,1)S(1)} collective-permute-done((bf16[32,8192]{1,0:T(8,128)(2,1)S(1)}, bf16[32,8192]{1,0:T(8,128)(2,1)S(1)}, u32[]{:S(2)}, u32[]{:S(2)}) %collective-permute-start.4) | collective-permute-done | bytes 524320 | tf_op jit(solution)/shard_map/ppermute | solution.py:37
  44.2 3.5 %qkv.1 = (bf16[256,512]{1,0:T(8,128)(2,1)S(1)}, bf16[256,256]{1,0:T(8,128)(2,1)S(1)}, bf16[384,16,256]{2,1,0:T(8,128)(2,1)}) custom-call(s32[8]{0:T(128)S(1)} %stack.35.order.order_ref, s32[1,128]{1,0:T(1,128)S(1)} %get-tuple-element.33.place, bf16[32,8192]{1,0:T(8,128)(2,1)S(1)} %collective-permute-done.1.refs_0_, ...), custom_call_target="tpu_custom_call", output_to_operand_aliasing={{2}: (11, {})} | custom-call | flops 1207959552 | bytes 14155776 | tf_op jit(solution)/shard_map/qkv/pallas_call | solution.py:187
  47.7 7.6 %all-to-all-start.1 = ((bf16[128,3,16,256]{3,2,1,0:T(8,128)(2,1)}), bf16[128,3,16,256]{3,2,1,0:T(8,128)(2,1)S(1)}, u32[]{:S(2)}, u32[]{:S(2)}) async-start(bf16[128,3,16,256]{3,2,1,0:T(8,128)(2,1)} %bitcast.39), calls=%async_computation.1 | async-start | bytes 6291456 | tf_op jit(solution)/shard_map/all_to_all | solution.py:625
  55.4 11.8 %attention.1 = (bf16[32,8192]{1,0:T(8,128)(2,1)}, bf16[32,8192]{1,0:T(8,128)(2,1)}, bf16[32,8192]{1,0:T(8,128)(2,1)}, bf16[32,8192]{1,0:T(8,128)(2,1)}, bf16[32,...) custom-call(s32[8]{0:T(128)S(1)} %stack.35.order.order_ref, ...), custom_call_target="tpu_custom_call" | custom-call | tf_op jit(solution)/shard_map/attention/pallas_call | solution.py:489
  67.2 1.2 collective-permute-start.9
  68.3 1.5 %collective-permute-start.10 = (bf16[32,8192]{1,0:T(8,128)(2,1)}, bf16[32,8192]{1,0:T(8,128)(2,1)}, u32[]{:S(2)}, u32[]{:S(2)}) collective-permute-start(bf16[32,8192]{1,0:T(8,128)(2,1)} %get-tuple-element.53), channel_id=1, source_target_pairs={{0,8},{4,12},{8,16},{12,20},{16,24},{20,28},{24,0},{28,4},{1,9},{5... | collective-permute-start | bytes 1572872 | tf_op jit(solution)/shard_map/ppermute | solution.py:37
  69.8 1.8 %collective-permute-start.11 = (bf16[32,8192]{1,0:T(8,128)(2,1)}, bf16[32,8192]{1,0:T(8,128)(2,1)}, u32[]{:S(2)}, u32[]{:S(2)}) collective-permute-start(bf16[32,8192]{1,0:T(8,128)(2,1)} %get-tuple-element.54), channel_id=1, source_target_pairs={{0,24},{4,28},{8,0},{12,4},{16,8},{20,12},{24,16},{28,20},{1,25},{... | collective-permute-start | bytes 1572872 | tf_op jit(solution)/shard_map/ppermute | solution.py:37
  71.6 0.1 lt.56
  71.7 0.3 collective-permute-start.7
  71.9 3.0 %collective-permute-start.8 = (bf16[32,8192]{1,0:T(8,128)(2,1)}, bf16[32,8192]{1,0:T(8,128)(2,1)}, u32[]{:S(2)}, u32[]{:S(2)}) collective-permute-start(bf16[32,8192]{1,0:T(8,128)(2,1)} %get-tuple-element.49), channel_id=1, source_target_pairs={{0,24},{4,28},{8,0},{12,4},{16,8},{20,12},{24,16},{28,20},{1,25},{... | collective-permute-start | bytes 1572872 | tf_op jit(solution)/shard_map/ppermute | solution.py:37
  74.9 28.2 %collective-permute-done.9 = bf16[32,8192]{1,0:T(8,128)(2,1)} collective-permute-done((bf16[32,8192]{1,0:T(8,128)(2,1)}, bf16[32,8192]{1,0:T(8,128)(2,1)}, u32[]{:S(2)}, u32[]{:S(2)}) %collective-permute-start.9) | collective-permute-done | bytes 524320 | tf_op jit(solution)/shard_map/ppermute | solution.py:37
  103.1 0.1 collective-permute-done.10
  103.2 2.3 %add_convert_fusion.2 = bf16[32,8192]{1,0:T(8,128)(2,1)} fusion(bf16[32,8192]{1,0:T(8,128)(2,1)} %collective-permute-done.11, bf16[32,8192]{1,0:T(8,128)(2,1)} %collective-permute-done.10, bf16[32,8192]{1,0:T(8,128)(2,1)} %get-tuple-element.50), kind=kLoop, calls=%fused_computation.2 | loop fusion | flops 1572864 | bytes 2097152 | tf_op jit(solution)/shard_map/convert_element_type | solution.py:662
  105.6 1.6 %collective-permute-start.12 = (bf16[32,8192]{1,0:T(8,128)(2,1)}, bf16[32,8192]{1,0:T(8,128)(2,1)}, u32[]{:S(2)}, u32[]{:S(2)}) collective-permute-start(bf16[32,8192]{1,0:T(8,128)(2,1)} %add_convert_fusion.2), channel_id=1, source_target_pairs={{0,4},{4,0},{8,12},{12,8},{16,20},{20,16},{24,28},{28,24},{1,5},{5... | collective-permute-start | bytes 1572872 | tf_op jit(solution)/shard_map/ppermute | solution.py:37
  107.2 2.1 %add_convert_fusion.1 = bf16[32,8192]{1,0:T(8,128)(2,1)} fusion(bf16[32,8192]{1,0:T(8,128)(2,1)} %collective-permute-done.9, bf16[32,8192]{1,0:T(8,128)(2,1)} %get-tuple-element.57), kind=kLoop, calls=%fused_computation.1 | loop fusion | flops 1048576 | bytes 1572864 | tf_op jit(solution)/shard_map/convert_element_type | solution.py:661
  109.3 1.6 %collective-permute-start.13 = (bf16[32,8192]{1,0:T(8,128)(2,1)}, bf16[32,8192]{1,0:T(8,128)(2,1)}, u32[]{:S(2)}, u32[]{:S(2)}) collective-permute-start(bf16[32,8192]{1,0:T(8,128)(2,1)} %add_convert_fusion.1), channel_id=1, source_target_pairs={{0,16},{4,20},{8,24},{12,28},{16,0},{20,4},{24,8},{28,12},{1,17},{... | collective-permute-start | bytes 1572872 | tf_op jit(solution)/shard_map/ppermute | solution.py:37
  111.1 0.1 lt.59
  111.2 0.1 fusion
  111.3 0.1 reduce_min.34
  111.4 0.2 fusion.1
  111.6 0.1 reduce_min.36
  111.7 0.2 fusion.2
  111.9 0.1 reduce_min.38
  111.9 2.4 %collective-permute-done.7 = bf16[32,8192]{1,0:T(8,128)(2,1)} collective-permute-done((bf16[32,8192]{1,0:T(8,128)(2,1)}, bf16[32,8192]{1,0:T(8,128)(2,1)}, u32[]{:S(2)}, u32[]{:S(2)}) %collective-permute-start.7) | collective-permute-done | bytes 524320 | tf_op jit(solution)/shard_map/ppermute | solution.py:37
  114.3 5.4 %collective-permute-done.12 = bf16[32,8192]{1,0:T(8,128)(2,1)} collective-permute-done((bf16[32,8192]{1,0:T(8,128)(2,1)}, bf16[32,8192]{1,0:T(8,128)(2,1)}, u32[]{:S(2)}, u32[]{:S(2)}) %collective-permute-start.12) | collective-permute-done | bytes 524320 | tf_op jit(solution)/shard_map/ppermute | solution.py:37
  119.7 5.9 %collective-permute-done.13 = bf16[32,8192]{1,0:T(8,128)(2,1)} collective-permute-done((bf16[32,8192]{1,0:T(8,128)(2,1)}, bf16[32,8192]{1,0:T(8,128)(2,1)}, u32[]{:S(2)}, u32[]{:S(2)}) %collective-permute-start.13) | collective-permute-done | bytes 524320 | tf_op jit(solution)/shard_map/ppermute | solution.py:37
  125.7 3.0 %add_convert_fusion = bf16[32,8192]{1,0:T(8,128)(2,1)} fusion(bf16[32,8192]{1,0:T(8,128)(2,1)} %collective-permute-done.13, bf16[32,8192]{1,0:T(8,128)(2,1)} %collective-permute-done.12, bf16[32,8192]{1,0:T(8,128)(2,1)} %collective-permute-done.8, bf16[32,8192]{1,0:T(8,128)(2,1)} %collective-permute-done.7, bf16[32,8192]{1,0:T(8,128)(2,1)} %get-tuple-element.47, ...), kind=kLoop, calls=%fused_computation | loop fusion | flops 3145728 | bytes 3670016 | tf_op jit(solution)/shard_map/convert_element_type | solution.py:663
  128.7 1.5 %collective-permute-start.14 = (bf16[32,8192]{1,0:T(8,128)(2,1)}, bf16[32,8192]{1,0:T(8,128)(2,1)}, u32[]{:S(2)}, u32[]{:S(2)}) collective-permute-start(bf16[32,8192]{1,0:T(8,128)(2,1)} %add_convert_fusion), channel_id=1, source_target_pairs={{96,0},{0,32},{32,64},{64,96},{97,1},{1,33},{33,65},{65,97},{98,2}... | collective-permute-start | bytes 1572872 | tf_op jit(solution)/shard_map/ppermute | solution.py:42
  130.2 0.7 reshape.114
  130.9 3.2 %keep.1 = bf16[128,3,16,256]{3,2,1,0:T(8,128)(2,1)} custom-call(bf16[128,3,16,256]{3,2,1,0:T(8,128)(2,1)S(1)} %all-to-all-done.1.in_ref), custom_call_target="tpu_custom_call" | custom-call | bytes 6291456 | tf_op jit(solution)/shard_map/keep/pallas_call | solution.py:520
  134.1 9.6 %collective-permute-done.14 = bf16[32,8192]{1,0:T(8,128)(2,1)} collective-permute-done((bf16[32,8192]{1,0:T(8,128)(2,1)}, bf16[32,8192]{1,0:T(8,128)(2,1)}, u32[]{:S(2)}, u32[]{:S(2)}) %collective-permute-start.14) | collective-permute-done | bytes 524320 | tf_op jit(solution)/shard_map/ppermute | solution.py:42
  143.7 1.9 %copy.28 = bf16[1,32,8192]{2,1,0:T(8,128)(2,1)} copy(bf16[1,32,8192]{2,1,0:T(8,128)(2,1)} %bitcast.22) | data formatting | bytes 1048576
  (29 shorter events, 0.3 us)
Async XLA Ops:
  2.0 25.6 %collective-permute-start = (bf16[32,8192]{1,0:T(8,128)(2,1)S(1)}, bf16[32,8192]{1,0:T(8,128)(2,1)S(1)}, u32[]{:S(2)}, u32[]{:S(2)}) collective-permute-start(bf16[32,8192]{1,0:T(8,128)(2,1)S(1)} %norm.1.refs_0_), channel_id=1, source_target_pairs={{0,4},{4,0},{8,12},{12,8},{16,20},{20,16},{24,28},{28,24},{1,5},{5... | collective-permute-start | bytes 1572872 | tf_op jit(solution)/shard_map/ppermute | solution.py:37
  4.1 26.7 %collective-permute-start.3 = (bf16[32,8192]{1,0:T(8,128)(2,1)S(1)}, bf16[32,8192]{1,0:T(8,128)(2,1)S(1)}, u32[]{:S(2)}, u32[]{:S(2)}) collective-permute-start(bf16[32,8192]{1,0:T(8,128)(2,1)S(1)} %norm.1.refs_0_), channel_id=1, source_target_pairs={{0,16},{4,20},{8,24},{12,28},{16,0},{20,4},{24,8},{28,12},{1,17},{... | collective-permute-start | bytes 1572872 | tf_op jit(solution)/shard_map/ppermute | solution.py:37
  7.1 31.2 %collective-permute-start.6 = (bf16[32,8192]{1,0:T(8,128)(2,1)S(1)}, bf16[32,8192]{1,0:T(8,128)(2,1)S(1)}, u32[]{:S(2)}, u32[]{:S(2)}) collective-permute-start(bf16[32,8192]{1,0:T(8,128)(2,1)S(1)} %norm.1.refs_0_), channel_id=1, source_target_pairs={{0,8},{4,12},{8,16},{12,20},{16,24},{20,28},{24,0},{28,4},{1,9},{5... | collective-permute-start | bytes 1572872 | tf_op jit(solution)/shard_map/ppermute | solution.py:37
  7.7 30.6 %collective-permute-start.5 = (bf16[32,8192]{1,0:T(8,128)(2,1)S(1)}, bf16[32,8192]{1,0:T(8,128)(2,1)S(1)}, u32[]{:S(2)}, u32[]{:S(2)}) collective-permute-start(bf16[32,8192]{1,0:T(8,128)(2,1)S(1)} %norm.1.refs_0_), channel_id=1, source_target_pairs={{0,24},{4,28},{8,0},{12,4},{16,8},{20,12},{24,16},{28,20},{1,25},{... | collective-permute-start | bytes 1572872 | tf_op jit(solution)/shard_map/ppermute | solution.py:37
  11.8 15.2 %all-to-all-start = ((s32[16,1,236]{2,1,0:T(1,128)}), s32[16,1,236]{2,1,0:T(1,128)S(1)}, u32[]{:S(2)}, u32[]{:S(2)}) async-start(s32[16,1,236]{2,1,0:T(1,128)} %broadcast_in_dim.42), calls=%async_computation | async-start | bytes 32768 | tf_op jit(solution)/shard_map/all_to_all | solution.py:598
  27.6 16.6 %collective-permute-start.2 = (bf16[32,8192]{1,0:T(8,128)(2,1)S(1)}, bf16[32,8192]{1,0:T(8,128)(2,1)S(1)}, u32[]{:S(2)}, u32[]{:S(2)}) collective-permute-start(bf16[32,8192]{1,0:T(8,128)(2,1)S(1)} %collective-permute-done.refs_1_), channel_id=1, source_target_pairs={{0,8},{4,12},{8,16},{12,20},{16,24},{20,28},{24,0},{28,4},{1,9},{5... | collective-permute-start | bytes 1572872 | tf_op jit(solution)/shard_map/ppermute | solution.py:37
  27.6 16.6 %collective-permute-start.1 = (bf16[32,8192]{1,0:T(8,128)(2,1)S(1)}, bf16[32,8192]{1,0:T(8,128)(2,1)S(1)}, u32[]{:S(2)}, u32[]{:S(2)}) collective-permute-start(bf16[32,8192]{1,0:T(8,128)(2,1)S(1)} %collective-permute-done.refs_1_), channel_id=1, source_target_pairs={{0,24},{4,28},{8,0},{12,4},{16,8},{20,12},{24,16},{28,20},{1,25},{... | collective-permute-start | bytes 1572872 | tf_op jit(solution)/shard_map/ppermute | solution.py:37
  30.8 13.4 %collective-permute-start.4 = (bf16[32,8192]{1,0:T(8,128)(2,1)S(1)}, bf16[32,8192]{1,0:T(8,128)(2,1)S(1)}, u32[]{:S(2)}, u32[]{:S(2)}) collective-permute-start(bf16[32,8192]{1,0:T(8,128)(2,1)S(1)} %collective-permute-done.3.refs_4_), channel_id=1, source_target_pairs={{0,4},{4,0},{8,12},{12,8},{16,20},{20,16},{24,28},{28,24},{1,5},{5... | collective-permute-start | bytes 1572872 | tf_op jit(solution)/shard_map/ppermute | solution.py:37
  37.6 3.6 %copy-start = (bf16[160,16,256]{2,1,0:T(8,128)(2,1)}, bf16[160,16,256]{2,1,0:T(8,128)(2,1)S(1)}, u32[]{:S(2)}) copy-start(bf16[160,16,256]{2,1,0:T(8,128)(2,1)S(1)} %get-tuple-element.46) | copy-start | bytes 3932164
  47.7 7.6 %copy-start.1 = (s32[1,4]{1,0:T(1,128)S(1)}, s32[1,4]{1,0:T(1,128)}, u32[]{:S(2)}) copy-start(s32[1,4]{1,0:T(1,128)} %new_len_ref.1) | copy-start | bytes 52
  47.7 7.6 %copy-start.2 = (s32[1,4]{1,0:T(1,128)S(1)}, s32[1,4]{1,0:T(1,128)}, u32[]{:S(2)}) copy-start(s32[1,4]{1,0:T(1,128)} %prefix_len_ref.1) | copy-start | bytes 52
  47.7 55.5 %all-to-all-start.1 = ((bf16[128,3,16,256]{3,2,1,0:T(8,128)(2,1)}), bf16[128,3,16,256]{3,2,1,0:T(8,128)(2,1)S(1)}, u32[]{:S(2)}, u32[]{:S(2)}) async-start(bf16[128,3,16,256]{3,2,1,0:T(8,128)(2,1)} %bitcast.39), calls=%async_computation.1 | async-start | bytes 6291456 | tf_op jit(solution)/shard_map/all_to_all | solution.py:625
  67.2 43.8 %copy-start.3 = (s32[16,1,236]{2,0,1:T(8,128)S(1)}, s32[16,1,236]{2,0,1:T(8,128)}, u32[]{:S(2)}) copy-start(s32[16,1,236]{2,0,1:T(8,128)} %copy.25) | copy-start | bytes 45316
  67.2 35.9 %collective-permute-start.9 = (bf16[32,8192]{1,0:T(8,128)(2,1)}, bf16[32,8192]{1,0:T(8,128)(2,1)}, u32[]{:S(2)}, u32[]{:S(2)}) collective-permute-start(bf16[32,8192]{1,0:T(8,128)(2,1)} %get-tuple-element.52), channel_id=1, source_target_pairs={{0,4},{4,0},{8,12},{12,8},{16,20},{20,16},{24,28},{28,24},{1,5},{5... | collective-permute-start | bytes 1572872 | tf_op jit(solution)/shard_map/ppermute | solution.py:37
  68.3 34.9 %collective-permute-start.10 = (bf16[32,8192]{1,0:T(8,128)(2,1)}, bf16[32,8192]{1,0:T(8,128)(2,1)}, u32[]{:S(2)}, u32[]{:S(2)}) collective-permute-start(bf16[32,8192]{1,0:T(8,128)(2,1)} %get-tuple-element.53), channel_id=1, source_target_pairs={{0,8},{4,12},{8,16},{12,20},{16,24},{20,28},{24,0},{28,4},{1,9},{5... | collective-permute-start | bytes 1572872 | tf_op jit(solution)/shard_map/ppermute | solution.py:37
  69.8 33.4 %collective-permute-start.11 = (bf16[32,8192]{1,0:T(8,128)(2,1)}, bf16[32,8192]{1,0:T(8,128)(2,1)}, u32[]{:S(2)}, u32[]{:S(2)}) collective-permute-start(bf16[32,8192]{1,0:T(8,128)(2,1)} %get-tuple-element.54), channel_id=1, source_target_pairs={{0,24},{4,28},{8,0},{12,4},{16,8},{20,12},{24,16},{28,20},{1,25},{... | collective-permute-start | bytes 1572872 | tf_op jit(solution)/shard_map/ppermute | solution.py:37
  71.7 42.6 %collective-permute-start.7 = (bf16[32,8192]{1,0:T(8,128)(2,1)}, bf16[32,8192]{1,0:T(8,128)(2,1)}, u32[]{:S(2)}, u32[]{:S(2)}) collective-permute-start(bf16[32,8192]{1,0:T(8,128)(2,1)} %get-tuple-element.48), channel_id=1, source_target_pairs={{0,8},{4,12},{8,16},{12,20},{16,24},{20,28},{24,0},{28,4},{1,9},{5... | collective-permute-start | bytes 1572872 | tf_op jit(solution)/shard_map/ppermute | solution.py:37
  71.9 42.4 %collective-permute-start.8 = (bf16[32,8192]{1,0:T(8,128)(2,1)}, bf16[32,8192]{1,0:T(8,128)(2,1)}, u32[]{:S(2)}, u32[]{:S(2)}) collective-permute-start(bf16[32,8192]{1,0:T(8,128)(2,1)} %get-tuple-element.49), channel_id=1, source_target_pairs={{0,24},{4,28},{8,0},{12,4},{16,8},{20,12},{24,16},{28,20},{1,25},{... | collective-permute-start | bytes 1572872 | tf_op jit(solution)/shard_map/ppermute | solution.py:37
  105.6 14.1 %collective-permute-start.12 = (bf16[32,8192]{1,0:T(8,128)(2,1)}, bf16[32,8192]{1,0:T(8,128)(2,1)}, u32[]{:S(2)}, u32[]{:S(2)}) collective-permute-start(bf16[32,8192]{1,0:T(8,128)(2,1)} %add_convert_fusion.2), channel_id=1, source_target_pairs={{0,4},{4,0},{8,12},{12,8},{16,20},{20,16},{24,28},{28,24},{1,5},{5... | collective-permute-start | bytes 1572872 | tf_op jit(solution)/shard_map/ppermute | solution.py:37
  109.3 16.4 %collective-permute-start.13 = (bf16[32,8192]{1,0:T(8,128)(2,1)}, bf16[32,8192]{1,0:T(8,128)(2,1)}, u32[]{:S(2)}, u32[]{:S(2)}) collective-permute-start(bf16[32,8192]{1,0:T(8,128)(2,1)} %add_convert_fusion.1), channel_id=1, source_target_pairs={{0,16},{4,20},{8,24},{12,28},{16,0},{20,4},{24,8},{28,12},{1,17},{... | collective-permute-start | bytes 1572872 | tf_op jit(solution)/shard_map/ppermute | solution.py:37
  128.7 15.0 %collective-permute-start.14 = (bf16[32,8192]{1,0:T(8,128)(2,1)}, bf16[32,8192]{1,0:T(8,128)(2,1)}, u32[]{:S(2)}, u32[]{:S(2)}) collective-permute-start(bf16[32,8192]{1,0:T(8,128)(2,1)} %add_convert_fusion), channel_id=1, source_target_pairs={{96,0},{0,32},{32,64},{64,96},{97,1},{1,33},{33,65},{65,97},{98,2}... | collective-permute-start | bytes 1572872 | tf_op jit(solution)/shard_map/ppermute | solution.py:42

commit v4 on v3

--- a/solution.py
+++ b/solution.py
@@ -660,7 +660,8 @@
     )
     from_far = send(total(parts[2, 0], far_pair).astype(jnp.bfloat16), 2, 0)
     from_z = send(total(parts[0, 1], from_left_z, from_right_z).astype(jnp.bfloat16), 0, 1)
-    mixed = total(x, parts[0, 0], from_left, from_right, from_z, from_far).astype(jnp.bfloat16)
+    ready = lax.optimization_barrier(total(x, parts[0, 0], from_left, from_right))
+    mixed = total(ready, from_z, from_far).astype(jnp.bfloat16)
     passed = shifted(mixed, "section", 1)[None]
     kept = copied(received_pages)
 

time: 146 us -> 144 us (0.986)
  waiting for transfers between devices: 62.1 us -> 60.6 us
    convert_element_type x1, other arithmetic: 3.02 us -> 0.95 us  [on_device(): mixed = total(ready, from_z, from_far).astype(jnp.bfloat16)]
    ppermute x14, waiting for transfers between devices: 45 us -> 43.5 us  [send(): return lax.ppermute(block, 'tp', tp_route(dx, dz, lax.axis_size('tp')))]
  transfers between devices with their start and end apart: 17 -> 17, of which waited for: 8 -> 8; matrix products, arithmetic and copies ran while one was open for 6% -> 7% of each run, Pallas kernels for 17% -> 17%
where the time goes in v4:
time: 144 us; the launch traced here: 143 us
  waiting for transfers between devices  60.6 us (42%)
  starting transfers between devices  39.3 us (27%)
  Pallas kernels  29.6 us (21%)
  other arithmetic  7.64 us (5%)
  local copies, waits for them, and re-layouts  5.41 us (4%)
    ppermute x14, waiting for transfers between devices, send(): return lax.ppermute(block, 'tp', tp_route(dx, dz, lax.axis_size('tp')))  43.5 us
    ppermute x14, starting transfers between devices, send(): return lax.ppermute(block, 'tp', tp_route(dx, dz, lax.axis_size('tp')))  22.6 us
    pallas_call x1, Pallas kernels, attend(): pl.pallas_call(attention_kernel, out_shape=[pltpu.HBM((ROWS, columns), jn...  11.8 us
    ppermute x1, waiting for transfers between devices, shifted(): lax.ppermute(block, axis, [((i - distance) % count, i) for i in range(cou...  9.62 us
    all_to_all x1, starting transfers between devices, on_device(): lax.all_to_all(buffer.reshape(devices, CAP, PAGE_TOKENS, 2 * HEAD_DIMENSI...  7.61 us
    all_to_all x1, starting transfers between devices, on_device(): lax.all_to_all(jnp.broadcast_to(plain, (n_section * n_dec,) + plain.shape...  7.59 us
    all_to_all x1, waiting for transfers between devices, on_device(): lax.all_to_all(jnp.broadcast_to(plain, (n_section * n_dec,) + plain.shape...  7.4 us
    pallas_call x1, Pallas kernels, prepare(): pl.pallas_call(functools.partial(prepare_kernel, devices), out_shape=[jax...  6.81 us
  transfers between devices with their start and end apart: 17, of which 8 were waited for; matrix products, arithmetic and copies ran while one was open for 7% of the time, Pallas kernels for 17%

profile of v4, /device:TPU:0, one launch (start us, length us, event | category | flops | bytes accessed | tf_op | source)
XLA Modules:
  0.0 143.4 jit_solution(2823988704213070411)
XLA Ops:
  0.6 1.4 norm.1.refs_0_
  2.0 2.1 %collective-permute-start = (bf16[32,8192]{1,0:T(8,128)(2,1)S(1)}, bf16[32,8192]{1,0:T(8,128)(2,1)S(1)}, u32[]{:S(2)}, u32[]{:S(2)}) collective-permute-start(bf16[32,8192]{1,0:T(8,128)(2,1)S(1)} %norm.1.refs_0_), channel_id=1, source_target_pairs={{0,4},{4,0},{8,12},{12,8},{16,20},{20,16},{24,28},{28,24},{1,5},{5... | collective-permute-start | bytes 1572872 | tf_op jit(solution)/shard_map/ppermute | solution.py:37
  4.1 3.0 %collective-permute-start.3 = (bf16[32,8192]{1,0:T(8,128)(2,1)S(1)}, bf16[32,8192]{1,0:T(8,128)(2,1)S(1)}, u32[]{:S(2)}, u32[]{:S(2)}) collective-permute-start(bf16[32,8192]{1,0:T(8,128)(2,1)S(1)} %norm.1.refs_0_), channel_id=1, source_target_pairs={{0,16},{4,20},{8,24},{12,28},{16,0},{20,4},{24,8},{28,12},{1,17},{... | collective-permute-start | bytes 1572872 | tf_op jit(solution)/shard_map/ppermute | solution.py:37
  7.1 0.6 collective-permute-start.6
  7.7 2.6 %collective-permute-start.5 = (bf16[32,8192]{1,0:T(8,128)(2,1)S(1)}, bf16[32,8192]{1,0:T(8,128)(2,1)S(1)}, u32[]{:S(2)}, u32[]{:S(2)}) collective-permute-start(bf16[32,8192]{1,0:T(8,128)(2,1)S(1)} %norm.1.refs_0_), channel_id=1, source_target_pairs={{0,24},{4,28},{8,0},{12,4},{16,8},{20,12},{24,16},{28,20},{1,25},{... | collective-permute-start | bytes 1572872 | tf_op jit(solution)/shard_map/ppermute | solution.py:37
  10.4 0.8 pad_add_fusion
  11.2 0.6 broadcast_in_dim.42
  11.8 7.6 %all-to-all-start = ((s32[16,1,236]{2,1,0:T(1,128)}), s32[16,1,236]{2,1,0:T(1,128)S(1)}, u32[]{:S(2)}, u32[]{:S(2)}) async-start(s32[16,1,236]{2,1,0:T(1,128)} %broadcast_in_dim.42), calls=%async_computation | async-start | bytes 32768 | tf_op jit(solution)/shard_map/all_to_all | solution.py:598
  19.5 0.1 stack.35.order.order_ref
  19.6 7.4 %all-to-all-done = s32[16,1,236]{2,1,0:T(1,128)S(1)} async-done(((s32[16,1,236]{2,1,0:T(1,128)}), s32[16,1,236]{2,1,0:T(1,128)S(1)}, u32[]{:S(2)}, u32[]{:S(2)}) %all-to-all-start) | async-done | bytes 15136 | tf_op jit(solution)/shard_map/all_to_all | solution.py:598
  27.0 0.6 copy.25
  27.6 3.2 %collective-permute-start.1 = (bf16[32,8192]{1,0:T(8,128)(2,1)S(1)}, bf16[32,8192]{1,0:T(8,128)(2,1)S(1)}, u32[]{:S(2)}, u32[]{:S(2)}) collective-permute-start(bf16[32,8192]{1,0:T(8,128)(2,1)S(1)} %collective-permute-done.refs_1_), channel_id=1, source_target_pairs={{0,24},{4,28},{8,0},{12,4},{16,8},{20,12},{24,16},{28,20},{1,25},{... | collective-permute-start | bytes 1572872 | tf_op jit(solution)/shard_map/ppermute | solution.py:37
  30.8 6.8 %prepare.1 = (f32[256,64]{1,0:T(8,128)S(1)}, bf16[384,16,256]{2,1,0:T(8,128)(2,1)}, bf16[160,16,256]{2,1,0:T(8,128)(2,1)S(1)}, s32[1,128]{1,0:T(1,128)S(1)}, bf1...) custom-call(s32[1,4]{1,0:T(1,128)} %prefix_len_ref.1, s32[1,4]{1,0:T(1,128)} %new_len_ref.1, ...), custom_call_target="tpu_custom_call" | custom-call | bytes 20971520 | tf_op jit(solution)/shard_map/prepare/pallas_call | solution.py:340
  37.7 0.5 fusion.8
  38.1 0.1 pad_maximum_fusion
  38.3 2.9 %qkv_first.1 = (bf16[256,512]{1,0:T(8,128)(2,1)S(1)}, bf16[256,256]{1,0:T(8,128)(2,1)S(1)}) custom-call(s32[8]{0:T(128)S(1)} %stack.35.order.order_ref, bf16[32,8192]{1,0:T(8,128)(2,1)S(1)} %norm.1.refs_0_, bf16[32,8192]{1,0:T(8,128)(2,1)S(1)} %collective-permute-done.refs_1_, bf16[32,8192]{1,0:T(8,128)(2,1)S(1)} %collective-permute-done.5.refs_2_, ...), custom_call_target="tpu_custom_call" | custom-call | flops 2013265920 | bytes 15204352 | tf_op jit(solution)/shard_map/qkv_first/pallas_call | solution.py:128
  41.2 3.0 %collective-permute-done.4.refs_2_ = bf16[32,8192]{1,0:T(8,128)(2,1)S(1)} collective-permute-done((bf16[32,8192]{1,0:T(8,128)(2,1)S(1)}, bf16[32,8192]{1,0:T(8,128)(2,1)S(1)}, u32[]{:S(2)}, u32[]{:S(2)}) %collective-permute-start.4) | collective-permute-done | bytes 524320 | tf_op jit(solution)/shard_map/ppermute | solution.py:37
  44.2 3.5 %qkv.1 = (bf16[256,512]{1,0:T(8,128)(2,1)S(1)}, bf16[256,256]{1,0:T(8,128)(2,1)S(1)}, bf16[384,16,256]{2,1,0:T(8,128)(2,1)}) custom-call(s32[8]{0:T(128)S(1)} %stack.35.order.order_ref, s32[1,128]{1,0:T(1,128)S(1)} %get-tuple-element.33.place, bf16[32,8192]{1,0:T(8,128)(2,1)S(1)} %collective-permute-done.1.refs_0_, ...), custom_call_target="tpu_custom_call", output_to_operand_aliasing={{2}: (11, {})} | custom-call | flops 1207959552 | bytes 14155776 | tf_op jit(solution)/shard_map/qkv/pallas_call | solution.py:187
  47.7 7.6 %all-to-all-start.1 = ((bf16[128,3,16,256]{3,2,1,0:T(8,128)(2,1)}), bf16[128,3,16,256]{3,2,1,0:T(8,128)(2,1)S(1)}, u32[]{:S(2)}, u32[]{:S(2)}) async-start(bf16[128,3,16,256]{3,2,1,0:T(8,128)(2,1)} %bitcast.39), calls=%async_computation.1 | async-start | bytes 6291456 | tf_op jit(solution)/shard_map/all_to_all | solution.py:625
  55.4 0.6 lt.56
  56.0 11.8 %attention.1 = (bf16[32,8192]{1,0:T(8,128)(2,1)}, bf16[32,8192]{1,0:T(8,128)(2,1)}, bf16[32,8192]{1,0:T(8,128)(2,1)}, bf16[32,8192]{1,0:T(8,128)(2,1)}, bf16[32,...) custom-call(s32[8]{0:T(128)S(1)} %stack.35.order.order_ref, ...), custom_call_target="tpu_custom_call" | custom-call | tf_op jit(solution)/shard_map/attention/pallas_call | solution.py:489
  67.8 1.2 collective-permute-start.9
  69.0 1.5 %collective-permute-start.10 = (bf16[32,8192]{1,0:T(8,128)(2,1)}, bf16[32,8192]{1,0:T(8,128)(2,1)}, u32[]{:S(2)}, u32[]{:S(2)}) collective-permute-start(bf16[32,8192]{1,0:T(8,128)(2,1)} %get-tuple-element.53), channel_id=1, source_target_pairs={{0,8},{4,12},{8,16},{12,20},{16,24},{20,28},{24,0},{28,4},{1,9},{5... | collective-permute-start | bytes 1572872 | tf_op jit(solution)/shard_map/ppermute | solution.py:37
  70.5 1.8 %collective-permute-start.11 = (bf16[32,8192]{1,0:T(8,128)(2,1)}, bf16[32,8192]{1,0:T(8,128)(2,1)}, u32[]{:S(2)}, u32[]{:S(2)}) collective-permute-start(bf16[32,8192]{1,0:T(8,128)(2,1)} %get-tuple-element.54), channel_id=1, source_target_pairs={{0,24},{4,28},{8,0},{12,4},{16,8},{20,12},{24,16},{28,20},{1,25},{... | collective-permute-start | bytes 1572872 | tf_op jit(solution)/shard_map/ppermute | solution.py:37
  72.4 0.1 lt.59
  72.5 0.9 fusion
  73.3 0.1 reduce_min.34
  73.4 0.2 fusion.1
  73.7 0.2 fusion.2
  73.9 0.1 reduce_min.38
  74.0 0.3 collective-permute-start.7
  74.2 3.0 %collective-permute-start.8 = (bf16[32,8192]{1,0:T(8,128)(2,1)}, bf16[32,8192]{1,0:T(8,128)(2,1)}, u32[]{:S(2)}, u32[]{:S(2)}) collective-permute-start(bf16[32,8192]{1,0:T(8,128)(2,1)} %get-tuple-element.49), channel_id=1, source_target_pairs={{0,24},{4,28},{8,0},{12,4},{16,8},{20,12},{24,16},{28,20},{1,25},{... | collective-permute-start | bytes 1572872 | tf_op jit(solution)/shard_map/ppermute | solution.py:37
  77.2 25.9 %collective-permute-done.9 = bf16[32,8192]{1,0:T(8,128)(2,1)} collective-permute-done((bf16[32,8192]{1,0:T(8,128)(2,1)}, bf16[32,8192]{1,0:T(8,128)(2,1)}, u32[]{:S(2)}, u32[]{:S(2)}) %collective-permute-start.9) | collective-permute-done | bytes 524320 | tf_op jit(solution)/shard_map/ppermute | solution.py:37
  103.1 0.1 collective-permute-done.10
  103.3 1.6 %add_convert_fusion.2 = bf16[32,8192]{1,0:T(8,128)(2,1)S(1)} fusion(bf16[32,8192]{1,0:T(8,128)(2,1)} %collective-permute-done.11, bf16[32,8192]{1,0:T(8,128)(2,1)} %collective-permute-done.10, bf16[32,8192]{1,0:T(8,128)(2,1)} %get-tuple-element.50), kind=kLoop, calls=%fused_computation.2 | loop fusion | flops 1572864 | bytes 2097152 | tf_op jit(solution)/shard_map/convert_element_type | solution.py:662
  104.9 1.7 %collective-permute-start.12 = (bf16[32,8192]{1,0:T(8,128)(2,1)S(1)}, bf16[32,8192]{1,0:T(8,128)(2,1)S(1)}, u32[]{:S(2)}, u32[]{:S(2)}) collective-permute-start(bf16[32,8192]{1,0:T(8,128)(2,1)S(1)} %add_convert_fusion.2), channel_id=1, source_target_pairs={{0,4},{4,0},{8,12},{12,8},{16,20},{20,16},{24,28},{28,24},{1,5},{5... | collective-permute-start | bytes 1572872 | tf_op jit(solution)/shard_map/ppermute | solution.py:37
  106.6 1.3 add_convert_fusion.1
  107.9 1.7 %collective-permute-start.13 = (bf16[32,8192]{1,0:T(8,128)(2,1)S(1)}, bf16[32,8192]{1,0:T(8,128)(2,1)S(1)}, u32[]{:S(2)}, u32[]{:S(2)}) collective-permute-start(bf16[32,8192]{1,0:T(8,128)(2,1)S(1)} %add_convert_fusion.1), channel_id=1, source_target_pairs={{0,16},{4,20},{8,24},{12,28},{16,0},{20,4},{24,8},{28,12},{1,17},{... | collective-permute-start | bytes 1572872 | tf_op jit(solution)/shard_map/ppermute | solution.py:37
  109.6 4.7 %collective-permute-done.7 = bf16[32,8192]{1,0:T(8,128)(2,1)} collective-permute-done((bf16[32,8192]{1,0:T(8,128)(2,1)}, bf16[32,8192]{1,0:T(8,128)(2,1)}, u32[]{:S(2)}, u32[]{:S(2)}) %collective-permute-start.7) | collective-permute-done | bytes 524320 | tf_op jit(solution)/shard_map/ppermute | solution.py:37
  114.3 1.4 %convert_add_fusion = f32[32,8192]{1,0:T(8,128)S(1)} fusion(bf16[32,8192]{1,0:T(8,128)(2,1)} %collective-permute-done.8, bf16[32,8192]{1,0:T(8,128)(2,1)} %collective-permute-done.7, bf16[32,8192]{1,0:T(8,128)(2,1)S(1)} %copy-done.4, bf16[1,32,8192]{2,1,0:T(8,128)(2,1)S(1)} %copy-done.3), kind=kLoop, calls=%fused_computation.3 | loop fusion | flops 1835008 | bytes 3145728 | tf_op jit(solution)/shard_map/add | solution.py:656
  115.8 3.0 %collective-permute-done.12 = bf16[32,8192]{1,0:T(8,128)(2,1)S(1)} collective-permute-done((bf16[32,8192]{1,0:T(8,128)(2,1)S(1)}, bf16[32,8192]{1,0:T(8,128)(2,1)S(1)}, u32[]{:S(2)}, u32[]{:S(2)}) %collective-permute-start.12) | collective-permute-done | bytes 524320 | tf_op jit(solution)/shard_map/ppermute | solution.py:37
  118.8 6.8 %collective-permute-done.13 = bf16[32,8192]{1,0:T(8,128)(2,1)S(1)} collective-permute-done((bf16[32,8192]{1,0:T(8,128)(2,1)S(1)}, bf16[32,8192]{1,0:T(8,128)(2,1)S(1)}, u32[]{:S(2)}, u32[]{:S(2)}) %collective-permute-start.13) | collective-permute-done | bytes 524320 | tf_op jit(solution)/shard_map/ppermute | solution.py:37
  125.6 0.9 add_convert_fusion
  126.5 1.5 %collective-permute-start.14 = (bf16[32,8192]{1,0:T(8,128)(2,1)}, bf16[32,8192]{1,0:T(8,128)(2,1)}, u32[]{:S(2)}, u32[]{:S(2)}) collective-permute-start(bf16[32,8192]{1,0:T(8,128)(2,1)} %add_convert_fusion), channel_id=1, source_target_pairs={{96,0},{0,32},{32,64},{64,96},{97,1},{1,33},{33,65},{65,97},{98,2}... | collective-permute-start | bytes 1572872 | tf_op jit(solution)/shard_map/ppermute | solution.py:42
  128.0 0.7 reshape.114
  128.7 3.2 %keep.1 = bf16[128,3,16,256]{3,2,1,0:T(8,128)(2,1)} custom-call(bf16[128,3,16,256]{3,2,1,0:T(8,128)(2,1)S(1)} %all-to-all-done.1.in_ref), custom_call_target="tpu_custom_call" | custom-call | bytes 6291456 | tf_op jit(solution)/shard_map/keep/pallas_call | solution.py:520
  131.9 9.6 %collective-permute-done.14 = bf16[32,8192]{1,0:T(8,128)(2,1)} collective-permute-done((bf16[32,8192]{1,0:T(8,128)(2,1)}, bf16[32,8192]{1,0:T(8,128)(2,1)}, u32[]{:S(2)}, u32[]{:S(2)}) %collective-permute-start.14) | collective-permute-done | bytes 524320 | tf_op jit(solution)/shard_map/ppermute | solution.py:42
  141.5 1.9 %copy.28 = bf16[1,32,8192]{2,1,0:T(8,128)(2,1)} copy(bf16[1,32,8192]{2,1,0:T(8,128)(2,1)} %bitcast.22) | data formatting | bytes 1048576
  (34 shorter events, 0.4 us)
Async XLA Ops:
  2.0 25.6 %collective-permute-start = (bf16[32,8192]{1,0:T(8,128)(2,1)S(1)}, bf16[32,8192]{1,0:T(8,128)(2,1)S(1)}, u32[]{:S(2)}, u32[]{:S(2)}) collective-permute-start(bf16[32,8192]{1,0:T(8,128)(2,1)S(1)} %norm.1.refs_0_), channel_id=1, source_target_pairs={{0,4},{4,0},{8,12},{12,8},{16,20},{20,16},{24,28},{28,24},{1,5},{5... | collective-permute-start | bytes 1572872 | tf_op jit(solution)/shard_map/ppermute | solution.py:37
  4.1 26.7 %collective-permute-start.3 = (bf16[32,8192]{1,0:T(8,128)(2,1)S(1)}, bf16[32,8192]{1,0:T(8,128)(2,1)S(1)}, u32[]{:S(2)}, u32[]{:S(2)}) collective-permute-start(bf16[32,8192]{1,0:T(8,128)(2,1)S(1)} %norm.1.refs_0_), channel_id=1, source_target_pairs={{0,16},{4,20},{8,24},{12,28},{16,0},{20,4},{24,8},{28,12},{1,17},{... | collective-permute-start | bytes 1572872 | tf_op jit(solution)/shard_map/ppermute | solution.py:37
  7.1 31.2 %collective-permute-start.6 = (bf16[32,8192]{1,0:T(8,128)(2,1)S(1)}, bf16[32,8192]{1,0:T(8,128)(2,1)S(1)}, u32[]{:S(2)}, u32[]{:S(2)}) collective-permute-start(bf16[32,8192]{1,0:T(8,128)(2,1)S(1)} %norm.1.refs_0_), channel_id=1, source_target_pairs={{0,8},{4,12},{8,16},{12,20},{16,24},{20,28},{24,0},{28,4},{1,9},{5... | collective-permute-start | bytes 1572872 | tf_op jit(solution)/shard_map/ppermute | solution.py:37
  7.7 30.6 %collective-permute-start.5 = (bf16[32,8192]{1,0:T(8,128)(2,1)S(1)}, bf16[32,8192]{1,0:T(8,128)(2,1)S(1)}, u32[]{:S(2)}, u32[]{:S(2)}) collective-permute-start(bf16[32,8192]{1,0:T(8,128)(2,1)S(1)} %norm.1.refs_0_), channel_id=1, source_target_pairs={{0,24},{4,28},{8,0},{12,4},{16,8},{20,12},{24,16},{28,20},{1,25},{... | collective-permute-start | bytes 1572872 | tf_op jit(solution)/shard_map/ppermute | solution.py:37
  11.8 15.2 %all-to-all-start = ((s32[16,1,236]{2,1,0:T(1,128)}), s32[16,1,236]{2,1,0:T(1,128)S(1)}, u32[]{:S(2)}, u32[]{:S(2)}) async-start(s32[16,1,236]{2,1,0:T(1,128)} %broadcast_in_dim.42), calls=%async_computation | async-start | bytes 32768 | tf_op jit(solution)/shard_map/all_to_all | solution.py:598
  27.6 16.6 %collective-permute-start.2 = (bf16[32,8192]{1,0:T(8,128)(2,1)S(1)}, bf16[32,8192]{1,0:T(8,128)(2,1)S(1)}, u32[]{:S(2)}, u32[]{:S(2)}) collective-permute-start(bf16[32,8192]{1,0:T(8,128)(2,1)S(1)} %collective-permute-done.refs_1_), channel_id=1, source_target_pairs={{0,8},{4,12},{8,16},{12,20},{16,24},{20,28},{24,0},{28,4},{1,9},{5... | collective-permute-start | bytes 1572872 | tf_op jit(solution)/shard_map/ppermute | solution.py:37
  27.6 16.6 %collective-permute-start.1 = (bf16[32,8192]{1,0:T(8,128)(2,1)S(1)}, bf16[32,8192]{1,0:T(8,128)(2,1)S(1)}, u32[]{:S(2)}, u32[]{:S(2)}) collective-permute-start(bf16[32,8192]{1,0:T(8,128)(2,1)S(1)} %collective-permute-done.refs_1_), channel_id=1, source_target_pairs={{0,24},{4,28},{8,0},{12,4},{16,8},{20,12},{24,16},{28,20},{1,25},{... | collective-permute-start | bytes 1572872 | tf_op jit(solution)/shard_map/ppermute | solution.py:37
  30.8 13.4 %collective-permute-start.4 = (bf16[32,8192]{1,0:T(8,128)(2,1)S(1)}, bf16[32,8192]{1,0:T(8,128)(2,1)S(1)}, u32[]{:S(2)}, u32[]{:S(2)}) collective-permute-start(bf16[32,8192]{1,0:T(8,128)(2,1)S(1)} %collective-permute-done.3.refs_4_), channel_id=1, source_target_pairs={{0,4},{4,0},{8,12},{12,8},{16,20},{20,16},{24,28},{28,24},{1,5},{5... | collective-permute-start | bytes 1572872 | tf_op jit(solution)/shard_map/ppermute | solution.py:37
  37.7 3.6 %copy-start = (bf16[160,16,256]{2,1,0:T(8,128)(2,1)}, bf16[160,16,256]{2,1,0:T(8,128)(2,1)S(1)}, u32[]{:S(2)}) copy-start(bf16[160,16,256]{2,1,0:T(8,128)(2,1)S(1)} %get-tuple-element.46) | copy-start | bytes 3932164
  47.7 8.3 %copy-start.1 = (s32[1,4]{1,0:T(1,128)S(1)}, s32[1,4]{1,0:T(1,128)}, u32[]{:S(2)}) copy-start(s32[1,4]{1,0:T(1,128)} %new_len_ref.1) | copy-start | bytes 52
  47.7 8.3 %copy-start.2 = (s32[1,4]{1,0:T(1,128)S(1)}, s32[1,4]{1,0:T(1,128)}, u32[]{:S(2)}) copy-start(s32[1,4]{1,0:T(1,128)} %prefix_len_ref.1) | copy-start | bytes 52
  47.7 55.5 %all-to-all-start.1 = ((bf16[128,3,16,256]{3,2,1,0:T(8,128)(2,1)}), bf16[128,3,16,256]{3,2,1,0:T(8,128)(2,1)S(1)}, u32[]{:S(2)}, u32[]{:S(2)}) async-start(bf16[128,3,16,256]{3,2,1,0:T(8,128)(2,1)} %bitcast.39), calls=%async_computation.1 | async-start | bytes 6291456 | tf_op jit(solution)/shard_map/all_to_all | solution.py:625
  56.0 16.2 %copy-start.5 = (s32[16,1,236]{2,0,1:T(8,128)S(1)}, s32[16,1,236]{2,0,1:T(8,128)}, u32[]{:S(2)}) copy-start(s32[16,1,236]{2,0,1:T(8,128)} %copy.25) | copy-start | bytes 45316
  67.8 35.3 %collective-permute-start.9 = (bf16[32,8192]{1,0:T(8,128)(2,1)}, bf16[32,8192]{1,0:T(8,128)(2,1)}, u32[]{:S(2)}, u32[]{:S(2)}) collective-permute-start(bf16[32,8192]{1,0:T(8,128)(2,1)} %get-tuple-element.52), channel_id=1, source_target_pairs={{0,4},{4,0},{8,12},{12,8},{16,20},{20,16},{24,28},{28,24},{1,5},{5... | collective-permute-start | bytes 1572872 | tf_op jit(solution)/shard_map/ppermute | solution.py:37
  69.0 34.2 %collective-permute-start.10 = (bf16[32,8192]{1,0:T(8,128)(2,1)}, bf16[32,8192]{1,0:T(8,128)(2,1)}, u32[]{:S(2)}, u32[]{:S(2)}) collective-permute-start(bf16[32,8192]{1,0:T(8,128)(2,1)} %get-tuple-element.53), channel_id=1, source_target_pairs={{0,8},{4,12},{8,16},{12,20},{16,24},{20,28},{24,0},{28,4},{1,9},{5... | collective-permute-start | bytes 1572872 | tf_op jit(solution)/shard_map/ppermute | solution.py:37
  70.5 32.8 %collective-permute-start.11 = (bf16[32,8192]{1,0:T(8,128)(2,1)}, bf16[32,8192]{1,0:T(8,128)(2,1)}, u32[]{:S(2)}, u32[]{:S(2)}) collective-permute-start(bf16[32,8192]{1,0:T(8,128)(2,1)} %get-tuple-element.54), channel_id=1, source_target_pairs={{0,24},{4,28},{8,0},{12,4},{16,8},{20,12},{24,16},{28,20},{1,25},{... | collective-permute-start | bytes 1572872 | tf_op jit(solution)/shard_map/ppermute | solution.py:37
  74.0 40.3 %collective-permute-start.7 = (bf16[32,8192]{1,0:T(8,128)(2,1)}, bf16[32,8192]{1,0:T(8,128)(2,1)}, u32[]{:S(2)}, u32[]{:S(2)}) collective-permute-start(bf16[32,8192]{1,0:T(8,128)(2,1)} %get-tuple-element.48), channel_id=1, source_target_pairs={{0,8},{4,12},{8,16},{12,20},{16,24},{20,28},{24,0},{28,4},{1,9},{5... | collective-permute-start | bytes 1572872 | tf_op jit(solution)/shard_map/ppermute | solution.py:37
  74.2 40.1 %collective-permute-start.8 = (bf16[32,8192]{1,0:T(8,128)(2,1)}, bf16[32,8192]{1,0:T(8,128)(2,1)}, u32[]{:S(2)}, u32[]{:S(2)}) collective-permute-start(bf16[32,8192]{1,0:T(8,128)(2,1)} %get-tuple-element.49), channel_id=1, source_target_pairs={{0,24},{4,28},{8,0},{12,4},{16,8},{20,12},{24,16},{28,20},{1,25},{... | collective-permute-start | bytes 1572872 | tf_op jit(solution)/shard_map/ppermute | solution.py:37
  103.2 11.1 %copy-start.3 = (bf16[1,32,8192]{2,1,0:T(8,128)(2,1)S(1)}, bf16[1,32,8192]{2,1,0:T(8,128)(2,1)}, u32[]{:S(2)}) copy-start(bf16[1,32,8192]{2,1,0:T(8,128)(2,1)} %param.12) | copy-start | bytes 1572868
  103.2 11.1 %copy-start.4 = (bf16[32,8192]{1,0:T(8,128)(2,1)S(1)}, bf16[32,8192]{1,0:T(8,128)(2,1)}, u32[]{:S(2)}) copy-start(bf16[32,8192]{1,0:T(8,128)(2,1)} %get-tuple-element.47) | copy-start | bytes 1572868
  104.9 13.9 %collective-permute-start.12 = (bf16[32,8192]{1,0:T(8,128)(2,1)S(1)}, bf16[32,8192]{1,0:T(8,128)(2,1)S(1)}, u32[]{:S(2)}, u32[]{:S(2)}) collective-permute-start(bf16[32,8192]{1,0:T(8,128)(2,1)S(1)} %add_convert_fusion.2), channel_id=1, source_target_pairs={{0,4},{4,0},{8,12},{12,8},{16,20},{20,16},{24,28},{28,24},{1,5},{5... | collective-permute-start | bytes 1572872 | tf_op jit(solution)/shard_map/ppermute | solution.py:37
  107.9 17.7 %collective-permute-start.13 = (bf16[32,8192]{1,0:T(8,128)(2,1)S(1)}, bf16[32,8192]{1,0:T(8,128)(2,1)S(1)}, u32[]{:S(2)}, u32[]{:S(2)}) collective-permute-start(bf16[32,8192]{1,0:T(8,128)(2,1)S(1)} %add_convert_fusion.1), channel_id=1, source_target_pairs={{0,16},{4,20},{8,24},{12,28},{16,0},{20,4},{24,8},{28,12},{1,17},{... | collective-permute-start | bytes 1572872 | tf_op jit(solution)/shard_map/ppermute | solution.py:37
  126.5 15.0 %collective-permute-start.14 = (bf16[32,8192]{1,0:T(8,128)(2,1)}, bf16[32,8192]{1,0:T(8,128)(2,1)}, u32[]{:S(2)}, u32[]{:S(2)}) collective-permute-start(bf16[32,8192]{1,0:T(8,128)(2,1)} %add_convert_fusion), channel_id=1, source_target_pairs={{96,0},{0,32},{32,64},{64,96},{97,1},{1,33},{33,65},{65,97},{98,2}... | collective-permute-start | bytes 1572872 | tf_op jit(solution)/shard_map/ppermute | solution.py:42

commit v5 on v4

--- a/solution.py
+++ b/solution.py
@@ -13,7 +13,7 @@
 MAXB = 40
 NB = 56
 CAP = 3
-SOON = 5
+SOON = 4
 ROWS = 32
 
 theta_base = 500000.0

time: 144 us -> 144 us (level)
  blocking collectives: 0 us -> 15 us
  waiting for transfers between devices: 60.6 us -> 53.5 us
  starting transfers between devices: 39.3 us -> 32.5 us
    all_to_all x0 -> x1, blocking collectives: none -> 15 us  [on_device(): lax.all_to_all(jnp.broadcast_to(plain, (n_section * n_dec,) + plain.shape...]
    all_to_all x1 -> x0, starting transfers between devices: 7.59 us -> none  [on_device(): lax.all_to_all(jnp.broadcast_to(plain, (n_section * n_dec,) + plain.shape...]
    all_to_all x1 -> x0, waiting for transfers between devices: 7.4 us -> none  [on_device(): lax.all_to_all(jnp.broadcast_to(plain, (n_section * n_dec,) + plain.shape...]
  transfers between devices with their start and end apart: 17 -> 16, of which waited for: 8 -> 7; matrix products, arithmetic and copies ran while one was open for 7% -> 7% of each run, Pallas kernels for 17% -> 17%
where the time goes in v5:
time: 144 us
  waiting for transfers between devices  53.5 us (37%)
  starting transfers between devices  32.5 us (23%)
  Pallas kernels  29.4 us (20%)
  blocking collectives  15 us (10%)
  other arithmetic  7.64 us (5%)
  local copies, waits for them, and re-layouts  4.81 us (3%)
    ppermute x14, waiting for transfers between devices, send(): return lax.ppermute(block, 'tp', tp_route(dx, dz, lax.axis_size('tp')))  43.9 us
    ppermute x14, starting transfers between devices, send(): return lax.ppermute(block, 'tp', tp_route(dx, dz, lax.axis_size('tp')))  22.6 us
    all_to_all x1, blocking collectives, on_device(): lax.all_to_all(jnp.broadcast_to(plain, (n_section * n_dec,) + plain.shape...  15 us
    pallas_call x1, Pallas kernels, attend(): pl.pallas_call(attention_kernel, out_shape=[pltpu.HBM((ROWS, columns), jn...  11.8 us
    ppermute x1, waiting for transfers between devices, shifted(): lax.ppermute(block, axis, [((i - distance) % count, i) for i in range(cou...  9.62 us
    all_to_all x1, starting transfers between devices, on_device(): lax.all_to_all(buffer.reshape(devices, CAP, PAGE_TOKENS, 2 * HEAD_DIMENSI...  8.39 us
    pallas_call x1, Pallas kernels, prepare(): pl.pallas_call(functools.partial(prepare_kernel, devices), out_shape=[jax...  6.81 us
    pallas_call x1, Pallas kernels, project(): pl.pallas_call(qkv_kernel, in_specs=[SMEM, SMEM] + [VMEM] * (8 - SOON + 6...  3.8 us
  transfers between devices with their start and end apart: 16, of which 7 were waited for; matrix products, arithmetic and copies ran while one was open for 7% of the time, Pallas kernels for 17%

profile of v5, /device:TPU:0, one launch (start us, length us, event | category | flops | bytes accessed | tf_op | source)
XLA Modules:
  0.0 143.8 jit_solution(2196089820828120411)
XLA Ops:
  0.6 1.4 norm.1.refs_0_
  2.0 2.1 %collective-permute-start = (bf16[32,8192]{1,0:T(8,128)(2,1)S(1)}, bf16[32,8192]{1,0:T(8,128)(2,1)S(1)}, u32[]{:S(2)}, u32[]{:S(2)}) collective-permute-start(bf16[32,8192]{1,0:T(8,128)(2,1)S(1)} %norm.1.refs_0_), channel_id=1, source_target_pairs={{0,4},{4,0},{8,12},{12,8},{16,20},{20,16},{24,28},{28,24},{1,5},{5... | collective-permute-start | bytes 1572872 | tf_op jit(solution)/shard_map/ppermute | solution.py:37
  4.1 3.0 %collective-permute-start.1 = (bf16[32,8192]{1,0:T(8,128)(2,1)S(1)}, bf16[32,8192]{1,0:T(8,128)(2,1)S(1)}, u32[]{:S(2)}, u32[]{:S(2)}) collective-permute-start(bf16[32,8192]{1,0:T(8,128)(2,1)S(1)} %norm.1.refs_0_), channel_id=1, source_target_pairs={{0,16},{4,20},{8,24},{12,28},{16,0},{20,4},{24,8},{28,12},{1,17},{... | collective-permute-start | bytes 1572872 | tf_op jit(solution)/shard_map/ppermute | solution.py:37
  7.1 0.6 collective-permute-start.6
  7.7 2.6 %collective-permute-start.5 = (bf16[32,8192]{1,0:T(8,128)(2,1)S(1)}, bf16[32,8192]{1,0:T(8,128)(2,1)S(1)}, u32[]{:S(2)}, u32[]{:S(2)}) collective-permute-start(bf16[32,8192]{1,0:T(8,128)(2,1)S(1)} %norm.1.refs_0_), channel_id=1, source_target_pairs={{0,24},{4,28},{8,0},{12,4},{16,8},{20,12},{24,16},{28,20},{1,25},{... | collective-permute-start | bytes 1572872 | tf_op jit(solution)/shard_map/ppermute | solution.py:37
  10.4 0.8 pad_add_fusion
  11.2 15.0 %all_to_all.14 = s32[16,1,236]{2,1,0:T(1,128)S(1)} all-to-all(s32[16,1,236]{2,1,0:T(1,128)S(1)} %broadcast_in_dim.42), channel_id=1, replica_groups=mesh['section'=4,'tp'=8,'dec'=4] {'section','dec'}, dimensions={0} | all-to-all | bytes 30208 | tf_op jit(solution)/shard_map/all_to_all | solution.py:598
  26.2 0.6 copy.25
  26.8 3.2 %collective-permute-start.2 = (bf16[32,8192]{1,0:T(8,128)(2,1)S(1)}, bf16[32,8192]{1,0:T(8,128)(2,1)}, u32[]{:S(2)}, u32[]{:S(2)}) collective-permute-start(bf16[32,8192]{1,0:T(8,128)(2,1)S(1)} %collective-permute-done.refs_1_), channel_id=1, source_target_pairs={{0,24},{4,28},{8,0},{12,4},{16,8},{20,12},{24,16},{28,20},{1,25},{... | collective-permute-start | bytes 1572872 | tf_op jit(solution)/shard_map/ppermute | solution.py:37
  30.1 0.1 stack.35.order.order_ref
  30.2 6.8 %prepare.1 = (f32[256,64]{1,0:T(8,128)S(1)}, bf16[384,16,256]{2,1,0:T(8,128)(2,1)}, bf16[160,16,256]{2,1,0:T(8,128)(2,1)S(1)}, s32[1,128]{1,0:T(1,128)S(1)}, bf1...) custom-call(s32[1,4]{1,0:T(1,128)} %prefix_len_ref.1, s32[1,4]{1,0:T(1,128)} %new_len_ref.1, ...), custom_call_target="tpu_custom_call" | custom-call | bytes 20971520 | tf_op jit(solution)/shard_map/prepare/pallas_call | solution.py:340
  37.0 0.5 fusion.8
  37.5 0.1 pad_maximum_fusion
  37.7 2.4 %qkv_first.1 = (bf16[256,512]{1,0:T(8,128)(2,1)S(1)}, bf16[256,256]{1,0:T(8,128)(2,1)S(1)}) custom-call(s32[8]{0:T(128)S(1)} %stack.35.order.order_ref, bf16[32,8192]{1,0:T(8,128)(2,1)S(1)} %norm.1.refs_0_, bf16[32,8192]{1,0:T(8,128)(2,1)S(1)} %collective-permute-done.refs_1_, bf16[32,8192]{1,0:T(8,128)(2,1)S(1)} %collective-permute-done.5.refs_2_, ...), custom_call_target="tpu_custom_call" | custom-call | flops 1610612736 | bytes 14680064 | tf_op jit(solution)/shard_map/qkv_first/pallas_call | solution.py:128
  40.1 3.4 %collective-permute-done.4.refs_3_ = bf16[32,8192]{1,0:T(8,128)(2,1)} collective-permute-done((bf16[32,8192]{1,0:T(8,128)(2,1)S(1)}, bf16[32,8192]{1,0:T(8,128)(2,1)}, u32[]{:S(2)}, u32[]{:S(2)}) %collective-permute-start.4) | collective-permute-done | bytes 524320 | tf_op jit(solution)/shard_map/ppermute | solution.py:37
  43.5 3.8 %qkv.1 = (bf16[256,512]{1,0:T(8,128)(2,1)S(1)}, bf16[256,256]{1,0:T(8,128)(2,1)S(1)}, bf16[384,16,256]{2,1,0:T(8,128)(2,1)}) custom-call(s32[8]{0:T(128)S(1)} %stack.35.order.order_ref, s32[1,128]{1,0:T(1,128)S(1)} %get-tuple-element.33.place, bf16[32,8192]{1,0:T(8,128)(2,1)S(1)} %collective-permute-done.1.refs_0_, ...), custom_call_target="tpu_custom_call", output_to_operand_aliasing={{2}: (12, {})} | custom-call | flops 1610612736 | bytes 14680064 | tf_op jit(solution)/shard_map/qkv/pallas_call | solution.py:187
  47.4 8.4 %all-to-all-start.1 = ((bf16[128,3,16,256]{3,2,1,0:T(8,128)(2,1)}), bf16[128,3,16,256]{3,2,1,0:T(8,128)(2,1)S(1)}, u32[]{:S(2)}, u32[]{:S(2)}) async-start(bf16[128,3,16,256]{3,2,1,0:T(8,128)(2,1)} %bitcast.39), calls=%async_computation.1 | async-start | bytes 6291456 | tf_op jit(solution)/shard_map/all_to_all | solution.py:625
  55.8 0.6 lt.56
  56.4 11.8 %attention.1 = (bf16[32,8192]{1,0:T(8,128)(2,1)}, bf16[32,8192]{1,0:T(8,128)(2,1)}, bf16[32,8192]{1,0:T(8,128)(2,1)}, bf16[32,8192]{1,0:T(8,128)(2,1)}, bf16[32,...) custom-call(s32[8]{0:T(128)S(1)} %stack.35.order.order_ref, ...), custom_call_target="tpu_custom_call" | custom-call | tf_op jit(solution)/shard_map/attention/pallas_call | solution.py:489
  68.2 1.2 collective-permute-start.9
  69.4 1.5 %collective-permute-start.10 = (bf16[32,8192]{1,0:T(8,128)(2,1)}, bf16[32,8192]{1,0:T(8,128)(2,1)}, u32[]{:S(2)}, u32[]{:S(2)}) collective-permute-start(bf16[32,8192]{1,0:T(8,128)(2,1)} %get-tuple-element.53), channel_id=1, source_target_pairs={{0,8},{4,12},{8,16},{12,20},{16,24},{20,28},{24,0},{28,4},{1,9},{5... | collective-permute-start | bytes 1572872 | tf_op jit(solution)/shard_map/ppermute | solution.py:37
  70.9 1.8 %collective-permute-start.11 = (bf16[32,8192]{1,0:T(8,128)(2,1)}, bf16[32,8192]{1,0:T(8,128)(2,1)}, u32[]{:S(2)}, u32[]{:S(2)}) collective-permute-start(bf16[32,8192]{1,0:T(8,128)(2,1)} %get-tuple-element.54), channel_id=1, source_target_pairs={{0,24},{4,28},{8,0},{12,4},{16,8},{20,12},{24,16},{28,20},{1,25},{... | collective-permute-start | bytes 1572872 | tf_op jit(solution)/shard_map/ppermute | solution.py:37
  72.7 0.1 lt.58
  72.8 0.1 lt.59
  72.9 0.9 fusion
  73.8 0.1 reduce_min.34
  73.8 0.2 fusion.1
  74.0 0.1 reduce_min.36
  74.1 0.2 fusion.2
  74.3 0.1 reduce_min.38
  74.4 0.3 collective-permute-start.7
  74.7 3.0 %collective-permute-start.8 = (bf16[32,8192]{1,0:T(8,128)(2,1)}, bf16[32,8192]{1,0:T(8,128)(2,1)}, u32[]{:S(2)}, u32[]{:S(2)}) collective-permute-start(bf16[32,8192]{1,0:T(8,128)(2,1)} %get-tuple-element.49), channel_id=1, source_target_pairs={{0,24},{4,28},{8,0},{12,4},{16,8},{20,12},{24,16},{28,20},{1,25},{... | collective-permute-start | bytes 1572872 | tf_op jit(solution)/shard_map/ppermute | solution.py:37
  77.6 25.9 %collective-permute-done.9 = bf16[32,8192]{1,0:T(8,128)(2,1)} collective-permute-done((bf16[32,8192]{1,0:T(8,128)(2,1)}, bf16[32,8192]{1,0:T(8,128)(2,1)}, u32[]{:S(2)}, u32[]{:S(2)}) %collective-permute-start.9) | collective-permute-done | bytes 524320 | tf_op jit(solution)/shard_map/ppermute | solution.py:37
  103.5 0.1 collective-permute-done.10
  103.6 1.6 %add_convert_fusion.2 = bf16[32,8192]{1,0:T(8,128)(2,1)S(1)} fusion(bf16[32,8192]{1,0:T(8,128)(2,1)} %collective-permute-done.11, bf16[32,8192]{1,0:T(8,128)(2,1)} %collective-permute-done.10, bf16[32,8192]{1,0:T(8,128)(2,1)} %get-tuple-element.50), kind=kLoop, calls=%fused_computation.2 | loop fusion | flops 1572864 | bytes 2097152 | tf_op jit(solution)/shard_map/convert_element_type | solution.py:662
  105.3 1.7 %collective-permute-start.12 = (bf16[32,8192]{1,0:T(8,128)(2,1)S(1)}, bf16[32,8192]{1,0:T(8,128)(2,1)S(1)}, u32[]{:S(2)}, u32[]{:S(2)}) collective-permute-start(bf16[32,8192]{1,0:T(8,128)(2,1)S(1)} %add_convert_fusion.2), channel_id=1, source_target_pairs={{0,4},{4,0},{8,12},{12,8},{16,20},{20,16},{24,28},{28,24},{1,5},{5... | collective-permute-start | bytes 1572872 | tf_op jit(solution)/shard_map/ppermute | solution.py:37
  107.0 1.3 add_convert_fusion.1
  108.3 1.7 %collective-permute-start.13 = (bf16[32,8192]{1,0:T(8,128)(2,1)S(1)}, bf16[32,8192]{1,0:T(8,128)(2,1)S(1)}, u32[]{:S(2)}, u32[]{:S(2)}) collective-permute-start(bf16[32,8192]{1,0:T(8,128)(2,1)S(1)} %add_convert_fusion.1), channel_id=1, source_target_pairs={{0,16},{4,20},{8,24},{12,28},{16,0},{20,4},{24,8},{28,12},{1,17},{... | collective-permute-start | bytes 1572872 | tf_op jit(solution)/shard_map/ppermute | solution.py:37
  110.0 4.7 %collective-permute-done.7 = bf16[32,8192]{1,0:T(8,128)(2,1)} collective-permute-done((bf16[32,8192]{1,0:T(8,128)(2,1)}, bf16[32,8192]{1,0:T(8,128)(2,1)}, u32[]{:S(2)}, u32[]{:S(2)}) %collective-permute-start.7) | collective-permute-done | bytes 524320 | tf_op jit(solution)/shard_map/ppermute | solution.py:37
  114.7 1.4 %convert_add_fusion = f32[32,8192]{1,0:T(8,128)S(1)} fusion(bf16[32,8192]{1,0:T(8,128)(2,1)} %collective-permute-done.8, bf16[32,8192]{1,0:T(8,128)(2,1)} %collective-permute-done.7, bf16[32,8192]{1,0:T(8,128)(2,1)S(1)} %copy-done.4, bf16[1,32,8192]{2,1,0:T(8,128)(2,1)S(1)} %copy-done.3), kind=kLoop, calls=%fused_computation.3 | loop fusion | flops 1835008 | bytes 3145728 | tf_op jit(solution)/shard_map/add | solution.py:656
  116.2 3.0 %collective-permute-done.12 = bf16[32,8192]{1,0:T(8,128)(2,1)S(1)} collective-permute-done((bf16[32,8192]{1,0:T(8,128)(2,1)S(1)}, bf16[32,8192]{1,0:T(8,128)(2,1)S(1)}, u32[]{:S(2)}, u32[]{:S(2)}) %collective-permute-start.12) | collective-permute-done | bytes 524320 | tf_op jit(solution)/shard_map/ppermute | solution.py:37
  119.2 6.8 %collective-permute-done.13 = bf16[32,8192]{1,0:T(8,128)(2,1)S(1)} collective-permute-done((bf16[32,8192]{1,0:T(8,128)(2,1)S(1)}, bf16[32,8192]{1,0:T(8,128)(2,1)S(1)}, u32[]{:S(2)}, u32[]{:S(2)}) %collective-permute-start.13) | collective-permute-done | bytes 524320 | tf_op jit(solution)/shard_map/ppermute | solution.py:37
  126.0 0.9 add_convert_fusion
  126.9 1.5 %collective-permute-start.14 = (bf16[32,8192]{1,0:T(8,128)(2,1)}, bf16[32,8192]{1,0:T(8,128)(2,1)}, u32[]{:S(2)}, u32[]{:S(2)}) collective-permute-start(bf16[32,8192]{1,0:T(8,128)(2,1)} %add_convert_fusion), channel_id=1, source_target_pairs={{96,0},{0,32},{32,64},{64,96},{97,1},{1,33},{33,65},{65,97},{98,2}... | collective-permute-start | bytes 1572872 | tf_op jit(solution)/shard_map/ppermute | solution.py:42
  128.4 0.7 reshape.114
  129.1 3.2 %keep.1 = bf16[128,3,16,256]{3,2,1,0:T(8,128)(2,1)} custom-call(bf16[128,3,16,256]{3,2,1,0:T(8,128)(2,1)S(1)} %all-to-all-done.1.in_ref), custom_call_target="tpu_custom_call" | custom-call | bytes 6291456 | tf_op jit(solution)/shard_map/keep/pallas_call | solution.py:520
  132.3 9.6 %collective-permute-done.14 = bf16[32,8192]{1,0:T(8,128)(2,1)} collective-permute-done((bf16[32,8192]{1,0:T(8,128)(2,1)}, bf16[32,8192]{1,0:T(8,128)(2,1)}, u32[]{:S(2)}, u32[]{:S(2)}) %collective-permute-start.14) | collective-permute-done | bytes 524320 | tf_op jit(solution)/shard_map/ppermute | solution.py:42
  141.9 1.9 %copy.28 = bf16[1,32,8192]{2,1,0:T(8,128)(2,1)} copy(bf16[1,32,8192]{2,1,0:T(8,128)(2,1)} %bitcast.22) | data formatting | bytes 1048576
  (33 shorter events, 0.2 us)
Async XLA Ops:
  2.0 24.8 %collective-permute-start = (bf16[32,8192]{1,0:T(8,128)(2,1)S(1)}, bf16[32,8192]{1,0:T(8,128)(2,1)S(1)}, u32[]{:S(2)}, u32[]{:S(2)}) collective-permute-start(bf16[32,8192]{1,0:T(8,128)(2,1)S(1)} %norm.1.refs_0_), channel_id=1, source_target_pairs={{0,4},{4,0},{8,12},{12,8},{16,20},{20,16},{24,28},{28,24},{1,5},{5... | collective-permute-start | bytes 1572872 | tf_op jit(solution)/shard_map/ppermute | solution.py:37
  4.1 25.9 %collective-permute-start.1 = (bf16[32,8192]{1,0:T(8,128)(2,1)S(1)}, bf16[32,8192]{1,0:T(8,128)(2,1)S(1)}, u32[]{:S(2)}, u32[]{:S(2)}) collective-permute-start(bf16[32,8192]{1,0:T(8,128)(2,1)S(1)} %norm.1.refs_0_), channel_id=1, source_target_pairs={{0,16},{4,20},{8,24},{12,28},{16,0},{20,4},{24,8},{28,12},{1,17},{... | collective-permute-start | bytes 1572872 | tf_op jit(solution)/shard_map/ppermute | solution.py:37
  7.1 30.5 %collective-permute-start.6 = (bf16[32,8192]{1,0:T(8,128)(2,1)S(1)}, bf16[32,8192]{1,0:T(8,128)(2,1)S(1)}, u32[]{:S(2)}, u32[]{:S(2)}) collective-permute-start(bf16[32,8192]{1,0:T(8,128)(2,1)S(1)} %norm.1.refs_0_), channel_id=1, source_target_pairs={{0,8},{4,12},{8,16},{12,20},{16,24},{20,28},{24,0},{28,4},{1,9},{5... | collective-permute-start | bytes 1572872 | tf_op jit(solution)/shard_map/ppermute | solution.py:37
  7.7 30.0 %collective-permute-start.5 = (bf16[32,8192]{1,0:T(8,128)(2,1)S(1)}, bf16[32,8192]{1,0:T(8,128)(2,1)S(1)}, u32[]{:S(2)}, u32[]{:S(2)}) collective-permute-start(bf16[32,8192]{1,0:T(8,128)(2,1)S(1)} %norm.1.refs_0_), channel_id=1, source_target_pairs={{0,24},{4,28},{8,0},{12,4},{16,8},{20,12},{24,16},{28,20},{1,25},{... | collective-permute-start | bytes 1572872 | tf_op jit(solution)/shard_map/ppermute | solution.py:37
  26.8 16.7 %collective-permute-start.3 = (bf16[32,8192]{1,0:T(8,128)(2,1)S(1)}, bf16[32,8192]{1,0:T(8,128)(2,1)S(1)}, u32[]{:S(2)}, u32[]{:S(2)}) collective-permute-start(bf16[32,8192]{1,0:T(8,128)(2,1)S(1)} %collective-permute-done.refs_1_), channel_id=1, source_target_pairs={{0,8},{4,12},{8,16},{12,20},{16,24},{20,28},{24,0},{28,4},{1,9},{5... | collective-permute-start | bytes 1572872 | tf_op jit(solution)/shard_map/ppermute | solution.py:37
  26.8 16.7 %collective-permute-start.2 = (bf16[32,8192]{1,0:T(8,128)(2,1)S(1)}, bf16[32,8192]{1,0:T(8,128)(2,1)}, u32[]{:S(2)}, u32[]{:S(2)}) collective-permute-start(bf16[32,8192]{1,0:T(8,128)(2,1)S(1)} %collective-permute-done.refs_1_), channel_id=1, source_target_pairs={{0,24},{4,28},{8,0},{12,4},{16,8},{20,12},{24,16},{28,20},{1,25},{... | collective-permute-start | bytes 1572872 | tf_op jit(solution)/shard_map/ppermute | solution.py:37
  30.0 13.5 %collective-permute-start.4 = (bf16[32,8192]{1,0:T(8,128)(2,1)S(1)}, bf16[32,8192]{1,0:T(8,128)(2,1)}, u32[]{:S(2)}, u32[]{:S(2)}) collective-permute-start(bf16[32,8192]{1,0:T(8,128)(2,1)S(1)} %collective-permute-done.1.refs_0_), channel_id=1, source_target_pairs={{0,4},{4,0},{8,12},{12,8},{16,20},{20,16},{24,28},{28,24},{1,5},{5... | collective-permute-start | bytes 1572872 | tf_op jit(solution)/shard_map/ppermute | solution.py:37
  37.0 3.1 %copy-start = (bf16[160,16,256]{2,1,0:T(8,128)(2,1)}, bf16[160,16,256]{2,1,0:T(8,128)(2,1)S(1)}, u32[]{:S(2)}) copy-start(bf16[160,16,256]{2,1,0:T(8,128)(2,1)S(1)} %get-tuple-element.46) | copy-start | bytes 3932164
  47.3 9.1 %copy-start.1 = (s32[1,4]{1,0:T(1,128)S(1)}, s32[1,4]{1,0:T(1,128)}, u32[]{:S(2)}) copy-start(s32[1,4]{1,0:T(1,128)} %new_len_ref.1) | copy-start | bytes 52
  47.3 9.1 %copy-start.2 = (s32[1,4]{1,0:T(1,128)S(1)}, s32[1,4]{1,0:T(1,128)}, u32[]{:S(2)}) copy-start(s32[1,4]{1,0:T(1,128)} %prefix_len_ref.1) | copy-start | bytes 52
  47.4 56.3 %all-to-all-start.1 = ((bf16[128,3,16,256]{3,2,1,0:T(8,128)(2,1)}), bf16[128,3,16,256]{3,2,1,0:T(8,128)(2,1)S(1)}, u32[]{:S(2)}, u32[]{:S(2)}) async-start(bf16[128,3,16,256]{3,2,1,0:T(8,128)(2,1)} %bitcast.39), calls=%async_computation.1 | async-start | bytes 6291456 | tf_op jit(solution)/shard_map/all_to_all | solution.py:625
  56.4 16.2 %copy-start.5 = (s32[16,1,236]{2,0,1:T(8,128)S(1)}, s32[16,1,236]{2,0,1:T(8,128)}, u32[]{:S(2)}) copy-start(s32[16,1,236]{2,0,1:T(8,128)} %copy.25) | copy-start | bytes 45316
  68.2 35.2 %collective-permute-start.9 = (bf16[32,8192]{1,0:T(8,128)(2,1)}, bf16[32,8192]{1,0:T(8,128)(2,1)}, u32[]{:S(2)}, u32[]{:S(2)}) collective-permute-start(bf16[32,8192]{1,0:T(8,128)(2,1)} %get-tuple-element.52), channel_id=1, source_target_pairs={{0,4},{4,0},{8,12},{12,8},{16,20},{20,16},{24,28},{28,24},{1,5},{5... | collective-permute-start | bytes 1572872 | tf_op jit(solution)/shard_map/ppermute | solution.py:37
  69.4 34.2 %collective-permute-start.10 = (bf16[32,8192]{1,0:T(8,128)(2,1)}, bf16[32,8192]{1,0:T(8,128)(2,1)}, u32[]{:S(2)}, u32[]{:S(2)}) collective-permute-start(bf16[32,8192]{1,0:T(8,128)(2,1)} %get-tuple-element.53), channel_id=1, source_target_pairs={{0,8},{4,12},{8,16},{12,20},{16,24},{20,28},{24,0},{28,4},{1,9},{5... | collective-permute-start | bytes 1572872 | tf_op jit(solution)/shard_map/ppermute | solution.py:37
  70.9 32.7 %collective-permute-start.11 = (bf16[32,8192]{1,0:T(8,128)(2,1)}, bf16[32,8192]{1,0:T(8,128)(2,1)}, u32[]{:S(2)}, u32[]{:S(2)}) collective-permute-start(bf16[32,8192]{1,0:T(8,128)(2,1)} %get-tuple-element.54), channel_id=1, source_target_pairs={{0,24},{4,28},{8,0},{12,4},{16,8},{20,12},{24,16},{28,20},{1,25},{... | collective-permute-start | bytes 1572872 | tf_op jit(solution)/shard_map/ppermute | solution.py:37
  74.4 40.3 %collective-permute-start.7 = (bf16[32,8192]{1,0:T(8,128)(2,1)}, bf16[32,8192]{1,0:T(8,128)(2,1)}, u32[]{:S(2)}, u32[]{:S(2)}) collective-permute-start(bf16[32,8192]{1,0:T(8,128)(2,1)} %get-tuple-element.48), channel_id=1, source_target_pairs={{0,8},{4,12},{8,16},{12,20},{16,24},{20,28},{24,0},{28,4},{1,9},{5... | collective-permute-start | bytes 1572872 | tf_op jit(solution)/shard_map/ppermute | solution.py:37
  74.7 40.1 %collective-permute-start.8 = (bf16[32,8192]{1,0:T(8,128)(2,1)}, bf16[32,8192]{1,0:T(8,128)(2,1)}, u32[]{:S(2)}, u32[]{:S(2)}) collective-permute-start(bf16[32,8192]{1,0:T(8,128)(2,1)} %get-tuple-element.49), channel_id=1, source_target_pairs={{0,24},{4,28},{8,0},{12,4},{16,8},{20,12},{24,16},{28,20},{1,25},{... | collective-permute-start | bytes 1572872 | tf_op jit(solution)/shard_map/ppermute | solution.py:37
  103.6 11.1 %copy-start.3 = (bf16[1,32,8192]{2,1,0:T(8,128)(2,1)S(1)}, bf16[1,32,8192]{2,1,0:T(8,128)(2,1)}, u32[]{:S(2)}) copy-start(bf16[1,32,8192]{2,1,0:T(8,128)(2,1)} %param.12) | copy-start | bytes 1572868
  103.6 11.1 %copy-start.4 = (bf16[32,8192]{1,0:T(8,128)(2,1)S(1)}, bf16[32,8192]{1,0:T(8,128)(2,1)}, u32[]{:S(2)}) copy-start(bf16[32,8192]{1,0:T(8,128)(2,1)} %get-tuple-element.47) | copy-start | bytes 1572868
  105.3 13.9 %collective-permute-start.12 = (bf16[32,8192]{1,0:T(8,128)(2,1)S(1)}, bf16[32,8192]{1,0:T(8,128)(2,1)S(1)}, u32[]{:S(2)}, u32[]{:S(2)}) collective-permute-start(bf16[32,8192]{1,0:T(8,128)(2,1)S(1)} %add_convert_fusion.2), channel_id=1, source_target_pairs={{0,4},{4,0},{8,12},{12,8},{16,20},{20,16},{24,28},{28,24},{1,5},{5... | collective-permute-start | bytes 1572872 | tf_op jit(solution)/shard_map/ppermute | solution.py:37
  108.3 17.7 %collective-permute-start.13 = (bf16[32,8192]{1,0:T(8,128)(2,1)S(1)}, bf16[32,8192]{1,0:T(8,128)(2,1)S(1)}, u32[]{:S(2)}, u32[]{:S(2)}) collective-permute-start(bf16[32,8192]{1,0:T(8,128)(2,1)S(1)} %add_convert_fusion.1), channel_id=1, source_target_pairs={{0,16},{4,20},{8,24},{12,28},{16,0},{20,4},{24,8},{28,12},{1,17},{... | collective-permute-start | bytes 1572872 | tf_op jit(solution)/shard_map/ppermute | solution.py:37
  126.9 15.0 %collective-permute-start.14 = (bf16[32,8192]{1,0:T(8,128)(2,1)}, bf16[32,8192]{1,0:T(8,128)(2,1)}, u32[]{:S(2)}, u32[]{:S(2)}) collective-permute-start(bf16[32,8192]{1,0:T(8,128)(2,1)} %add_convert_fusion), channel_id=1, source_target_pairs={{96,0},{0,32},{32,64},{64,96},{97,1},{1,33},{33,65},{65,97},{98,2}... | collective-permute-start | bytes 1572872 | tf_op jit(solution)/shard_map/ppermute | solution.py:42
